TPU v7x, 32 devices: a whole 2x2x4 slice. The times are simulated.
32 devices in a mesh: bis: 8 (over z, y), src: 4 (over x, core).
Axes of the slice: x: 2, y: 2, z: 4, core: 2. Of those that a mesh axis runs over, the one named last changes fastest.
Arguments:
- coefficients: float32 [4, 2, 64, 2048], P('src', None, None, 'bis'), may hold values from -6 to 6
- factors: float32 [4, 3, 128, 64, 256], P('src', None, 'bis'), may hold values from -0.375 to 0.375
Outputs:
- potentials: float32 [2, 64, 2048], P(None, 'src', 'bis')
All inputs are finite; a program needn't handle non-finite values.
Results may differ from a plain program's by a relative error of at most 0.0001.
Values sent between devices are 32-bit elements; how exact they have to be, the bound alone decides.
No kernel may reach another device: no remote copies, remote signals or barrier semaphores. Data moves between devices by JAX's collectives and lax.ppermute only.
A program may use at most 64 MiB of HBM per device.

v0:
```python
import jax
import jax.numpy as jnp
from jax import lax
from jax.sharding import PartitionSpec as P

LEVELS = 3


def swapped(value, axis, stride):
    mask = 2**stride
    pairs = [(source, source ^ mask) for source in range(lax.axis_size(axis))]
    return lax.ppermute(value, axis, pairs)


def mix_blocks(factor, stacked):
    return jnp.einsum("boj,jbk->obk", factor, stacked, precision=lax.Precision.HIGHEST)


def advance(state, factor, bit):
    real_part = state[0]
    imag_part = state[1]
    partner = swapped(state, "bis", bit)
    other_re = partner[0]
    other_im = partner[1]
    stack_re = jnp.concatenate([real_part, -imag_part, other_re, -other_im], axis=0)
    stack_im = jnp.concatenate([imag_part, real_part, other_im, other_re], axis=0)
    new_re = mix_blocks(factor, stack_re)
    new_im = mix_blocks(factor, stack_im)
    return jnp.stack([new_re, new_im], axis=0)


def per_device(coefficients, factors):
    middle = (lax.axis_size("bis").bit_length() - 1) // 2
    rank = coefficients.shape[2]
    columns = coefficients.shape[3]
    blocks = factors.shape[2]
    state = coefficients[0].reshape(2, rank, blocks, columns // blocks)
    for level_num in range(LEVELS):
        state = advance(state, factors[0, level_num], middle + 1 - level_num)
    flat = state.reshape(2, rank, columns)
    total = lax.psum(flat, "src")
    share = rank // lax.axis_size("src")
    start = lax.axis_index("src") * share
    return lax.dynamic_slice_in_dim(total, start, share, 1)


def solution(mesh):
    placed = (P("src", None, None, "bis"), P("src", None, "bis", None, None))
    return jax.shard_map(
        per_device, mesh=mesh, in_specs=placed, out_specs=P(None, "src", "bis"), check_vma=False
    )
```

profile of v0, /device:TPU:0, one launch (start us, length us, event | category | flops | bytes accessed | tf_op | source)
XLA Modules:
  0.0 98.1 jit_solution(677798274362134685)
XLA Ops:
  6.5 0.0 copy-start
  6.5 0.0 all-reduce.2.cloned.1.call-start
  6.5 1.9 %copy.5 = f32[1,2,64,256]{2,3,1,0:T(8,128)} copy(f32[1,2,64,256]{3,2,1,0:T(8,128)} %param.2) | data formatting | bytes 262144 | tf_op args[0]
  8.4 4.0 %collective-permute-start = (f32[2,64,16,16]{1,3,2,0:T(8,128)}, f32[2,64,16,16]{1,3,2,0:T(8,128)}, u32[]{:S(2)}, u32[]{:S(2)}) collective-permute-start(f32[2,64,16,16]{1,3,2,0:T(8,128)} %bitcast.2), channel_id=1, source_target_pairs={{0,16},{4,20},{8,24},{12,28},{16,0},{20,4},{24,8},{28,12},{1,17},{... | collective-permute-start | bytes 393224 | tf_op jit(solution)/shard_map/ppermute | solution.py:12
  12.5 1.5 %fusion.69 = (f32[1,1,64,256]{3,2,1,0:T(8,128)S(1)}, f32[1,1,64,256]{3,2,1,0:T(8,128)}) fusion(f32[1,2,64,256]{3,2,1,0:T(8,128)} %param.2), kind=kLoop, calls=%fused_computation.81 | loop fusion | bytes 262144 | tf_op jit(solution)/shard_map/slice | solution.py:21
  14.0 0.1 copy.4
  14.1 0.9 copy.3
  15.0 9.7 %collective-permute-done = f32[2,64,16,16]{1,3,2,0:T(8,128)} collective-permute-done((f32[2,64,16,16]{1,3,2,0:T(8,128)}, f32[2,64,16,16]{1,3,2,0:T(8,128)}, u32[]{:S(2)}, u32[]{:S(2)}) %collective-permute-start) | collective-permute-done | bytes 131104 | tf_op jit(solution)/shard_map/ppermute | solution.py:12
  24.7 1.0 %slice_bitcast_fusion.4 = (f32[64,16,16]{0,2,1:T(8,128)S(1)}, f32[64,16,16]{0,2,1:T(8,128)S(1)}) fusion(f32[2,64,16,16]{1,3,2,0:T(8,128)} %collective-permute-done), kind=kLoop, calls=%fused_computation.66 | loop fusion | bytes 262144 | tf_op jit(solution)/shard_map/squeeze | solution.py:24
  25.7 2.3 %bitcast_negate_fusion.1 = (f32[64,16,16]{0,2,1:T(8,128)S(1)}, f32[16,16,64]{2,1,0:T(8,128)S(1)}) fusion(f32[1,3,16,64,256]{4,3,2,1,0:T(8,128)} %param.3, f32[64,16,16]{0,2,1:T(8,128)S(1)} %get-tuple-element.10, f32[64,16,16]{0,2,1:T(8,128)S(1)} %get-tuple-element.9, f32[64,16,16]{0,2,1:T(8,128)S(1)} %bitcast.70, f32[64,16,16]{0,2,1:T(8,128)S(1)} %bitcast.69), kind=kOutput, calls=%fused_computation.77 | convolution fusion | flops 50544640 | bytes 1441792 | tf_op jit(solution)/shard_map/boj,jbk->obk/dot_general | solution.py:16
  28.0 0.9 fusion.66
  28.9 0.0 copy-done
  28.9 1.1 %fusion.10 = f32[16,16,64]{2,1,0:T(8,128)S(1)} fusion(f32[1,3,16,64,256]{4,3,2,1,0:T(8,128)S(1)} %copy-done, f32[64,16,16]{0,2,1:T(8,128)S(1)} %fusion.66, f32[64,16,16]{0,2,1:T(8,128)S(1)} %get-tuple-element.10, f32[64,16,16]{0,2,1:T(8,128)S(1)} %neg.18, f32[64,16,16]{0,2,1:T(8,128)S(1)} %bitcast.71), kind=kOutput, calls=%fused_computation.10 | convolution fusion | flops 50528256 | bytes 1638400 | tf_op jit(solution)/shard_map/boj,jbk->obk/dot_general | solution.py:16
  30.0 0.8 collective-permute-start.1
  30.8 6.8 %collective-permute-done.1 = f32[2,64,16,16]{1,3,2,0:T(8,128)S(1)} collective-permute-done((f32[2,64,16,16]{1,3,2,0:T(8,128)S(1)}, f32[2,64,16,16]{1,3,2,0:T(8,128)S(1)}, u32[]{:S(2)}, u32[]{:S(2)}) %collective-permute-start.1) | collective-permute-done | bytes 131104 | tf_op jit(solution)/shard_map/ppermute | solution.py:12
  37.6 1.1 %fusion.6 = f32[16,16,64]{2,1,0:T(8,128)S(1)} fusion(f32[1,3,16,64,256]{4,3,2,1,0:T(8,128)S(1)} %copy-done, f32[64,16,16]{0,2,1:T(8,128)S(1)} %fusion.67, f32[64,16,16]{0,2,1:T(8,128)S(1)} %get-tuple-element.8, f32[64,16,16]{0,2,1:T(8,128)S(1)} %get-tuple-element.13, f32[64,16,16]{0,2,1:T(8,128)S(1)} %bitcast.61), kind=kOutput, calls=%fused_computation.6 | convolution fusion | flops 50528256 | bytes 1638400 | tf_op jit(solution)/shard_map/boj,jbk->obk/dot_general | solution.py:16
  38.6 1.1 %bitcast_negate_fusion = (f32[64,16,16]{0,2,1:T(8,128)S(1)}, f32[16,16,64]{2,1,0:T(8,128)S(1)}) fusion(f32[1,3,16,64,256]{4,3,2,1,0:T(8,128)S(1)} %copy-done, f32[64,16,16]{0,2,1:T(8,128)S(1)} %get-tuple-element.8, f32[64,16,16]{0,2,1:T(8,128)S(1)} %get-tuple-element.7, f32[64,16,16]{0,2,1:T(8,128)S(1)} %bitcast.62, f32[64,16,16]{0,2,1:T(8,128)S(1)} %bitcast.67), kind=kOutput, calls=%fused_computation.76 | convolution fusion | flops 50544640 | bytes 1703936 | tf_op jit(solution)/shard_map/boj,jbk->obk/dot_general | solution.py:16
  39.7 1.3 %collective-permute-start.2 = (f32[2,64,16,16]{1,3,2,0:T(8,128)S(1)}, f32[2,64,16,16]{1,3,2,0:T(8,128)S(1)}, u32[]{:S(2)}, u32[]{:S(2)}) collective-permute-start(f32[2,64,16,16]{1,3,2,0:T(8,128)S(1)} %pad_maximum_fusion.1), channel_id=1, source_target_pairs={{0,4},{4,0},{8,12},{12,8},{16,20},{20,16},{24,28},{28,24},{1,5},{5... | collective-permute-start | bytes 393224 | tf_op jit(solution)/shard_map/ppermute | solution.py:12
  41.1 5.3 %collective-permute-done.2 = f32[2,64,16,16]{1,3,2,0:T(8,128)S(1)} collective-permute-done((f32[2,64,16,16]{1,3,2,0:T(8,128)S(1)}, f32[2,64,16,16]{1,3,2,0:T(8,128)S(1)}, u32[]{:S(2)}, u32[]{:S(2)}) %collective-permute-start.2) | collective-permute-done | bytes 131104 | tf_op jit(solution)/shard_map/ppermute | solution.py:12
  46.4 0.0 copy-start.1
  46.4 0.7 copy-done.1
  47.1 1.7 %fusion = f32[16,16,64]{2,1,0:T(8,128)} fusion(f32[1,3,16,64,256]{4,3,2,1,0:T(8,128)S(1)} %copy-done, f32[64,16,16]{0,2,1:T(8,128)S(1)} %get-tuple-element.6, f32[64,16,16]{0,2,1:T(8,128)S(1)} %get-tuple-element.5, f32[64,16,16]{0,2,1:T(8,128)S(1)} %bitcast.64, f32[64,16,16]{0,2,1:T(8,128)S(1)} %bitcast.73), kind=kOutput, calls=%fused_computation | convolution fusion | flops 50528256 | bytes 1638400 | tf_op jit(solution)/shard_map/boj,jbk->obk/dot_general | solution.py:16
  48.8 1.6 %copy.7 = f32[1,64,256]{2,1,0:T(8,128)} copy(f32[1,64,256]{1,2,0:T(8,128)} %bitcast.75) | data formatting | bytes 131072 | tf_op jit(solution)/shard_map/stack | solution.py:29
  50.4 0.9 fusion.68
  51.3 1.7 %fusion.2 = f32[16,16,64]{2,1,0:T(8,128)} fusion(f32[1,3,16,64,256]{4,3,2,1,0:T(8,128)S(1)} %copy-done, f32[64,16,16]{0,2,1:T(8,128)S(1)} %fusion.68, f32[64,16,16]{0,2,1:T(8,128)S(1)} %get-tuple-element.6, f32[64,16,16]{0,2,1:T(8,128)S(1)} %get-tuple-element.15, f32[64,16,16]{0,2,1:T(8,128)S(1)} %bitcast.65), kind=kOutput, calls=%fused_computation.2 | convolution fusion | flops 50528256 | bytes 1638400 | tf_op jit(solution)/shard_map/boj,jbk->obk/dot_general | solution.py:16
  53.1 1.0 %copy.6 = f32[1,64,256]{2,1,0:T(8,128)S(1)} copy(f32[1,64,256]{1,2,0:T(8,128)} %bitcast.74) | data formatting | bytes 131072 | tf_op jit(solution)/shard_map/stack | solution.py:29
  54.0 1.5 %pad_maximum_fusion.2 = f32[2,64,256]{2,1,0:T(8,128)} fusion(f32[1,64,256]{2,1,0:T(8,128)} %copy.7, f32[1,64,256]{2,1,0:T(8,128)S(1)} %copy.6), kind=kLoop, calls=%fused_computation.68 | loop fusion | flops 32768 | bytes 262144 | tf_op jit(solution)/shard_map/stack | solution.py:29
  55.5 0.0 all-reduce.2.cloned.1.call-update
  55.6 34.3 %all-reduce.2.cloned.1.call-done = f32[2,64,256]{2,1,0:T(8,128)} async-done(((f32[2,64,256]{2,1,0:T(8,128)}), f32[2,64,256]{2,1,0:T(8,128)}) %all-reduce.2.cloned.1.call-update) | async-done | bytes 131088 | tf_op jit(solution)/shard_map/psum | solution.py:41
  89.8 1.4 %constant_dynamic-slice_fusion = f32[2,16,256]{2,1,0:T(8,128)} fusion(f32[2,64,256]{2,1,0:T(8,128)} %all-reduce.2.cloned.1.call-done, s32[]{:T(128)S(6)} %select_n.3), kind=kLoop, calls=%fused_computation.69 | loop fusion | bytes 65540 | tf_op jit(solution)/shard_map/dynamic_slice | solution.py:44
  (6 shorter events, 0.1 us)
Async XLA Ops:
  6.5 22.4 %copy-start = (f32[1,3,16,64,256]{4,3,2,1,0:T(8,128)S(1)}, f32[1,3,16,64,256]{4,3,2,1,0:T(8,128)}, u32[]{:S(2)}) copy-start(f32[1,3,16,64,256]{4,3,2,1,0:T(8,128)} %param.3) | copy-start | bytes 9437188
  6.5 83.3 %all-reduce.2.cloned.1.call-start = ((), (), s32[]{:S(2)}) async-start(), calls=%async_computation | async-start | bytes 262144 | tf_op jit(solution)/shard_map/psum | solution.py:41
  8.4 16.3 %collective-permute-start = (f32[2,64,16,16]{1,3,2,0:T(8,128)}, f32[2,64,16,16]{1,3,2,0:T(8,128)}, u32[]{:S(2)}, u32[]{:S(2)}) collective-permute-start(f32[2,64,16,16]{1,3,2,0:T(8,128)} %bitcast.2), channel_id=1, source_target_pairs={{0,16},{4,20},{8,24},{12,28},{16,0},{20,4},{24,8},{28,12},{1,17},{... | collective-permute-start | bytes 393224 | tf_op jit(solution)/shard_map/ppermute | solution.py:12
  30.0 7.6 %collective-permute-start.1 = (f32[2,64,16,16]{1,3,2,0:T(8,128)S(1)}, f32[2,64,16,16]{1,3,2,0:T(8,128)S(1)}, u32[]{:S(2)}, u32[]{:S(2)}) collective-permute-start(f32[2,64,16,16]{1,3,2,0:T(8,128)S(1)} %pad_maximum_fusion), channel_id=1, source_target_pairs={{0,8},{4,12},{8,0},{12,4},{16,24},{20,28},{24,16},{28,20},{1,9},{5... | collective-permute-start | bytes 393224 | tf_op jit(solution)/shard_map/ppermute | solution.py:12
  39.7 6.6 %collective-permute-start.2 = (f32[2,64,16,16]{1,3,2,0:T(8,128)S(1)}, f32[2,64,16,16]{1,3,2,0:T(8,128)S(1)}, u32[]{:S(2)}, u32[]{:S(2)}) collective-permute-start(f32[2,64,16,16]{1,3,2,0:T(8,128)S(1)} %pad_maximum_fusion.1), channel_id=1, source_target_pairs={{0,4},{4,0},{8,12},{12,8},{16,20},{20,16},{24,28},{28,24},{1,5},{5... | collective-permute-start | bytes 393224 | tf_op jit(solution)/shard_map/ppermute | solution.py:12
  46.4 0.7 copy-start.1
Sparse Core Ops, SparseCore 0:
  55.7 34.1 all-reduce.1
where the time goes:
time: 98.5 us; the launch traced here: 98.1 us
  waiting for transfers between devices  56.1 us (57%)
  between operations  13.5 us (14%)
  local copies, waits for them, and re-layouts  10.1 us (10%)
  matrix products  8.87 us (9%)
  starting transfers between devices  6.17 us (6%)
  other arithmetic  3.4 us (3%)
    psum x1, waiting for transfers between devices, per_device(): total = lax.psum(flat, 'src')  34.3 us
    ppermute x3, waiting for transfers between devices, swapped(): return lax.ppermute(value, axis, pairs)  21.8 us
    dot_general x6, matrix products, mix_blocks(): jnp.einsum('boj,jbk->obk', factor, stacked, precision=lax.Precision.HIGHEST)  8.87 us
    ppermute x3, starting transfers between devices, swapped(): return lax.ppermute(value, axis, pairs)  6.17 us
    unnamed x5, local copies, waits for them, and re-layouts  2.6 us
    another operation x2, local copies, waits for them, and re-layouts, advance(): return jnp.stack([new_re, new_im], axis=0)  2.59 us
  transfers between devices with their start and end apart: 4, of which 4 were waited for; matrix products, arithmetic and copies ran while one was open for 3% of the time, Pallas kernels for 0%

commit v1 on v0

v1 whole, which is shorter than its diff:
```python
import functools
import jax
import jax.numpy as jnp
from jax import lax
from jax.experimental import pallas as pl
from jax.experimental.pallas import tpu as pltpu
from jax.sharding import PartitionSpec as P

LEVELS = 3
VMEM = pltpu.MemorySpace.VMEM


def swapped(value, axis, mask):
    pairs = [(source, source ^ mask) for source in range(lax.axis_size(axis))]
    return lax.ppermute(value, axis, pairs)


def split(value):
    high = value.astype(jnp.bfloat16)
    low = (value - high.astype(jnp.float32)).astype(jnp.bfloat16)
    return high, low


def prepare_kernel(f_ref, high_ref, low_ref):
    lane = lax.broadcasted_iota(jnp.int32, (64, 256), 1)
    sign = jnp.where((lane // 64) % 2 == 0, 1.0, -1.0).astype(jnp.float32)

    def one(i, carry):
        f = f_ref[i]
        swap = jnp.concatenate(
            [pltpu.roll(f[:, :128], 64, 1), pltpu.roll(f[:, 128:], 64, 1)], axis=1
        )
        full = jnp.concatenate([f * sign, swap], axis=0)
        high, low = split(full)
        high_ref[i] = high
        low_ref[i] = low
        return carry

    lax.fori_loop(0, f_ref.shape[0], one, 0, unroll=2)


def product(own, partner, high_ref, low_ref, blocks, width):
    high, low = split(jnp.concatenate([own, partner], axis=1))
    outs = []
    dims = (((1,), (1,)), ((), ()))
    for b in range(blocks):
        rows = slice(b * width, (b + 1) * width)
        both = jnp.concatenate([high[rows], low[rows]], axis=0)
        first = lax.dot_general(both, high_ref[b], dims, preferred_element_type=jnp.float32)
        second = lax.dot_general(high[rows], low_ref[b], dims, preferred_element_type=jnp.float32)
        outs.append(first[:width] + first[width:] + second)
    return jnp.concatenate(outs, axis=0)


def first_kernel(own_ref, partner_ref, high_ref, low_ref, out_ref, *, blocks, width):
    own = own_ref[...].T
    partner = partner_ref[...].T
    out_ref[...] = product(own, partner, high_ref, low_ref, blocks, width)


def middle_kernel(own_ref, partner_ref, high_ref, low_ref, out_ref, *, blocks, width):
    out_ref[...] = product(own_ref[...], partner_ref[...], high_ref, low_ref, blocks, width)


def last_kernel(own_ref, partner_ref, high_ref, low_ref, out_ref, *, blocks, width):
    out_ref[...] = product(own_ref[...], partner_ref[...], high_ref, low_ref, blocks, width).T


def call(kernel, outs, *args):
    return pl.pallas_call(
        kernel,
        out_shape=outs,
        in_specs=[pl.BlockSpec(memory_space=VMEM)] * len(args),
        out_specs=jax.tree.map(lambda _: pl.BlockSpec(memory_space=VMEM), outs),
        compiler_params=pltpu.CompilerParams(vmem_limit_bytes=32 * 2**20),
    )(*args)


def per_device(coefficients, factors):
    middle = (lax.axis_size("bis").bit_length() - 1) // 2
    rank, columns, blocks = coefficients.shape[2], coefficients.shape[3], factors.shape[2]
    kw = dict(blocks=blocks, width=columns // blocks)
    raw = coefficients.reshape(2 * rank, columns)
    got = swapped(raw, "bis", 2 ** (middle + 1))
    weights = []
    for level in range(LEVELS):
        shape = jax.ShapeDtypeStruct((blocks, 2 * rank, 4 * rank), jnp.bfloat16)
        weights.append(call(prepare_kernel, [shape, shape], factors[0, level]))
    st = jax.ShapeDtypeStruct((columns, 2 * rank), jnp.float32)
    state = call(functools.partial(first_kernel, **kw), st, raw, got, *weights[0])
    got = swapped(state, "bis", 2 ** middle)
    state = call(functools.partial(middle_kernel, **kw), st, state, got, *weights[1])
    got = swapped(state, "bis", 2 ** (middle - 1))
    st = jax.ShapeDtypeStruct((2 * rank, columns), jnp.float32)
    total = call(functools.partial(last_kernel, **kw), st, state, got, *weights[2])
    groups = lax.axis_size("src")
    me = lax.axis_index("src")
    parts = total.reshape(2, groups, rank // groups, columns)
    mine = lax.dynamic_index_in_dim(parts, me, 1, keepdims=False)
    others = [
        swapped(lax.dynamic_index_in_dim(parts, me ^ m, 1, keepdims=False), "src", m)
        for m in range(1, groups)
    ]
    for o in others:
        mine = mine + o
    return mine


def solution(mesh):
    placed = (P("src", None, None, "bis"), P("src", None, "bis", None, None))
    return jax.shard_map(
        per_device, mesh=mesh, in_specs=placed, out_specs=P(None, "src", "bis"), check_vma=False
    )
```

time: 98.5 us -> 28.6 us (0.29)
  waiting for transfers between devices: 56.1 us -> 12.5 us
  between operations: 13.5 us -> 0.08 us
  matrix products: 8.87 us -> 0 us
  local copies, waits for them, and re-layouts: 10.1 us -> 2.18 us
  Pallas kernels: 0 us -> 4.76 us
  other arithmetic: 3.4 us -> 0.63 us
  starting transfers between devices: 6.17 us -> 8.29 us
    psum x1 -> x0, waiting for transfers between devices: 34.3 us -> none  [per_device(): total = lax.psum(flat, 'src')]
    ppermute x3 -> x6, waiting for transfers between devices: 21.8 us -> 12.5 us  [swapped(): return lax.ppermute(value, axis, pairs)]
    dot_general x6 -> x0, matrix products: 8.87 us -> none  [mix_blocks(): jnp.einsum('boj,jbk->obk', factor, stacked, precision=lax.Precision.HIGHEST)]
    pallas_call x0 -> x6, Pallas kernels: none -> 4.76 us  [call(): pl.pallas_call(kernel, out_shape=outs, in_specs=[pl.BlockSpec(memory_spac...]
    unnamed x5 -> x2, local copies, waits for them, and re-layouts: 2.6 us -> 0.01 us
    another operation x2 -> x0, local copies, waits for them, and re-layouts: 2.59 us -> none  [advance(): return jnp.stack([new_re, new_im], axis=0)]
    slice x3 -> x0, local copies, waits for them, and re-layouts: 2.52 us -> none  [the longest x2 1.59 us: advance(): imag_part = state[1]]
    ppermute x3 -> x6, starting transfers between devices: 6.17 us -> 8.29 us  [swapped(): return lax.ppermute(value, axis, pairs)]
  transfers between devices with their start and end apart: 4 -> 6, of which waited for: 4 -> 5; matrix products, arithmetic and copies ran while one was open for 3% -> 8% of each run, Pallas kernels for 0% -> 9%
where the time goes in v1:
time: 28.6 us; the launch traced here: 28.5 us
  waiting for transfers between devices  12.5 us (44%)
  starting transfers between devices  8.29 us (29%)
  Pallas kernels  4.76 us (17%)
  local copies, waits for them, and re-layouts  2.18 us (8%)
  other arithmetic  0.63 us (2%)
    ppermute x6, waiting for transfers between devices, swapped(): return lax.ppermute(value, axis, pairs)  12.5 us
    ppermute x6, starting transfers between devices, swapped(): return lax.ppermute(value, axis, pairs)  8.29 us
    pallas_call x6, Pallas kernels, call(): pl.pallas_call(kernel, out_shape=outs, in_specs=[pl.BlockSpec(memory_spac...  4.76 us
    squeeze x1, local copies, waits for them, and re-layouts, per_device(): weights.append(call(prepare_kernel, [shape, shape], factors[0, level]))  2.16 us
    add x1, other arithmetic, per_device(): mine = mine + o  0.63 us
  transfers between devices with their start and end apart: 6, of which 5 were waited for; matrix products, arithmetic and copies ran while one was open for 8% of the time, Pallas kernels for 9%

profile of v1, /device:TPU:0, one launch (start us, length us, event | category | flops | bytes accessed | tf_op | source)
XLA Modules:
  0.0 28.5 jit_solution(18320787388409227773)
XLA Ops:
  0.0 0.0 copy-start
  0.0 4.0 %collective-permute-start = (f32[128,256]{1,0:T(8,128)}, f32[128,256]{1,0:T(8,128)S(1)}, u32[]{:S(2)}, u32[]{:S(2)}) collective-permute-start(f32[128,256]{1,0:T(8,128)} %bitcast.22), channel_id=1, source_target_pairs={{0,16},{4,20},{8,24},{12,28},{16,0},{20,4},{24,8},{28,12},{1,17},{... | collective-permute-start | bytes 393224 | tf_op jit(solution)/shard_map/ppermute | solution.py:15
  4.0 2.2 %slice_bitcast_fusion = (f32[16,64,256]{2,1,0:T(8,128)S(1)}, f32[16,64,256]{2,1,0:T(8,128)S(1)}, f32[16,64,256]{2,1,0:T(8,128)S(1)}) fusion(f32[1,3,16,64,256]{4,3,2,1,0:T(8,128)} %param.3), kind=kLoop, calls=%fused_computation | loop fusion | bytes 6291456 | tf_op jit(solution)/shard_map/squeeze | solution.py:88
  6.2 0.8 %shard_map.28 = (bf16[16,128,256]{2,1,0:T(8,128)(2,1)S(1)}, bf16[16,128,256]{2,1,0:T(8,128)(2,1)S(1)}) custom-call(f32[16,64,256]{2,1,0:T(8,128)S(1)} %get-tuple-element.18.f_ref), custom_call_target="tpu_custom_call" | custom-call | tf_op jit(solution)/shard_map/pallas_call | solution.py:70
  7.1 3.6 %collective-permute-done.partner_ref = f32[128,256]{1,0:T(8,128)S(1)} collective-permute-done((f32[128,256]{1,0:T(8,128)}, f32[128,256]{1,0:T(8,128)S(1)}, u32[]{:S(2)}, u32[]{:S(2)}) %collective-permute-start) | collective-permute-done | bytes 131104 | tf_op jit(solution)/shard_map/ppermute | solution.py:15
  10.6 0.0 copy-done
  10.6 0.7 %shard_map.29.own_ref = f32[256,128]{1,0:T(8,128)S(1)} custom-call(f32[128,256]{1,0:T(8,128)S(1)} %bitcast.23, f32[128,256]{1,0:T(8,128)S(1)} %collective-permute-done.partner_ref, bf16[16,128,256]{2,1,0:T(8,128)(2,1)S(1)} %get-tuple-element.11.high_ref, bf16[16,128,256]{2,1,0:T(8,128)(2,1)S(1)} %get-tuple-element.12.low_ref), custom_call_target="tpu_custom_call" | custom-call | tf_op jit(solution)/shard_map/pallas_call | solution.py:70
  11.3 0.8 %collective-permute-start.1 = (f32[256,128]{1,0:T(8,128)S(1)}, f32[256,128]{1,0:T(8,128)S(1)}, u32[]{:S(2)}, u32[]{:S(2)}) collective-permute-start(f32[256,128]{1,0:T(8,128)S(1)} %shard_map.29.own_ref), channel_id=1, source_target_pairs={{0,8},{4,12},{8,0},{12,4},{16,24},{20,28},{24,16},{28,20},{1,9},{5... | collective-permute-start | bytes 393224 | tf_op jit(solution)/shard_map/ppermute | solution.py:15
  12.1 0.8 %shard_map.30 = (bf16[16,128,256]{2,1,0:T(8,128)(2,1)S(1)}, bf16[16,128,256]{2,1,0:T(8,128)(2,1)S(1)}) custom-call(f32[16,64,256]{2,1,0:T(8,128)S(1)} %get-tuple-element.19.f_ref), custom_call_target="tpu_custom_call" | custom-call | tf_op jit(solution)/shard_map/pallas_call | solution.py:70
  13.0 3.4 %collective-permute-done.1.partner_ref = f32[256,128]{1,0:T(8,128)S(1)} collective-permute-done((f32[256,128]{1,0:T(8,128)S(1)}, f32[256,128]{1,0:T(8,128)S(1)}, u32[]{:S(2)}, u32[]{:S(2)}) %collective-permute-start.1) | collective-permute-done | bytes 131104 | tf_op jit(solution)/shard_map/ppermute | solution.py:15
  16.3 0.7 %shard_map.31.own_ref = f32[256,128]{1,0:T(8,128)S(1)} custom-call(f32[256,128]{1,0:T(8,128)S(1)} %shard_map.29.own_ref, f32[256,128]{1,0:T(8,128)S(1)} %collective-permute-done.1.partner_ref, bf16[16,128,256]{2,1,0:T(8,128)(2,1)S(1)} %get-tuple-element.13.high_ref, bf16[16,128,256]{2,1,0:T(8,128)(2,1)S(1)} %get-tuple-element.14.low_ref), custom_call_target="tpu_custom_call" | custom-call | tf_op jit(solution)/shard_map/pallas_call | solution.py:70
  17.0 1.5 %collective-permute-start.2 = (f32[256,128]{1,0:T(8,128)S(1)}, f32[256,128]{1,0:T(8,128)S(1)}, u32[]{:S(2)}, u32[]{:S(2)}) collective-permute-start(f32[256,128]{1,0:T(8,128)S(1)} %shard_map.31.own_ref), channel_id=1, source_target_pairs={{0,4},{4,0},{8,12},{12,8},{16,20},{20,16},{24,28},{28,24},{1,5},{5... | collective-permute-start | bytes 393224 | tf_op jit(solution)/shard_map/ppermute | solution.py:15
  18.6 0.8 %shard_map.32 = (bf16[16,128,256]{2,1,0:T(8,128)(2,1)S(1)}, bf16[16,128,256]{2,1,0:T(8,128)(2,1)S(1)}) custom-call(f32[16,64,256]{2,1,0:T(8,128)S(1)} %get-tuple-element.17.f_ref), custom_call_target="tpu_custom_call" | custom-call | tf_op jit(solution)/shard_map/pallas_call | solution.py:70
  19.4 2.6 %collective-permute-done.2.partner_ref = f32[256,128]{1,0:T(8,128)S(1)} collective-permute-done((f32[256,128]{1,0:T(8,128)S(1)}, f32[256,128]{1,0:T(8,128)S(1)}, u32[]{:S(2)}, u32[]{:S(2)}) %collective-permute-start.2) | collective-permute-done | bytes 131104 | tf_op jit(solution)/shard_map/ppermute | solution.py:15
  22.0 0.8 %shard_map.33 = f32[128,256]{1,0:T(8,128)S(1)} custom-call(f32[256,128]{1,0:T(8,128)S(1)} %shard_map.31.own_ref, f32[256,128]{1,0:T(8,128)S(1)} %collective-permute-done.2.partner_ref, bf16[16,128,256]{2,1,0:T(8,128)(2,1)S(1)} %get-tuple-element.15.high_ref, bf16[16,128,256]{2,1,0:T(8,128)(2,1)S(1)} %get-tuple-element.16.low_ref), custom_call_target="tpu_custom_call" | custom-call | tf_op jit(solution)/shard_map/pallas_call | solution.py:70
  22.9 0.1 collective-permute-start.3
  22.9 1.6 %collective-permute-start.4 = (f32[2,16,256]{2,1,0:T(8,128)S(1)}, f32[2,16,256]{2,1,0:T(8,128)S(1)}, u32[]{:S(2)}, u32[]{:S(2)}) collective-permute-start(f32[2,16,256]{2,1,0:T(8,128)S(1)} %get-tuple-element.22), channel_id=1, source_target_pairs={{0,2},{1,3},{2,0},{3,1},{4,6},{5,7},{6,4},{7,5},{8,10},{9,11},{10,... | collective-permute-start | bytes 98312 | tf_op jit(solution)/shard_map/ppermute | solution.py:15
  24.5 0.3 %collective-permute-start.5 = (f32[2,16,256]{2,1,0:T(8,128)S(1)}, f32[2,16,256]{2,1,0:T(8,128)S(1)}, u32[]{:S(2)}, u32[]{:S(2)}) collective-permute-start(f32[2,16,256]{2,1,0:T(8,128)S(1)} %get-tuple-element.21), channel_id=1, source_target_pairs={{0,3},{1,2},{2,1},{3,0},{4,7},{5,6},{6,5},{7,4},{8,11},{9,10},{10,... | collective-permute-start | bytes 98312 | tf_op jit(solution)/shard_map/ppermute | solution.py:15
  24.8 0.0 collective-permute-done.3
  24.8 2.1 %collective-permute-done.4 = f32[2,16,256]{2,1,0:T(8,128)S(1)} collective-permute-done((f32[2,16,256]{2,1,0:T(8,128)S(1)}, f32[2,16,256]{2,1,0:T(8,128)S(1)}, u32[]{:S(2)}, u32[]{:S(2)}) %collective-permute-start.4) | collective-permute-done | bytes 32800 | tf_op jit(solution)/shard_map/ppermute | solution.py:15
  26.9 0.9 %collective-permute-done.5 = f32[2,16,256]{2,1,0:T(8,128)S(1)} collective-permute-done((f32[2,16,256]{2,1,0:T(8,128)S(1)}, f32[2,16,256]{2,1,0:T(8,128)S(1)}, u32[]{:S(2)}, u32[]{:S(2)}) %collective-permute-start.5) | collective-permute-done | bytes 32800 | tf_op jit(solution)/shard_map/ppermute | solution.py:15
  27.8 0.6 %fusion.1 = f32[2,16,256]{2,1,0:T(8,128)} fusion(f32[2,16,256]{2,1,0:T(8,128)S(1)} %collective-permute-done.5, f32[2,16,256]{2,1,0:T(8,128)S(1)} %collective-permute-done.4, f32[2,16,256]{2,1,0:T(8,128)S(1)} %collective-permute-done.3, f32[2,4,16,256]{3,2,1,0:T(8,128)S(1)} %bitcast.21, s32[]{:T(128)S(6)} %select_n.13), kind=kLoop, calls=%fused_computation.5 | loop fusion | flops 24576 | bytes 163844 | tf_op jit(solution)/shard_map/add | solution.py:105
  (1 shorter events, 0.0 us)
Async XLA Ops:
  0.0 10.6 %copy-start = (f32[1,2,64,256]{3,2,1,0:T(8,128)S(1)}, f32[1,2,64,256]{3,2,1,0:T(8,128)}, u32[]{:S(2)}) copy-start(f32[1,2,64,256]{3,2,1,0:T(8,128)} %param.2) | copy-start | bytes 393220
  0.0 10.6 %collective-permute-start = (f32[128,256]{1,0:T(8,128)}, f32[128,256]{1,0:T(8,128)S(1)}, u32[]{:S(2)}, u32[]{:S(2)}) collective-permute-start(f32[128,256]{1,0:T(8,128)} %bitcast.22), channel_id=1, source_target_pairs={{0,16},{4,20},{8,24},{12,28},{16,0},{20,4},{24,8},{28,12},{1,17},{... | collective-permute-start | bytes 393224 | tf_op jit(solution)/shard_map/ppermute | solution.py:15
  11.3 5.0 %collective-permute-start.1 = (f32[256,128]{1,0:T(8,128)S(1)}, f32[256,128]{1,0:T(8,128)S(1)}, u32[]{:S(2)}, u32[]{:S(2)}) collective-permute-start(f32[256,128]{1,0:T(8,128)S(1)} %shard_map.29.own_ref), channel_id=1, source_target_pairs={{0,8},{4,12},{8,0},{12,4},{16,24},{20,28},{24,16},{28,20},{1,9},{5... | collective-permute-start | bytes 393224 | tf_op jit(solution)/shard_map/ppermute | solution.py:15
  17.0 5.0 %collective-permute-start.2 = (f32[256,128]{1,0:T(8,128)S(1)}, f32[256,128]{1,0:T(8,128)S(1)}, u32[]{:S(2)}, u32[]{:S(2)}) collective-permute-start(f32[256,128]{1,0:T(8,128)S(1)} %shard_map.31.own_ref), channel_id=1, source_target_pairs={{0,4},{4,0},{8,12},{12,8},{16,20},{20,16},{24,28},{28,24},{1,5},{5... | collective-permute-start | bytes 393224 | tf_op jit(solution)/shard_map/ppermute | solution.py:15
  22.9 1.9 %collective-permute-start.3 = (f32[2,16,256]{2,1,0:T(8,128)S(1)}, f32[2,16,256]{2,1,0:T(8,128)S(1)}, u32[]{:S(2)}, u32[]{:S(2)}) collective-permute-start(f32[2,16,256]{2,1,0:T(8,128)S(1)} %get-tuple-element.20), channel_id=1, source_target_pairs={{0,1},{1,0},{2,3},{3,2},{4,5},{5,4},{6,7},{7,6},{8,9},{9,8},{10,11... | collective-permute-start | bytes 98312 | tf_op jit(solution)/shard_map/ppermute | solution.py:15
  22.9 4.0 %collective-permute-start.4 = (f32[2,16,256]{2,1,0:T(8,128)S(1)}, f32[2,16,256]{2,1,0:T(8,128)S(1)}, u32[]{:S(2)}, u32[]{:S(2)}) collective-permute-start(f32[2,16,256]{2,1,0:T(8,128)S(1)} %get-tuple-element.22), channel_id=1, source_target_pairs={{0,2},{1,3},{2,0},{3,1},{4,6},{5,7},{6,4},{7,5},{8,10},{9,11},{10,... | collective-permute-start | bytes 98312 | tf_op jit(solution)/shard_map/ppermute | solution.py:15
  24.5 3.3 %collective-permute-start.5 = (f32[2,16,256]{2,1,0:T(8,128)S(1)}, f32[2,16,256]{2,1,0:T(8,128)S(1)}, u32[]{:S(2)}, u32[]{:S(2)}) collective-permute-start(f32[2,16,256]{2,1,0:T(8,128)S(1)} %get-tuple-element.21), channel_id=1, source_target_pairs={{0,3},{1,2},{2,1},{3,0},{4,7},{5,6},{6,5},{7,4},{8,11},{9,10},{10,... | collective-permute-start | bytes 98312 | tf_op jit(solution)/shard_map/ppermute | solution.py:15

commit v2 on v0

v2 whole, which is shorter than its diff:
```python
import functools
import jax
import jax.numpy as jnp
from jax import lax
from jax.experimental import pallas as pl
from jax.experimental.pallas import tpu as pltpu
from jax.sharding import PartitionSpec as P

LEVELS = 3
CHUNKS = 2
VMEM = pl.BlockSpec(memory_space=pltpu.MemorySpace.VMEM)
SMEM = pl.BlockSpec(memory_space=pltpu.MemorySpace.SMEM)
HBM = pl.BlockSpec(memory_space=pltpu.MemorySpace.HBM)


def swapped(value, axis, mask):
    pairs = [(source, source ^ mask) for source in range(lax.axis_size(axis))]
    return lax.ppermute(value, axis, pairs)


def split(value):
    high = value.astype(jnp.bfloat16)
    low = (value - high.astype(jnp.float32)).astype(jnp.bfloat16)
    return high, low


def advance(own, partner, fh, fl, width):
    blocks, rank, depth = fh.shape
    n = own.shape[1]
    fh, fl = fh.reshape(blocks * rank, depth), fl.reshape(blocks * rank, depth)
    re, im, other_re, other_im = own[:rank], own[rank:], partner[:rank], partner[rank:]
    stack = jnp.concatenate(
        [
            jnp.concatenate([re, -im, other_re, -other_im], axis=0),
            jnp.concatenate([im, re, other_im, other_re], axis=0),
        ],
        axis=1,
    )
    xh, xl = split(stack)
    dot = functools.partial(jnp.dot, preferred_element_type=jnp.float32)
    full = dot(fh, xh) + dot(fh, xl) + dot(fl, xh)
    block = lax.broadcasted_iota(jnp.int32, (rank, n), 1) // width
    halves = []
    for q in range(2):
        out = full[:rank, q * n : (q + 1) * n]
        for b in range(1, blocks):
            out = jnp.where(block == b, full[b * rank : (b + 1) * rank, q * n : (q + 1) * n], out)
        halves.append(out)
    return jnp.concatenate(halves, axis=0)


def arrange_kernel(x_hbm, *refs):
    *outs, sems = refs
    n = outs[0].shape[1]
    copies = [
        pltpu.make_async_copy(x_hbm.at[:, i * n : (i + 1) * n], o, sems.at[i])
        for i, o in enumerate(outs)
    ]
    for c in copies:
        c.start()
    for c in copies:
        c.wait()


def prepare_kernel(f_hbm, *refs):
    *outs, f_ref, sems = refs
    copies = [
        pltpu.make_async_copy(f_hbm.at[0, i], f_ref.at[i], sems.at[i]) for i in range(LEVELS)
    ]
    for c in copies:
        c.start()
    for level in range(LEVELS):
        copies[level].wait()
        high_ref, low_ref = outs[2 * level : 2 * level + 2]

        def one(b, carry):
            high_ref[b], low_ref[b] = split(f_ref[level, b])
            return carry

        lax.fori_loop(0, f_ref.shape[1], one, 0, unroll=4)


def middle_kernel(own_ref, got_ref, fh_ref, fl_ref, out_ref, *, i, width):
    blocks = own_ref.shape[1] // width
    rows = slice(i * blocks, (i + 1) * blocks)
    out_ref[...] = advance(own_ref[...], got_ref[...], fh_ref[rows], fl_ref[rows], width)


def turn_kernel(me_ref, done_ref, own_ref, got_ref, fh_ref, fl_ref, *out_refs, i, width):
    blocks = own_ref.shape[1] // width
    rows = slice(i * blocks, (i + 1) * blocks)
    total = advance(own_ref[...], got_ref[...], fh_ref[rows], fl_ref[rows], width)
    total = jnp.concatenate([total, done_ref[...]] if i == 0 else [done_ref[...], total], axis=1)
    groups = len(out_refs)
    share = total.shape[0] // 2 // groups
    for g in range(groups):
        part = jnp.stack([total[q * share : (q + 1) * share] for q in (g, groups + g)])
        m = me_ref[0] ^ g
        for j in range(groups):

            @pl.when(m == j)
            def _():
                out_refs[j][...] = part


def sum_kernel(*refs):
    *parts, out_ref = refs
    total = parts[0][...]
    for r in parts[1:]:
        total = total + r[...]
    out_ref[...] = total


def call(kernel, outs, *args, specs=None, limit=16, scratch=(), name=None):
    return pl.pallas_call(
        kernel,
        out_shape=outs,
        in_specs=specs or [VMEM] * len(args),
        out_specs=jax.tree.map(lambda _: VMEM, outs),
        scratch_shapes=scratch,
        compiler_params=pltpu.CompilerParams(vmem_limit_bytes=limit * 2**20),
        name=name,
    )(*args)


def per_device(coefficients, factors):
    middle = (lax.axis_size("bis").bit_length() - 1) // 2
    rank, columns, blocks = coefficients.shape[2], coefficients.shape[3], factors.shape[2]
    width = columns // blocks
    groups = lax.axis_size("src")
    f32 = jnp.float32
    raw = coefficients.reshape(2 * rank, columns)
    part = jax.ShapeDtypeStruct((2 * rank, columns // CHUNKS), f32)
    step = columns // CHUNKS
    states = [raw[:, i * step : (i + 1) * step] for i in range(CHUNKS)]
    me = jnp.reshape(lax.axis_index("src"), (1,)).astype(jnp.int32)
    piece = jax.ShapeDtypeStruct((2, rank // groups, columns), f32)
    gots = [swapped(s, "bis", 2 ** (middle + 1)) for s in states]
    half = jax.ShapeDtypeStruct(factors.shape[2:], jnp.bfloat16)
    halves = call(
        prepare_kernel, [half] * (2 * LEVELS), factors, specs=[HBM],
        scratch=[pltpu.VMEM(factors.shape[1:], f32), pltpu.SemaphoreType.DMA((LEVELS,))],
        name="prepare",
    )
    order = tuple(reversed(range(CHUNKS)))
    for level in range(LEVELS):
        for i in order:
            kw = dict(i=i, width=width)
            if (level, i) != (LEVELS - 1, order[-1]):
                states[i] = call(
                    functools.partial(middle_kernel, **kw), part, states[i], gots[i],
                    *halves[2 * level : 2 * level + 2], name=f"level{level}_{i}",
                )
            else:
                pieces = call(
                    functools.partial(turn_kernel, **kw), [piece] * groups,
                    me, states[order[0]], states[i], gots[i], *halves[2 * level : 2 * level + 2],
                    specs=[SMEM] + [VMEM] * 5, name=f"level{level}_{i}",
                )
            if level < LEVELS - 1:
                gots[i] = swapped(states[i], "bis", 2 ** (middle - level))
    parts = [pieces[0]] + [swapped(pieces[m], "src", m) for m in reversed(range(1, groups))]
    return call(sum_kernel, piece, *parts, name="total")


def solution(mesh):
    placed = (P("src", None, None, "bis"), P("src", None, "bis", None, None))
    return jax.shard_map(
        per_device, mesh=mesh, in_specs=placed, out_specs=P(None, "src", "bis"), check_vma=False
    )
```

time: 98.5 us -> 26.3 us (0.27)
  waiting for transfers between devices: 56.1 us -> 6.98 us
  between operations: 13.5 us -> 0.08 us
  matrix products: 8.87 us -> 0 us
  local copies, waits for them, and re-layouts: 10.1 us -> 2.77 us
  starting transfers between devices: 6.17 us -> 12.7 us
  Pallas kernels: 0 us -> 3.58 us
  other arithmetic: 3.4 us -> 0 us
    psum x1 -> x0, waiting for transfers between devices: 34.3 us -> none  [per_device(): total = lax.psum(flat, 'src')]
    ppermute x3 -> x9, waiting for transfers between devices: 21.8 us -> 6.98 us  [swapped(): return lax.ppermute(value, axis, pairs)]
    dot_general x6 -> x0, matrix products: 8.87 us -> none  [mix_blocks(): jnp.einsum('boj,jbk->obk', factor, stacked, precision=lax.Precision.HIGHEST)]
    ppermute x3 -> x9, starting transfers between devices: 6.17 us -> 12.7 us  [swapped(): return lax.ppermute(value, axis, pairs)]
    pallas_call x0 -> x8, Pallas kernels: none -> 3.58 us  [call(): pl.pallas_call(kernel, out_shape=outs, in_specs=specs or [VMEM] * len(arg...]
    another operation x2 -> x0, local copies, waits for them, and re-layouts: 2.59 us -> none  [advance(): return jnp.stack([new_re, new_im], axis=0)]
    neg x4 -> x0, other arithmetic: 1.86 us -> none  [the longest x3 1.85 us: advance(): -other_im]
    slice x3 -> x1, local copies, waits for them, and re-layouts: 2.52 us -> 0.88 us  [per_device(): states = [raw[:, i * step:(i + 1) * step] for i in range(CHUNKS)]]
  transfers between devices with their start and end apart: 4 -> 9, of which waited for: 4 -> 8; matrix products, arithmetic and copies ran while one was open for 3% -> 0% of each run, Pallas kernels for 0% -> 10%
where the time goes in v2:
time: 26.3 us; the launch traced here: 26.1 us
  starting transfers between devices  12.7 us (48%)
  waiting for transfers between devices  6.98 us (27%)
  Pallas kernels  3.58 us (14%)
  local copies, waits for them, and re-layouts  2.77 us (11%)
    ppermute x9, starting transfers between devices, swapped(): return lax.ppermute(value, axis, pairs)  12.7 us
    ppermute x9, waiting for transfers between devices, swapped(): return lax.ppermute(value, axis, pairs)  6.98 us
    pallas_call x8, Pallas kernels, call(): pl.pallas_call(kernel, out_shape=outs, in_specs=specs or [VMEM] * len(arg...  3.58 us
    unnamed x2, local copies, waits for them, and re-layouts  1.89 us
    slice x1, local copies, waits for them, and re-layouts, per_device(): states = [raw[:, i * step:(i + 1) * step] for i in range(CHUNKS)]  0.88 us
  transfers between devices with their start and end apart: 9, of which 8 were waited for; matrix products, arithmetic and copies ran while one was open for 0% of the time, Pallas kernels for 10%

profile of v2, /device:TPU:0, one launch (start us, length us, event | category | flops | bytes accessed | tf_op | source)
XLA Modules:
  0.0 26.1 jit_solution(8328471780969679687)
XLA Ops:
  0.0 0.9 %fusion = (f32[128,128]{1,0:T(8,128)S(1)}, f32[128,128]{1,0:T(8,128)S(1)}) fusion(f32[128,256]{1,0:T(8,128)} %bitcast.2), kind=kLoop, calls=%fused_computation | loop fusion | bytes 262144 | tf_op jit(solution)/shard_map/slice | solution.py:135
  0.9 4.1 %collective-permute-start = (f32[128,128]{1,0:T(8,128)S(1)}, f32[128,128]{1,0:T(8,128)S(1)}, u32[]{:S(2)}, u32[]{:S(2)}) collective-permute-start(f32[128,128]{1,0:T(8,128)S(1)} %get-tuple-element.26.own_ref), channel_id=1, source_target_pairs={{0,16},{4,20},{8,24},{12,28},{16,0},{20,4},{24,8},{28,12},{1,17},{... | collective-permute-start | bytes 196616 | tf_op jit(solution)/shard_map/ppermute | solution.py:18
  5.0 0.1 collective-permute-start.3
  5.1 0.0 copy-start
  5.1 1.9 %copy-done = f32[1,3,16,64,256]{4,3,2,1,0:T(8,128)S(1)} copy-done((f32[1,3,16,64,256]{4,3,2,1,0:T(8,128)S(1)}, f32[1,3,16,64,256]{4,3,2,1,0:T(8,128)}, u32[]{:S(2)}) %copy-start) | copy-done | bytes 3145752
  7.0 0.6 %prepare.1 = (bf16[16,64,256]{2,1,0:T(8,128)(2,1)S(1)}, bf16[16,64,256]{2,1,0:T(8,128)(2,1)S(1)}, bf16[16,64,256]{2,1,0:T(8,128)(2,1)S(1)}, bf16[16,64,256]{2,1,...) custom-call(f32[1,3,16,64,256]{4,3,2,1,0:T(8,128)S(1)} %copy-done), custom_call_target="tpu_custom_call" | custom-call | tf_op jit(solution)/shard_map/prepare/pallas_call | solution.py:115
  7.6 1.0 %collective-permute-done.got_ref = f32[128,128]{1,0:T(8,128)S(1)} collective-permute-done((f32[128,128]{1,0:T(8,128)S(1)}, f32[128,128]{1,0:T(8,128)S(1)}, u32[]{:S(2)}, u32[]{:S(2)}) %collective-permute-start) | collective-permute-done | bytes 65568 | tf_op jit(solution)/shard_map/ppermute | solution.py:18
  8.6 0.4 %level0_1.1.own_ref = f32[128,128]{1,0:T(8,128)S(1)} custom-call(f32[128,128]{1,0:T(8,128)S(1)} %get-tuple-element.26.own_ref, f32[128,128]{1,0:T(8,128)S(1)} %collective-permute-done.got_ref, bf16[16,64,256]{2,1,0:T(8,128)(2,1)S(1)} %get-tuple-element.15.fh_ref, bf16[16,64,256]{2,1,0:T(8,128)(2,1)S(1)} %get-tuple-element.16.fl_ref), custom_call_target="tpu_custom_call" | custom-call | tf_op jit(solution)/shard_map/level0_1/pallas_call | solution.py:115
  9.0 2.1 %collective-permute-start.1 = (f32[128,128]{1,0:T(8,128)S(1)}, f32[128,128]{1,0:T(8,128)S(1)}, u32[]{:S(2)}, u32[]{:S(2)}) collective-permute-start(f32[128,128]{1,0:T(8,128)S(1)} %level0_1.1.own_ref), channel_id=1, source_target_pairs={{0,8},{4,12},{8,0},{12,4},{16,24},{20,28},{24,16},{28,20},{1,9},{5... | collective-permute-start | bytes 196616 | tf_op jit(solution)/shard_map/ppermute | solution.py:18
  11.1 0.3 %collective-permute-done.3.got_ref = f32[128,128]{1,0:T(8,128)S(1)} collective-permute-done((f32[128,128]{1,0:T(8,128)S(1)}, f32[128,128]{1,0:T(8,128)S(1)}, u32[]{:S(2)}, u32[]{:S(2)}) %collective-permute-start.3) | collective-permute-done | bytes 65568 | tf_op jit(solution)/shard_map/ppermute | solution.py:18
  11.4 0.4 %level0_0.1.own_ref = f32[128,128]{1,0:T(8,128)S(1)} custom-call(f32[128,128]{1,0:T(8,128)S(1)} %get-tuple-element.25.own_ref, f32[128,128]{1,0:T(8,128)S(1)} %collective-permute-done.3.got_ref, bf16[16,64,256]{2,1,0:T(8,128)(2,1)S(1)} %get-tuple-element.15.fh_ref, bf16[16,64,256]{2,1,0:T(8,128)(2,1)S(1)} %get-tuple-element.16.fl_ref), custom_call_target="tpu_custom_call" | custom-call | tf_op jit(solution)/shard_map/level0_0/pallas_call | solution.py:115
  11.8 0.6 %collective-permute-start.4 = (f32[128,128]{1,0:T(8,128)S(1)}, f32[128,128]{1,0:T(8,128)S(1)}, u32[]{:S(2)}, u32[]{:S(2)}) collective-permute-start(f32[128,128]{1,0:T(8,128)S(1)} %level0_0.1.own_ref), channel_id=1, source_target_pairs={{0,8},{4,12},{8,0},{12,4},{16,24},{20,28},{24,16},{28,20},{1,9},{5... | collective-permute-start | bytes 196616 | tf_op jit(solution)/shard_map/ppermute | solution.py:18
  12.5 0.9 %collective-permute-done.1.got_ref = f32[128,128]{1,0:T(8,128)S(1)} collective-permute-done((f32[128,128]{1,0:T(8,128)S(1)}, f32[128,128]{1,0:T(8,128)S(1)}, u32[]{:S(2)}, u32[]{:S(2)}) %collective-permute-start.1) | collective-permute-done | bytes 65568 | tf_op jit(solution)/shard_map/ppermute | solution.py:18
  13.4 0.4 %level1_1.1.own_ref = f32[128,128]{1,0:T(8,128)S(1)} custom-call(f32[128,128]{1,0:T(8,128)S(1)} %level0_1.1.own_ref, f32[128,128]{1,0:T(8,128)S(1)} %collective-permute-done.1.got_ref, bf16[16,64,256]{2,1,0:T(8,128)(2,1)S(1)} %get-tuple-element.17.fh_ref, bf16[16,64,256]{2,1,0:T(8,128)(2,1)S(1)} %get-tuple-element.18.fl_ref), custom_call_target="tpu_custom_call" | custom-call | tf_op jit(solution)/shard_map/level1_1/pallas_call | solution.py:115
  13.8 2.0 %collective-permute-start.2 = (f32[128,128]{1,0:T(8,128)S(1)}, f32[128,128]{1,0:T(8,128)S(1)}, u32[]{:S(2)}, u32[]{:S(2)}) collective-permute-start(f32[128,128]{1,0:T(8,128)S(1)} %level1_1.1.own_ref), channel_id=1, source_target_pairs={{0,4},{4,0},{8,12},{12,8},{16,20},{20,16},{24,28},{28,24},{1,5},{5... | collective-permute-start | bytes 196616 | tf_op jit(solution)/shard_map/ppermute | solution.py:18
  15.8 0.4 %collective-permute-done.4.got_ref = f32[128,128]{1,0:T(8,128)S(1)} collective-permute-done((f32[128,128]{1,0:T(8,128)S(1)}, f32[128,128]{1,0:T(8,128)S(1)}, u32[]{:S(2)}, u32[]{:S(2)}) %collective-permute-start.4) | collective-permute-done | bytes 65568 | tf_op jit(solution)/shard_map/ppermute | solution.py:18
  16.2 0.4 %level1_0.1.own_ref = f32[128,128]{1,0:T(8,128)S(1)} custom-call(f32[128,128]{1,0:T(8,128)S(1)} %level0_0.1.own_ref, f32[128,128]{1,0:T(8,128)S(1)} %collective-permute-done.4.got_ref, bf16[16,64,256]{2,1,0:T(8,128)(2,1)S(1)} %get-tuple-element.17.fh_ref, bf16[16,64,256]{2,1,0:T(8,128)(2,1)S(1)} %get-tuple-element.18.fl_ref), custom_call_target="tpu_custom_call" | custom-call | tf_op jit(solution)/shard_map/level1_0/pallas_call | solution.py:115
  16.5 1.8 %collective-permute-start.5 = (f32[128,128]{1,0:T(8,128)S(1)}, f32[128,128]{1,0:T(8,128)S(1)}, u32[]{:S(2)}, u32[]{:S(2)}) collective-permute-start(f32[128,128]{1,0:T(8,128)S(1)} %level1_0.1.own_ref), channel_id=1, source_target_pairs={{0,4},{4,0},{8,12},{12,8},{16,20},{20,16},{24,28},{28,24},{1,5},{5... | collective-permute-start | bytes 196616 | tf_op jit(solution)/shard_map/ppermute | solution.py:18
  18.3 0.1 collective-permute-done.2.got_ref
  18.4 0.4 %level2_1.1.done_ref = f32[128,128]{1,0:T(8,128)S(1)} custom-call(f32[128,128]{1,0:T(8,128)S(1)} %level1_1.1.own_ref, f32[128,128]{1,0:T(8,128)S(1)} %collective-permute-done.2.got_ref, bf16[16,64,256]{2,1,0:T(8,128)(2,1)S(1)} %get-tuple-element.19.fh_ref, bf16[16,64,256]{2,1,0:T(8,128)(2,1)S(1)} %get-tuple-element.20.fl_ref), custom_call_target="tpu_custom_call" | custom-call | tf_op jit(solution)/shard_map/level2_1/pallas_call | solution.py:115
  18.8 2.0 %collective-permute-done.5.got_ref = f32[128,128]{1,0:T(8,128)S(1)} collective-permute-done((f32[128,128]{1,0:T(8,128)S(1)}, f32[128,128]{1,0:T(8,128)S(1)}, u32[]{:S(2)}, u32[]{:S(2)}) %collective-permute-start.5) | collective-permute-done | bytes 65568 | tf_op jit(solution)/shard_map/ppermute | solution.py:18
  20.9 0.4 %level2_0.1 = (f32[2,16,256]{2,1,0:T(8,128)S(1)}, f32[2,16,256]{2,1,0:T(8,128)S(1)}, f32[2,16,256]{2,1,0:T(8,128)S(1)}, f32[2,16,256]{2,1,0:T(8,128)S(1)}) custom-call(s32[1]{0:T(128)} %bitcast.me_ref, f32[128,128]{1,0:T(8,128)S(1)} %level2_1.1.done_ref, f32[128,128]{1,0:T(8,128)S(1)} %level1_0.1.own_ref, f32[128,128]{1,0:T(8,128)S(1)} %collective-permute-done.5.got_ref, ...), custom_call_target="tpu_custom_call" | custom-call | tf_op jit(solution)/shard_map/level2_0/pallas_call | solution.py:115
  21.3 0.1 collective-permute-start.6
  21.4 1.8 %collective-permute-start.7 = (f32[2,16,256]{2,1,0:T(8,128)S(1)}, f32[2,16,256]{2,1,0:T(8,128)S(1)}, u32[]{:S(2)}, u32[]{:S(2)}) collective-permute-start(f32[2,16,256]{2,1,0:T(8,128)S(1)} %get-tuple-element.23), channel_id=1, source_target_pairs={{0,2},{1,3},{2,0},{3,1},{4,6},{5,7},{6,4},{7,5},{8,10},{9,11},{10,... | collective-permute-start | bytes 98312 | tf_op jit(solution)/shard_map/ppermute | solution.py:18
  23.2 0.1 collective-permute-start.8
  23.2 1.6 %collective-permute-done.6.refs_1_ = f32[2,16,256]{2,1,0:T(8,128)S(1)} collective-permute-done((f32[2,16,256]{2,1,0:T(8,128)S(1)}, f32[2,16,256]{2,1,0:T(8,128)S(1)}, u32[]{:S(2)}, u32[]{:S(2)}) %collective-permute-start.6) | collective-permute-done | bytes 32800 | tf_op jit(solution)/shard_map/ppermute | solution.py:18
  24.8 0.6 %collective-permute-done.7.refs_2_ = f32[2,16,256]{2,1,0:T(8,128)S(1)} collective-permute-done((f32[2,16,256]{2,1,0:T(8,128)S(1)}, f32[2,16,256]{2,1,0:T(8,128)S(1)}, u32[]{:S(2)}, u32[]{:S(2)}) %collective-permute-start.7) | collective-permute-done | bytes 32800 | tf_op jit(solution)/shard_map/ppermute | solution.py:18
  25.4 0.0 collective-permute-done.8.refs_3_
  25.4 0.6 %total.1 = f32[2,16,256]{2,1,0:T(8,128)} custom-call(f32[2,16,256]{2,1,0:T(8,128)S(1)} %get-tuple-element.21.refs_0_, f32[2,16,256]{2,1,0:T(8,128)S(1)} %collective-permute-done.6.refs_1_, f32[2,16,256]{2,1,0:T(8,128)S(1)} %collective-permute-done.7.refs_2_, f32[2,16,256]{2,1,0:T(8,128)S(1)} %collective-permute-done.8.refs_3_), custom_call_target="tpu_custom_call" | custom-call | tf_op jit(solution)/shard_map/total/pallas_call | solution.py:115
Async XLA Ops:
  0.9 7.8 %collective-permute-start = (f32[128,128]{1,0:T(8,128)S(1)}, f32[128,128]{1,0:T(8,128)S(1)}, u32[]{:S(2)}, u32[]{:S(2)}) collective-permute-start(f32[128,128]{1,0:T(8,128)S(1)} %get-tuple-element.26.own_ref), channel_id=1, source_target_pairs={{0,16},{4,20},{8,24},{12,28},{16,0},{20,4},{24,8},{28,12},{1,17},{... | collective-permute-start | bytes 196616 | tf_op jit(solution)/shard_map/ppermute | solution.py:18
  5.0 6.5 %collective-permute-start.3 = (f32[128,128]{1,0:T(8,128)S(1)}, f32[128,128]{1,0:T(8,128)S(1)}, u32[]{:S(2)}, u32[]{:S(2)}) collective-permute-start(f32[128,128]{1,0:T(8,128)S(1)} %get-tuple-element.25.own_ref), channel_id=1, source_target_pairs={{0,16},{4,20},{8,24},{12,28},{16,0},{20,4},{24,8},{28,12},{1,17},{... | collective-permute-start | bytes 196616 | tf_op jit(solution)/shard_map/ppermute | solution.py:18
  5.1 1.9 %copy-start = (f32[1,3,16,64,256]{4,3,2,1,0:T(8,128)S(1)}, f32[1,3,16,64,256]{4,3,2,1,0:T(8,128)}, u32[]{:S(2)}) copy-start(f32[1,3,16,64,256]{4,3,2,1,0:T(8,128)} %f_hbm.1) | copy-start | bytes 9437188
  9.0 4.4 %collective-permute-start.1 = (f32[128,128]{1,0:T(8,128)S(1)}, f32[128,128]{1,0:T(8,128)S(1)}, u32[]{:S(2)}, u32[]{:S(2)}) collective-permute-start(f32[128,128]{1,0:T(8,128)S(1)} %level0_1.1.own_ref), channel_id=1, source_target_pairs={{0,8},{4,12},{8,0},{12,4},{16,24},{20,28},{24,16},{28,20},{1,9},{5... | collective-permute-start | bytes 196616 | tf_op jit(solution)/shard_map/ppermute | solution.py:18
  11.8 4.3 %collective-permute-start.4 = (f32[128,128]{1,0:T(8,128)S(1)}, f32[128,128]{1,0:T(8,128)S(1)}, u32[]{:S(2)}, u32[]{:S(2)}) collective-permute-start(f32[128,128]{1,0:T(8,128)S(1)} %level0_0.1.own_ref), channel_id=1, source_target_pairs={{0,8},{4,12},{8,0},{12,4},{16,24},{20,28},{24,16},{28,20},{1,9},{5... | collective-permute-start | bytes 196616 | tf_op jit(solution)/shard_map/ppermute | solution.py:18
  13.8 4.7 %collective-permute-start.2 = (f32[128,128]{1,0:T(8,128)S(1)}, f32[128,128]{1,0:T(8,128)S(1)}, u32[]{:S(2)}, u32[]{:S(2)}) collective-permute-start(f32[128,128]{1,0:T(8,128)S(1)} %level1_1.1.own_ref), channel_id=1, source_target_pairs={{0,4},{4,0},{8,12},{12,8},{16,20},{20,16},{24,28},{28,24},{1,5},{5... | collective-permute-start | bytes 196616 | tf_op jit(solution)/shard_map/ppermute | solution.py:18
  16.5 4.3 %collective-permute-start.5 = (f32[128,128]{1,0:T(8,128)S(1)}, f32[128,128]{1,0:T(8,128)S(1)}, u32[]{:S(2)}, u32[]{:S(2)}) collective-permute-start(f32[128,128]{1,0:T(8,128)S(1)} %level1_0.1.own_ref), channel_id=1, source_target_pairs={{0,4},{4,0},{8,12},{12,8},{16,20},{20,16},{24,28},{28,24},{1,5},{5... | collective-permute-start | bytes 196616 | tf_op jit(solution)/shard_map/ppermute | solution.py:18
  21.3 3.5 %collective-permute-start.6 = (f32[2,16,256]{2,1,0:T(8,128)S(1)}, f32[2,16,256]{2,1,0:T(8,128)S(1)}, u32[]{:S(2)}, u32[]{:S(2)}) collective-permute-start(f32[2,16,256]{2,1,0:T(8,128)S(1)} %get-tuple-element.22), channel_id=1, source_target_pairs={{0,3},{1,2},{2,1},{3,0},{4,7},{5,6},{6,5},{7,4},{8,11},{9,10},{10,... | collective-permute-start | bytes 98312 | tf_op jit(solution)/shard_map/ppermute | solution.py:18
  21.4 4.0 %collective-permute-start.7 = (f32[2,16,256]{2,1,0:T(8,128)S(1)}, f32[2,16,256]{2,1,0:T(8,128)S(1)}, u32[]{:S(2)}, u32[]{:S(2)}) collective-permute-start(f32[2,16,256]{2,1,0:T(8,128)S(1)} %get-tuple-element.23), channel_id=1, source_target_pairs={{0,2},{1,3},{2,0},{3,1},{4,6},{5,7},{6,4},{7,5},{8,10},{9,11},{10,... | collective-permute-start | bytes 98312 | tf_op jit(solution)/shard_map/ppermute | solution.py:18
  23.2 2.3 %collective-permute-start.8 = (f32[2,16,256]{2,1,0:T(8,128)S(1)}, f32[2,16,256]{2,1,0:T(8,128)S(1)}, u32[]{:S(2)}, u32[]{:S(2)}) collective-permute-start(f32[2,16,256]{2,1,0:T(8,128)S(1)} %get-tuple-element.24), channel_id=1, source_target_pairs={{0,1},{1,0},{2,3},{3,2},{4,5},{5,4},{6,7},{7,6},{8,9},{9,8},{10,11... | collective-permute-start | bytes 98312 | tf_op jit(solution)/shard_map/ppermute | solution.py:18

commit v3 on v2

v3 whole, which is shorter than its diff:
```python
import functools
import jax
import jax.numpy as jnp
from jax import lax
from jax.experimental import pallas as pl
from jax.experimental.pallas import tpu as pltpu
from jax.sharding import PartitionSpec as P

LEVELS = 3
CHUNKS = 2
VMEM = pl.BlockSpec(memory_space=pltpu.MemorySpace.VMEM)
SMEM = pl.BlockSpec(memory_space=pltpu.MemorySpace.SMEM)
ANY = pl.BlockSpec(memory_space=pl.ANY)


def swapped(value, axis, mask):
    pairs = [(source, source ^ mask) for source in range(lax.axis_size(axis))]
    return lax.ppermute(value, axis, pairs)


def split(value):
    high = value.astype(jnp.bfloat16)
    low = (value - high.astype(jnp.float32)).astype(jnp.bfloat16)
    return high, low


def product(state, factor, width):
    rank, n = state.shape[0] // 2, state.shape[1]
    re, im = state[:rank], state[rank:]
    stack = jnp.concatenate(
        [jnp.concatenate([re, -im], axis=0), jnp.concatenate([im, re], axis=0)], axis=1
    )
    lane = lax.broadcasted_iota(jnp.int32, stack.shape, 1) % n
    zero = jnp.zeros_like(stack)
    stack = jnp.concatenate(
        [jnp.where(lane < n // 2, stack, zero), jnp.where(lane < n // 2, zero, stack)], axis=0
    )
    high, low = split(stack)
    rows = factor.shape[0] // 2
    dot = functools.partial(jnp.dot, preferred_element_type=jnp.float32)
    full = dot(factor[:rows], high) + dot(factor[:rows], low) + dot(factor[rows:], high)
    block = lax.broadcasted_iota(jnp.int32, (rank, 2 * n), 1) % (n // 2) // width
    out = full[:rank]
    for p in range(1, rows // rank):
        out = jnp.where(block == p, full[p * rank : (p + 1) * rank], out)
    return jnp.concatenate([out[:, :n], out[:, n:]], axis=0)


def prepare_kernel(f_hbm, *refs):
    *outs, f_ref, sems = refs
    copies = [
        pltpu.make_async_copy(f_hbm.at[0, i], f_ref.at[i], sems.at[i]) for i in range(LEVELS)
    ]
    for c in copies:
        c.start()
    rank, depth = f_ref.shape[2:]
    half = depth // 2
    for level in range(LEVELS):
        copies[level].wait()
        chunks, rows, _ = outs[2 * level].shape
        rows = rows // 2
        per = rows // rank
        for c in range(chunks):
            for u in range(2):
                first = (2 * c + u) * per
                high, low = split(f_ref[level, first : first + per].reshape(rows, depth))
                side = slice(u * half, (u + 1) * half)
                for part in range(2):
                    out = outs[2 * level + part]
                    out[c, :rows, side] = high[:, part * half : (part + 1) * half]
                    out[c, rows:, side] = low[:, part * half : (part + 1) * half]


def own_kernel(own_ref, f_ref, out_ref, *, i, width):
    out_ref[...] = product(own_ref[...], f_ref[i], width)


def level_kernel(base_ref, got_ref, f_ref, out_ref, *, i, width):
    out_ref[...] = base_ref[...] + product(got_ref[...], f_ref[i], width)


def last_kernel(me_ref, done_ref, base_ref, got_ref, f_ref, *refs, i, width):
    *outs, total_ref = refs
    n = got_ref.shape[1]
    other = 1 - i
    total_ref[:, other * n : (other + 1) * n] = done_ref[...]
    total_ref[:, i * n : (i + 1) * n] = base_ref[...] + product(got_ref[...], f_ref[i], width)
    rank = total_ref.shape[0] // 2
    share = rank // len(outs)
    for m, out in enumerate(outs):
        start = pl.multiple_of((me_ref[0] ^ m) * share, share)
        for q in range(2):
            out[q] = total_ref[pl.ds(q * rank + start, share), :]


def sum_kernel(*refs):
    *parts, out_ref = refs
    total = parts[0][...]
    for r in parts[1:]:
        total = total + r[...]
    out_ref[...] = total


def call(kernel, outs, *args, specs=None, scratch=(), name=None):
    return pl.pallas_call(
        kernel,
        out_shape=outs,
        in_specs=specs or [VMEM] * len(args),
        out_specs=jax.tree.map(lambda _: VMEM, outs),
        scratch_shapes=scratch,
        compiler_params=pltpu.CompilerParams(vmem_limit_bytes=16 * 2**20),
        name=name,
    )(*args)


def per_device(coefficients, factors):
    middle = (lax.axis_size("bis").bit_length() - 1) // 2
    rank, columns, blocks = coefficients.shape[2], coefficients.shape[3], factors.shape[2]
    width = columns // blocks
    step = columns // CHUNKS
    groups = lax.axis_size("src")
    f32 = jnp.float32
    raw = coefficients.reshape(2 * rank, columns)
    states = [raw[:, i * step : (i + 1) * step] for i in range(CHUNKS)]
    gots = [swapped(s, "bis", 2 ** (middle + 1)) for s in states]
    stacked = jax.ShapeDtypeStruct((CHUNKS, blocks // CHUNKS * rank, 4 * rank), jnp.bfloat16)
    halves = call(
        prepare_kernel, [stacked] * (2 * LEVELS), factors, specs=[ANY],
        scratch=[pltpu.VMEM(factors.shape[1:], f32), pltpu.SemaphoreType.DMA((LEVELS,))],
        name="prepare",
    )
    me = jnp.reshape(lax.axis_index("src"), (1,)).astype(jnp.int32)
    shape = jax.ShapeDtypeStruct((2 * rank, step), f32)
    piece = jax.ShapeDtypeStruct((2, rank // groups, columns), f32)
    order = tuple(reversed(range(CHUNKS)))
    for level in range(LEVELS):
        own, other = halves[2 * level : 2 * level + 2]
        for i in order:
            kw = dict(i=i, width=width)
            base = call(
                functools.partial(own_kernel, **kw), shape, states[i], own, name=f"own{level}_{i}"
            )
            if (level, i) == (LEVELS - 1, order[-1]):
                pieces = call(
                    functools.partial(last_kernel, **kw), [piece] * groups,
                    me, states[order[0]], base, gots[i], other, specs=[SMEM] + [VMEM] * 4,
                    scratch=[pltpu.VMEM((2 * rank, columns), f32)], name="last",
                )
                continue
            states[i] = call(
                functools.partial(level_kernel, **kw), shape, base, gots[i], other,
                name=f"level{level}_{i}",
            )
            if level < LEVELS - 1:
                gots[i] = swapped(states[i], "bis", 2 ** (middle - level))
    parts = [pieces[0]] + [swapped(pieces[m], "src", m) for m in reversed(range(1, groups))]
    return call(sum_kernel, piece, *parts, name="total")


def solution(mesh):
    placed = (P("src", None, None, "bis"), P("src", None, "bis", None, None))
    return jax.shard_map(
        per_device, mesh=mesh, in_specs=placed, out_specs=P(None, "src", "bis"), check_vma=False
    )
```

time: 26.3 us -> 26 us (0.989)
  waiting for transfers between devices: 6.98 us -> 5.45 us
  Pallas kernels: 3.58 us -> 4.69 us
    ppermute x9, waiting for transfers between devices: 6.98 us -> 5.45 us  [swapped(): return lax.ppermute(value, axis, pairs)]
    pallas_call x8 -> x14, Pallas kernels: 3.58 us -> 4.69 us  [call(): pl.pallas_call(kernel, out_shape=outs, in_specs=specs or [VMEM] * len(arg...]
  transfers between devices with their start and end apart: 9 -> 9, of which waited for: 8 -> 7; matrix products, arithmetic and copies ran while one was open for 0% -> 0% of each run, Pallas kernels for 10% -> 15%
where the time goes in v3:
time: 26 us; the launch traced here: 25.7 us
  starting transfers between devices  12.7 us (49%)
  waiting for transfers between devices  5.45 us (21%)
  Pallas kernels  4.69 us (18%)
  local copies, waits for them, and re-layouts  2.77 us (11%)
    ppermute x9, starting transfers between devices, swapped(): return lax.ppermute(value, axis, pairs)  12.7 us
    ppermute x9, waiting for transfers between devices, swapped(): return lax.ppermute(value, axis, pairs)  5.45 us
    pallas_call x14, Pallas kernels, call(): pl.pallas_call(kernel, out_shape=outs, in_specs=specs or [VMEM] * len(arg...  4.69 us
    unnamed x2, local copies, waits for them, and re-layouts  1.89 us
    slice x1, local copies, waits for them, and re-layouts, per_device(): states = [raw[:, i * step:(i + 1) * step] for i in range(CHUNKS)]  0.88 us
  transfers between devices with their start and end apart: 9, of which 7 were waited for; matrix products, arithmetic and copies ran while one was open for 0% of the time, Pallas kernels for 15%

profile of v3, /device:TPU:0, one launch (start us, length us, event | category | flops | bytes accessed | tf_op | source)
XLA Modules:
  0.0 25.7 jit_solution(17464347466409360195)
XLA Ops:
  0.0 0.9 %fusion = (f32[128,128]{1,0:T(8,128)S(1)}, f32[128,128]{1,0:T(8,128)S(1)}) fusion(f32[128,256]{1,0:T(8,128)} %bitcast.2), kind=kLoop, calls=%fused_computation | loop fusion | bytes 262144 | tf_op jit(solution)/shard_map/slice | solution.py:124
  0.9 4.1 %collective-permute-start = (f32[128,128]{1,0:T(8,128)S(1)}, f32[128,128]{1,0:T(8,128)S(1)}, u32[]{:S(2)}, u32[]{:S(2)}) collective-permute-start(f32[128,128]{1,0:T(8,128)S(1)} %get-tuple-element.26.own_ref), channel_id=1, source_target_pairs={{0,16},{4,20},{8,24},{12,28},{16,0},{20,4},{24,8},{28,12},{1,17},{... | collective-permute-start | bytes 196616 | tf_op jit(solution)/shard_map/ppermute | solution.py:18
  5.0 0.1 collective-permute-start.3
  5.1 0.0 copy-start
  5.1 1.9 %copy-done = f32[1,3,16,64,256]{4,3,2,1,0:T(8,128)S(1)} copy-done((f32[1,3,16,64,256]{4,3,2,1,0:T(8,128)S(1)}, f32[1,3,16,64,256]{4,3,2,1,0:T(8,128)}, u32[]{:S(2)}) %copy-start) | copy-done | bytes 3145752
  7.0 0.8 %prepare.1 = (bf16[2,512,256]{2,1,0:T(8,128)(2,1)S(1)}, bf16[2,512,256]{2,1,0:T(8,128)(2,1)S(1)}, bf16[2,512,256]{2,1,0:T(8,128)(2,1)S(1)}, bf16[2,512,256]{2,1,...) custom-call(f32[1,3,16,64,256]{4,3,2,1,0:T(8,128)S(1)} %copy-done), custom_call_target="tpu_custom_call" | custom-call | tf_op jit(solution)/shard_map/prepare/pallas_call | solution.py:105
  7.7 0.3 %own0_1.1.base_ref = f32[128,128]{1,0:T(8,128)S(1)} custom-call(f32[128,128]{1,0:T(8,128)S(1)} %get-tuple-element.26.own_ref, bf16[2,512,256]{2,1,0:T(8,128)(2,1)S(1)} %get-tuple-element.15.f_ref), custom_call_target="tpu_custom_call" | custom-call | tf_op jit(solution)/shard_map/own0_1/pallas_call | solution.py:105
  8.0 0.6 %collective-permute-done.got_ref = f32[128,128]{1,0:T(8,128)S(1)} collective-permute-done((f32[128,128]{1,0:T(8,128)S(1)}, f32[128,128]{1,0:T(8,128)S(1)}, u32[]{:S(2)}, u32[]{:S(2)}) %collective-permute-start) | collective-permute-done | bytes 65568 | tf_op jit(solution)/shard_map/ppermute | solution.py:18
  8.6 0.3 %level0_1.1.own_ref = f32[128,128]{1,0:T(8,128)S(1)} custom-call(f32[128,128]{1,0:T(8,128)S(1)} %own0_1.1.base_ref, f32[128,128]{1,0:T(8,128)S(1)} %collective-permute-done.got_ref, bf16[2,512,256]{2,1,0:T(8,128)(2,1)S(1)} %get-tuple-element.16.f_ref), custom_call_target="tpu_custom_call" | custom-call | tf_op jit(solution)/shard_map/level0_1/pallas_call | solution.py:105
  8.9 2.1 %collective-permute-start.1 = (f32[128,128]{1,0:T(8,128)S(1)}, f32[128,128]{1,0:T(8,128)S(1)}, u32[]{:S(2)}, u32[]{:S(2)}) collective-permute-start(f32[128,128]{1,0:T(8,128)S(1)} %level0_1.1.own_ref), channel_id=1, source_target_pairs={{0,8},{4,12},{8,0},{12,4},{16,24},{20,28},{24,16},{28,20},{1,9},{5... | collective-permute-start | bytes 196616 | tf_op jit(solution)/shard_map/ppermute | solution.py:18
  11.1 0.3 %own0_0.1.base_ref = f32[128,128]{1,0:T(8,128)S(1)} custom-call(f32[128,128]{1,0:T(8,128)S(1)} %get-tuple-element.25.own_ref, bf16[2,512,256]{2,1,0:T(8,128)(2,1)S(1)} %get-tuple-element.15.f_ref), custom_call_target="tpu_custom_call" | custom-call | tf_op jit(solution)/shard_map/own0_0/pallas_call | solution.py:105
  11.3 0.1 collective-permute-done.3.got_ref
  11.4 0.3 %level0_0.1.own_ref = f32[128,128]{1,0:T(8,128)S(1)} custom-call(f32[128,128]{1,0:T(8,128)S(1)} %own0_0.1.base_ref, f32[128,128]{1,0:T(8,128)S(1)} %collective-permute-done.3.got_ref, bf16[2,512,256]{2,1,0:T(8,128)(2,1)S(1)} %get-tuple-element.16.f_ref), custom_call_target="tpu_custom_call" | custom-call | tf_op jit(solution)/shard_map/level0_0/pallas_call | solution.py:105
  11.7 0.6 %collective-permute-start.4 = (f32[128,128]{1,0:T(8,128)S(1)}, f32[128,128]{1,0:T(8,128)S(1)}, u32[]{:S(2)}, u32[]{:S(2)}) collective-permute-start(f32[128,128]{1,0:T(8,128)S(1)} %level0_0.1.own_ref), channel_id=1, source_target_pairs={{0,8},{4,12},{8,0},{12,4},{16,24},{20,28},{24,16},{28,20},{1,9},{5... | collective-permute-start | bytes 196616 | tf_op jit(solution)/shard_map/ppermute | solution.py:18
  12.4 0.3 %own1_0.1.base_ref = f32[128,128]{1,0:T(8,128)S(1)} custom-call(f32[128,128]{1,0:T(8,128)S(1)} %level0_0.1.own_ref, bf16[2,512,256]{2,1,0:T(8,128)(2,1)S(1)} %get-tuple-element.17.f_ref), custom_call_target="tpu_custom_call" | custom-call | tf_op jit(solution)/shard_map/own1_0/pallas_call | solution.py:105
  12.6 0.3 %own1_1.1.base_ref = f32[128,128]{1,0:T(8,128)S(1)} custom-call(f32[128,128]{1,0:T(8,128)S(1)} %level0_1.1.own_ref, bf16[2,512,256]{2,1,0:T(8,128)(2,1)S(1)} %get-tuple-element.17.f_ref), custom_call_target="tpu_custom_call" | custom-call | tf_op jit(solution)/shard_map/own1_1/pallas_call | solution.py:105
  12.9 0.4 %collective-permute-done.1.got_ref = f32[128,128]{1,0:T(8,128)S(1)} collective-permute-done((f32[128,128]{1,0:T(8,128)S(1)}, f32[128,128]{1,0:T(8,128)S(1)}, u32[]{:S(2)}, u32[]{:S(2)}) %collective-permute-start.1) | collective-permute-done | bytes 65568 | tf_op jit(solution)/shard_map/ppermute | solution.py:18
  13.3 0.3 %level1_1.1.own_ref = f32[128,128]{1,0:T(8,128)S(1)} custom-call(f32[128,128]{1,0:T(8,128)S(1)} %own1_1.1.base_ref, f32[128,128]{1,0:T(8,128)S(1)} %collective-permute-done.1.got_ref, bf16[2,512,256]{2,1,0:T(8,128)(2,1)S(1)} %get-tuple-element.18.f_ref), custom_call_target="tpu_custom_call" | custom-call | tf_op jit(solution)/shard_map/level1_1/pallas_call | solution.py:105
  13.6 2.0 %collective-permute-start.2 = (f32[128,128]{1,0:T(8,128)S(1)}, f32[128,128]{1,0:T(8,128)S(1)}, u32[]{:S(2)}, u32[]{:S(2)}) collective-permute-start(f32[128,128]{1,0:T(8,128)S(1)} %level1_1.1.own_ref), channel_id=1, source_target_pairs={{0,4},{4,0},{8,12},{12,8},{16,20},{20,16},{24,28},{28,24},{1,5},{5... | collective-permute-start | bytes 196616 | tf_op jit(solution)/shard_map/ppermute | solution.py:18
  15.6 0.5 %collective-permute-done.4.got_ref = f32[128,128]{1,0:T(8,128)S(1)} collective-permute-done((f32[128,128]{1,0:T(8,128)S(1)}, f32[128,128]{1,0:T(8,128)S(1)}, u32[]{:S(2)}, u32[]{:S(2)}) %collective-permute-start.4) | collective-permute-done | bytes 65568 | tf_op jit(solution)/shard_map/ppermute | solution.py:18
  16.1 0.3 %level1_0.1.own_ref = f32[128,128]{1,0:T(8,128)S(1)} custom-call(f32[128,128]{1,0:T(8,128)S(1)} %own1_0.1.base_ref, f32[128,128]{1,0:T(8,128)S(1)} %collective-permute-done.4.got_ref, bf16[2,512,256]{2,1,0:T(8,128)(2,1)S(1)} %get-tuple-element.18.f_ref), custom_call_target="tpu_custom_call" | custom-call | tf_op jit(solution)/shard_map/level1_0/pallas_call | solution.py:105
  16.3 1.8 %collective-permute-start.5 = (f32[128,128]{1,0:T(8,128)S(1)}, f32[128,128]{1,0:T(8,128)S(1)}, u32[]{:S(2)}, u32[]{:S(2)}) collective-permute-start(f32[128,128]{1,0:T(8,128)S(1)} %level1_0.1.own_ref), channel_id=1, source_target_pairs={{0,4},{4,0},{8,12},{12,8},{16,20},{20,16},{24,28},{28,24},{1,5},{5... | collective-permute-start | bytes 196616 | tf_op jit(solution)/shard_map/ppermute | solution.py:18
  18.1 0.3 %own2_0.1.base_ref = f32[128,128]{1,0:T(8,128)S(1)} custom-call(f32[128,128]{1,0:T(8,128)S(1)} %level1_0.1.own_ref, bf16[2,512,256]{2,1,0:T(8,128)(2,1)S(1)} %get-tuple-element.19.f_ref), custom_call_target="tpu_custom_call" | custom-call | tf_op jit(solution)/shard_map/own2_0/pallas_call | solution.py:105
  18.4 0.3 %own2_1.1.base_ref = f32[128,128]{1,0:T(8,128)S(1)} custom-call(f32[128,128]{1,0:T(8,128)S(1)} %level1_1.1.own_ref, bf16[2,512,256]{2,1,0:T(8,128)(2,1)S(1)} %get-tuple-element.19.f_ref), custom_call_target="tpu_custom_call" | custom-call | tf_op jit(solution)/shard_map/own2_1/pallas_call | solution.py:105
  18.7 0.0 collective-permute-done.2.got_ref
  18.7 0.3 %level2_1.1.done_ref = f32[128,128]{1,0:T(8,128)S(1)} custom-call(f32[128,128]{1,0:T(8,128)S(1)} %own2_1.1.base_ref, f32[128,128]{1,0:T(8,128)S(1)} %collective-permute-done.2.got_ref, bf16[2,512,256]{2,1,0:T(8,128)(2,1)S(1)} %get-tuple-element.20.f_ref), custom_call_target="tpu_custom_call" | custom-call | tf_op jit(solution)/shard_map/level2_1/pallas_call | solution.py:105
  19.0 1.7 %collective-permute-done.5.got_ref = f32[128,128]{1,0:T(8,128)S(1)} collective-permute-done((f32[128,128]{1,0:T(8,128)S(1)}, f32[128,128]{1,0:T(8,128)S(1)}, u32[]{:S(2)}, u32[]{:S(2)}) %collective-permute-start.5) | collective-permute-done | bytes 65568 | tf_op jit(solution)/shard_map/ppermute | solution.py:18
  20.7 0.3 %last.1 = (f32[2,16,256]{2,1,0:T(8,128)S(1)}, f32[2,16,256]{2,1,0:T(8,128)S(1)}, f32[2,16,256]{2,1,0:T(8,128)S(1)}, f32[2,16,256]{2,1,0:T(8,128)S(1)}) custom-call(s32[1]{0:T(128)} %bitcast.me_ref, f32[128,128]{1,0:T(8,128)S(1)} %level2_1.1.done_ref, f32[128,128]{1,0:T(8,128)S(1)} %own2_0.1.base_ref, f32[128,128]{1,0:T(8,128)S(1)} %collective-permute-done.5.got_ref, ...), custom_call_target="tpu_custom_call" | custom-call | tf_op jit(solution)/shard_map/last/pallas_call | solution.py:105
  21.0 0.1 collective-permute-start.6
  21.0 1.8 %collective-permute-start.7 = (f32[2,16,256]{2,1,0:T(8,128)S(1)}, f32[2,16,256]{2,1,0:T(8,128)S(1)}, u32[]{:S(2)}, u32[]{:S(2)}) collective-permute-start(f32[2,16,256]{2,1,0:T(8,128)S(1)} %get-tuple-element.23), channel_id=1, source_target_pairs={{0,2},{1,3},{2,0},{3,1},{4,6},{5,7},{6,4},{7,5},{8,10},{9,11},{10,... | collective-permute-start | bytes 98312 | tf_op jit(solution)/shard_map/ppermute | solution.py:18
  22.8 0.1 collective-permute-start.8
  22.9 1.6 %collective-permute-done.6.refs_1_ = f32[2,16,256]{2,1,0:T(8,128)S(1)} collective-permute-done((f32[2,16,256]{2,1,0:T(8,128)S(1)}, f32[2,16,256]{2,1,0:T(8,128)S(1)}, u32[]{:S(2)}, u32[]{:S(2)}) %collective-permute-start.6) | collective-permute-done | bytes 32800 | tf_op jit(solution)/shard_map/ppermute | solution.py:18
  24.5 0.6 %collective-permute-done.7.refs_2_ = f32[2,16,256]{2,1,0:T(8,128)S(1)} collective-permute-done((f32[2,16,256]{2,1,0:T(8,128)S(1)}, f32[2,16,256]{2,1,0:T(8,128)S(1)}, u32[]{:S(2)}, u32[]{:S(2)}) %collective-permute-start.7) | collective-permute-done | bytes 32800 | tf_op jit(solution)/shard_map/ppermute | solution.py:18
  25.1 0.0 collective-permute-done.8.refs_3_
  25.1 0.6 %total.1 = f32[2,16,256]{2,1,0:T(8,128)} custom-call(f32[2,16,256]{2,1,0:T(8,128)S(1)} %get-tuple-element.21.refs_0_, f32[2,16,256]{2,1,0:T(8,128)S(1)} %collective-permute-done.6.refs_1_, f32[2,16,256]{2,1,0:T(8,128)S(1)} %collective-permute-done.7.refs_2_, f32[2,16,256]{2,1,0:T(8,128)S(1)} %collective-permute-done.8.refs_3_), custom_call_target="tpu_custom_call" | custom-call | tf_op jit(solution)/shard_map/total/pallas_call | solution.py:105
Async XLA Ops:
  0.9 7.8 %collective-permute-start = (f32[128,128]{1,0:T(8,128)S(1)}, f32[128,128]{1,0:T(8,128)S(1)}, u32[]{:S(2)}, u32[]{:S(2)}) collective-permute-start(f32[128,128]{1,0:T(8,128)S(1)} %get-tuple-element.26.own_ref), channel_id=1, source_target_pairs={{0,16},{4,20},{8,24},{12,28},{16,0},{20,4},{24,8},{28,12},{1,17},{... | collective-permute-start | bytes 196616 | tf_op jit(solution)/shard_map/ppermute | solution.py:18
  5.0 6.5 %collective-permute-start.3 = (f32[128,128]{1,0:T(8,128)S(1)}, f32[128,128]{1,0:T(8,128)S(1)}, u32[]{:S(2)}, u32[]{:S(2)}) collective-permute-start(f32[128,128]{1,0:T(8,128)S(1)} %get-tuple-element.25.own_ref), channel_id=1, source_target_pairs={{0,16},{4,20},{8,24},{12,28},{16,0},{20,4},{24,8},{28,12},{1,17},{... | collective-permute-start | bytes 196616 | tf_op jit(solution)/shard_map/ppermute | solution.py:18
  5.1 1.9 %copy-start = (f32[1,3,16,64,256]{4,3,2,1,0:T(8,128)S(1)}, f32[1,3,16,64,256]{4,3,2,1,0:T(8,128)}, u32[]{:S(2)}) copy-start(f32[1,3,16,64,256]{4,3,2,1,0:T(8,128)} %f_hbm.1) | copy-start | bytes 9437188
  8.9 4.4 %collective-permute-start.1 = (f32[128,128]{1,0:T(8,128)S(1)}, f32[128,128]{1,0:T(8,128)S(1)}, u32[]{:S(2)}, u32[]{:S(2)}) collective-permute-start(f32[128,128]{1,0:T(8,128)S(1)} %level0_1.1.own_ref), channel_id=1, source_target_pairs={{0,8},{4,12},{8,0},{12,4},{16,24},{20,28},{24,16},{28,20},{1,9},{5... | collective-permute-start | bytes 196616 | tf_op jit(solution)/shard_map/ppermute | solution.py:18
  11.7 4.3 %collective-permute-start.4 = (f32[128,128]{1,0:T(8,128)S(1)}, f32[128,128]{1,0:T(8,128)S(1)}, u32[]{:S(2)}, u32[]{:S(2)}) collective-permute-start(f32[128,128]{1,0:T(8,128)S(1)} %level0_0.1.own_ref), channel_id=1, source_target_pairs={{0,8},{4,12},{8,0},{12,4},{16,24},{20,28},{24,16},{28,20},{1,9},{5... | collective-permute-start | bytes 196616 | tf_op jit(solution)/shard_map/ppermute | solution.py:18
  13.6 5.1 %collective-permute-start.2 = (f32[128,128]{1,0:T(8,128)S(1)}, f32[128,128]{1,0:T(8,128)S(1)}, u32[]{:S(2)}, u32[]{:S(2)}) collective-permute-start(f32[128,128]{1,0:T(8,128)S(1)} %level1_1.1.own_ref), channel_id=1, source_target_pairs={{0,4},{4,0},{8,12},{12,8},{16,20},{20,16},{24,28},{28,24},{1,5},{5... | collective-permute-start | bytes 196616 | tf_op jit(solution)/shard_map/ppermute | solution.py:18
  16.3 4.3 %collective-permute-start.5 = (f32[128,128]{1,0:T(8,128)S(1)}, f32[128,128]{1,0:T(8,128)S(1)}, u32[]{:S(2)}, u32[]{:S(2)}) collective-permute-start(f32[128,128]{1,0:T(8,128)S(1)} %level1_0.1.own_ref), channel_id=1, source_target_pairs={{0,4},{4,0},{8,12},{12,8},{16,20},{20,16},{24,28},{28,24},{1,5},{5... | collective-permute-start | bytes 196616 | tf_op jit(solution)/shard_map/ppermute | solution.py:18
  21.0 3.5 %collective-permute-start.6 = (f32[2,16,256]{2,1,0:T(8,128)S(1)}, f32[2,16,256]{2,1,0:T(8,128)S(1)}, u32[]{:S(2)}, u32[]{:S(2)}) collective-permute-start(f32[2,16,256]{2,1,0:T(8,128)S(1)} %get-tuple-element.22), channel_id=1, source_target_pairs={{0,3},{1,2},{2,1},{3,0},{4,7},{5,6},{6,5},{7,4},{8,11},{9,10},{10,... | collective-permute-start | bytes 98312 | tf_op jit(solution)/shard_map/ppermute | solution.py:18
  21.0 4.0 %collective-permute-start.7 = (f32[2,16,256]{2,1,0:T(8,128)S(1)}, f32[2,16,256]{2,1,0:T(8,128)S(1)}, u32[]{:S(2)}, u32[]{:S(2)}) collective-permute-start(f32[2,16,256]{2,1,0:T(8,128)S(1)} %get-tuple-element.23), channel_id=1, source_target_pairs={{0,2},{1,3},{2,0},{3,1},{4,6},{5,7},{6,4},{7,5},{8,10},{9,11},{10,... | collective-permute-start | bytes 98312 | tf_op jit(solution)/shard_map/ppermute | solution.py:18
  22.8 2.3 %collective-permute-start.8 = (f32[2,16,256]{2,1,0:T(8,128)S(1)}, f32[2,16,256]{2,1,0:T(8,128)S(1)}, u32[]{:S(2)}, u32[]{:S(2)}) collective-permute-start(f32[2,16,256]{2,1,0:T(8,128)S(1)} %get-tuple-element.24), channel_id=1, source_target_pairs={{0,1},{1,0},{2,3},{3,2},{4,5},{5,4},{6,7},{7,6},{8,9},{9,8},{10,11... | collective-permute-start | bytes 98312 | tf_op jit(solution)/shard_map/ppermute | solution.py:18

commit v4 on v3

--- a/solution.py
+++ b/solution.py
@@ -44,6 +44,16 @@
     for p in range(1, rows // rank):
         out = jnp.where(block == p, full[p * rank : (p + 1) * rank], out)
     return jnp.concatenate([out[:, :n], out[:, n:]], axis=0)
+
+
+def arrange_kernel(me_ref, first_ref, second_ref, *outs):
+    first, second = first_ref[...], second_ref[...]
+    swap = me_ref[0] % 2 == 1
+    re, im = jnp.where(swap, second, first), jnp.where(swap, first, second)
+    n = outs[0].shape[1]
+    for i, out in enumerate(outs):
+        cols = slice(i * n, (i + 1) * n)
+        out[...] = jnp.concatenate([re[:, cols], im[:, cols]], axis=0)
 
 
 def prepare_kernel(f_hbm, *refs):
@@ -120,8 +130,18 @@
     step = columns // CHUNKS
     groups = lax.axis_size("src")
     f32 = jnp.float32
-    raw = coefficients.reshape(2 * rank, columns)
-    states = [raw[:, i * step : (i + 1) * step] for i in range(CHUNKS)]
+    me = lax.axis_index("src")
+    where = jnp.reshape(me, (1,)).astype(jnp.int32)
+    shape = jax.ShapeDtypeStruct((2 * rank, step), f32)
+    first = lax.dynamic_index_in_dim(coefficients[0], me % 2, 0, keepdims=False)
+    first, rest = lax.optimization_barrier((first, 1 - me % 2))
+    second = lax.dynamic_index_in_dim(coefficients[0], rest, 0, keepdims=False)
+    states = list(
+        call(
+            arrange_kernel, [shape] * CHUNKS, where, first, second, specs=[SMEM] + [VMEM] * 2,
+            name="arrange",
+        )
+    )
     gots = [swapped(s, "bis", 2 ** (middle + 1)) for s in states]
     stacked = jax.ShapeDtypeStruct((CHUNKS, blocks // CHUNKS * rank, 4 * rank), jnp.bfloat16)
     halves = call(
@@ -129,8 +149,6 @@
         scratch=[pltpu.VMEM(factors.shape[1:], f32), pltpu.SemaphoreType.DMA((LEVELS,))],
         name="prepare",
     )
-    me = jnp.reshape(lax.axis_index("src"), (1,)).astype(jnp.int32)
-    shape = jax.ShapeDtypeStruct((2 * rank, step), f32)
     piece = jax.ShapeDtypeStruct((2, rank // groups, columns), f32)
     order = tuple(reversed(range(CHUNKS)))
     for level in range(LEVELS):
@@ -143,7 +161,7 @@
             if (level, i) == (LEVELS - 1, order[-1]):
                 pieces = call(
                     functools.partial(last_kernel, **kw), [piece] * groups,
-                    me, states[order[0]], base, gots[i], other, specs=[SMEM] + [VMEM] * 4,
+                    where, states[order[0]], base, gots[i], other, specs=[SMEM] + [VMEM] * 4,
                     scratch=[pltpu.VMEM((2 * rank, columns), f32)], name="last",
                 )
                 continue

time: 26 us -> 26 us (level)
    unnamed x2 -> x4, local copies, waits for them, and re-layouts: 1.89 us -> 2.79 us
    slice x1 -> x0, local copies, waits for them, and re-layouts: 0.88 us -> none  [per_device(): states = [raw[:, i * step:(i + 1) * step] for i in range(CHUNKS)]]
    pallas_call x14 -> x15, Pallas kernels: 4.69 us -> 4.72 us  [call(): pl.pallas_call(kernel, out_shape=outs, in_specs=specs or [VMEM] * len(arg...]
where the time goes in v4:
time: 26 us; the launch traced here: 25.8 us
  starting transfers between devices  12.7 us (49%)
  waiting for transfers between devices  5.45 us (21%)
  Pallas kernels  4.72 us (18%)
  local copies, waits for them, and re-layouts  2.8 us (11%)
    ppermute x9, starting transfers between devices, swapped(): return lax.ppermute(value, axis, pairs)  12.7 us
    ppermute x9, waiting for transfers between devices, swapped(): return lax.ppermute(value, axis, pairs)  5.45 us
    pallas_call x15, Pallas kernels, call(): pl.pallas_call(kernel, out_shape=outs, in_specs=specs or [VMEM] * len(arg...  4.72 us
    unnamed x4, local copies, waits for them, and re-layouts  2.79 us
  transfers between devices with their start and end apart: 9, of which 7 were waited for; matrix products, arithmetic and copies ran while one was open for 0% of the time, Pallas kernels for 15%

profile of v4, /device:TPU:0, one launch (start us, length us, event | category | flops | bytes accessed | tf_op | source)
XLA Modules:
  0.0 25.8 jit_solution(9583347033406408214)
XLA Ops:
  0.0 0.0 copy-start
  0.0 0.9 %copy-done = f32[1,2,64,256]{3,2,1,0:T(8,128)S(1)} copy-done((f32[1,2,64,256]{3,2,1,0:T(8,128)S(1)}, f32[1,2,64,256]{3,2,1,0:T(8,128)}, u32[]{:S(2)}) %copy-start) | copy-done | bytes 131096
  0.9 4.1 %collective-permute-start = (f32[128,128]{1,0:T(8,128)S(1)}, f32[128,128]{1,0:T(8,128)S(1)}, u32[]{:S(2)}, u32[]{:S(2)}) collective-permute-start(f32[128,128]{1,0:T(8,128)S(1)} %get-tuple-element.21.own_ref), channel_id=1, source_target_pairs={{0,16},{4,20},{8,24},{12,28},{16,0},{20,4},{24,8},{28,12},{1,17},{... | collective-permute-start | bytes 196616 | tf_op jit(solution)/shard_map/ppermute | solution.py:18
  5.1 0.1 collective-permute-start.3
  5.1 0.0 copy-start.1
  5.1 1.9 %copy-done.1 = f32[1,3,16,64,256]{4,3,2,1,0:T(8,128)S(1)} copy-done((f32[1,3,16,64,256]{4,3,2,1,0:T(8,128)S(1)}, f32[1,3,16,64,256]{4,3,2,1,0:T(8,128)}, u32[]{:S(2)}) %copy-start.1) | copy-done | bytes 3145752
  7.0 0.8 %prepare.1 = (bf16[2,512,256]{2,1,0:T(8,128)(2,1)S(1)}, bf16[2,512,256]{2,1,0:T(8,128)(2,1)S(1)}, bf16[2,512,256]{2,1,0:T(8,128)(2,1)S(1)}, bf16[2,512,256]{2,1,...) custom-call(f32[1,3,16,64,256]{4,3,2,1,0:T(8,128)S(1)} %copy-done.1), custom_call_target="tpu_custom_call" | custom-call | tf_op jit(solution)/shard_map/prepare/pallas_call | solution.py:115
  7.8 0.3 %own0_1.1.base_ref = f32[128,128]{1,0:T(8,128)S(1)} custom-call(f32[128,128]{1,0:T(8,128)S(1)} %get-tuple-element.21.own_ref, bf16[2,512,256]{2,1,0:T(8,128)(2,1)S(1)} %get-tuple-element.22.f_ref), custom_call_target="tpu_custom_call" | custom-call | tf_op jit(solution)/shard_map/own0_1/pallas_call | solution.py:115
  8.1 0.6 %collective-permute-done.got_ref = f32[128,128]{1,0:T(8,128)S(1)} collective-permute-done((f32[128,128]{1,0:T(8,128)S(1)}, f32[128,128]{1,0:T(8,128)S(1)}, u32[]{:S(2)}, u32[]{:S(2)}) %collective-permute-start) | collective-permute-done | bytes 65568 | tf_op jit(solution)/shard_map/ppermute | solution.py:18
  8.7 0.3 %level0_1.1.own_ref = f32[128,128]{1,0:T(8,128)S(1)} custom-call(f32[128,128]{1,0:T(8,128)S(1)} %own0_1.1.base_ref, f32[128,128]{1,0:T(8,128)S(1)} %collective-permute-done.got_ref, bf16[2,512,256]{2,1,0:T(8,128)(2,1)S(1)} %get-tuple-element.23.f_ref), custom_call_target="tpu_custom_call" | custom-call | tf_op jit(solution)/shard_map/level0_1/pallas_call | solution.py:115
  9.0 2.1 %collective-permute-start.1 = (f32[128,128]{1,0:T(8,128)S(1)}, f32[128,128]{1,0:T(8,128)S(1)}, u32[]{:S(2)}, u32[]{:S(2)}) collective-permute-start(f32[128,128]{1,0:T(8,128)S(1)} %level0_1.1.own_ref), channel_id=1, source_target_pairs={{0,8},{4,12},{8,0},{12,4},{16,24},{20,28},{24,16},{28,20},{1,9},{5... | collective-permute-start | bytes 196616 | tf_op jit(solution)/shard_map/ppermute | solution.py:18
  11.1 0.3 %own0_0.1.base_ref = f32[128,128]{1,0:T(8,128)S(1)} custom-call(f32[128,128]{1,0:T(8,128)S(1)} %get-tuple-element.28.own_ref, bf16[2,512,256]{2,1,0:T(8,128)(2,1)S(1)} %get-tuple-element.22.f_ref), custom_call_target="tpu_custom_call" | custom-call | tf_op jit(solution)/shard_map/own0_0/pallas_call | solution.py:115
  11.4 0.1 collective-permute-done.3.got_ref
  11.5 0.3 %level0_0.1.own_ref = f32[128,128]{1,0:T(8,128)S(1)} custom-call(f32[128,128]{1,0:T(8,128)S(1)} %own0_0.1.base_ref, f32[128,128]{1,0:T(8,128)S(1)} %collective-permute-done.3.got_ref, bf16[2,512,256]{2,1,0:T(8,128)(2,1)S(1)} %get-tuple-element.23.f_ref), custom_call_target="tpu_custom_call" | custom-call | tf_op jit(solution)/shard_map/level0_0/pallas_call | solution.py:115
  11.8 0.6 %collective-permute-start.4 = (f32[128,128]{1,0:T(8,128)S(1)}, f32[128,128]{1,0:T(8,128)S(1)}, u32[]{:S(2)}, u32[]{:S(2)}) collective-permute-start(f32[128,128]{1,0:T(8,128)S(1)} %level0_0.1.own_ref), channel_id=1, source_target_pairs={{0,8},{4,12},{8,0},{12,4},{16,24},{20,28},{24,16},{28,20},{1,9},{5... | collective-permute-start | bytes 196616 | tf_op jit(solution)/shard_map/ppermute | solution.py:18
  12.4 0.3 %own1_0.1.base_ref = f32[128,128]{1,0:T(8,128)S(1)} custom-call(f32[128,128]{1,0:T(8,128)S(1)} %level0_0.1.own_ref, bf16[2,512,256]{2,1,0:T(8,128)(2,1)S(1)} %get-tuple-element.24.f_ref), custom_call_target="tpu_custom_call" | custom-call | tf_op jit(solution)/shard_map/own1_0/pallas_call | solution.py:115
  12.7 0.3 %own1_1.1.base_ref = f32[128,128]{1,0:T(8,128)S(1)} custom-call(f32[128,128]{1,0:T(8,128)S(1)} %level0_1.1.own_ref, bf16[2,512,256]{2,1,0:T(8,128)(2,1)S(1)} %get-tuple-element.24.f_ref), custom_call_target="tpu_custom_call" | custom-call | tf_op jit(solution)/shard_map/own1_1/pallas_call | solution.py:115
  13.0 0.4 %collective-permute-done.1.got_ref = f32[128,128]{1,0:T(8,128)S(1)} collective-permute-done((f32[128,128]{1,0:T(8,128)S(1)}, f32[128,128]{1,0:T(8,128)S(1)}, u32[]{:S(2)}, u32[]{:S(2)}) %collective-permute-start.1) | collective-permute-done | bytes 65568 | tf_op jit(solution)/shard_map/ppermute | solution.py:18
  13.4 0.3 %level1_1.1.own_ref = f32[128,128]{1,0:T(8,128)S(1)} custom-call(f32[128,128]{1,0:T(8,128)S(1)} %own1_1.1.base_ref, f32[128,128]{1,0:T(8,128)S(1)} %collective-permute-done.1.got_ref, bf16[2,512,256]{2,1,0:T(8,128)(2,1)S(1)} %get-tuple-element.25.f_ref), custom_call_target="tpu_custom_call" | custom-call | tf_op jit(solution)/shard_map/level1_1/pallas_call | solution.py:115
  13.6 2.0 %collective-permute-start.2 = (f32[128,128]{1,0:T(8,128)S(1)}, f32[128,128]{1,0:T(8,128)S(1)}, u32[]{:S(2)}, u32[]{:S(2)}) collective-permute-start(f32[128,128]{1,0:T(8,128)S(1)} %level1_1.1.own_ref), channel_id=1, source_target_pairs={{0,4},{4,0},{8,12},{12,8},{16,20},{20,16},{24,28},{28,24},{1,5},{5... | collective-permute-start | bytes 196616 | tf_op jit(solution)/shard_map/ppermute | solution.py:18
  15.6 0.5 %collective-permute-done.4.got_ref = f32[128,128]{1,0:T(8,128)S(1)} collective-permute-done((f32[128,128]{1,0:T(8,128)S(1)}, f32[128,128]{1,0:T(8,128)S(1)}, u32[]{:S(2)}, u32[]{:S(2)}) %collective-permute-start.4) | collective-permute-done | bytes 65568 | tf_op jit(solution)/shard_map/ppermute | solution.py:18
  16.1 0.3 %level1_0.1.own_ref = f32[128,128]{1,0:T(8,128)S(1)} custom-call(f32[128,128]{1,0:T(8,128)S(1)} %own1_0.1.base_ref, f32[128,128]{1,0:T(8,128)S(1)} %collective-permute-done.4.got_ref, bf16[2,512,256]{2,1,0:T(8,128)(2,1)S(1)} %get-tuple-element.25.f_ref), custom_call_target="tpu_custom_call" | custom-call | tf_op jit(solution)/shard_map/level1_0/pallas_call | solution.py:115
  16.4 1.8 %collective-permute-start.5 = (f32[128,128]{1,0:T(8,128)S(1)}, f32[128,128]{1,0:T(8,128)S(1)}, u32[]{:S(2)}, u32[]{:S(2)}) collective-permute-start(f32[128,128]{1,0:T(8,128)S(1)} %level1_0.1.own_ref), channel_id=1, source_target_pairs={{0,4},{4,0},{8,12},{12,8},{16,20},{20,16},{24,28},{28,24},{1,5},{5... | collective-permute-start | bytes 196616 | tf_op jit(solution)/shard_map/ppermute | solution.py:18
  18.2 0.3 %own2_0.1.base_ref = f32[128,128]{1,0:T(8,128)S(1)} custom-call(f32[128,128]{1,0:T(8,128)S(1)} %level1_0.1.own_ref, bf16[2,512,256]{2,1,0:T(8,128)(2,1)S(1)} %get-tuple-element.26.f_ref), custom_call_target="tpu_custom_call" | custom-call | tf_op jit(solution)/shard_map/own2_0/pallas_call | solution.py:115
  18.5 0.3 %own2_1.1.base_ref = f32[128,128]{1,0:T(8,128)S(1)} custom-call(f32[128,128]{1,0:T(8,128)S(1)} %level1_1.1.own_ref, bf16[2,512,256]{2,1,0:T(8,128)(2,1)S(1)} %get-tuple-element.26.f_ref), custom_call_target="tpu_custom_call" | custom-call | tf_op jit(solution)/shard_map/own2_1/pallas_call | solution.py:115
  18.8 0.0 collective-permute-done.2.got_ref
  18.8 0.3 %level2_1.1.done_ref = f32[128,128]{1,0:T(8,128)S(1)} custom-call(f32[128,128]{1,0:T(8,128)S(1)} %own2_1.1.base_ref, f32[128,128]{1,0:T(8,128)S(1)} %collective-permute-done.2.got_ref, bf16[2,512,256]{2,1,0:T(8,128)(2,1)S(1)} %get-tuple-element.27.f_ref), custom_call_target="tpu_custom_call" | custom-call | tf_op jit(solution)/shard_map/level2_1/pallas_call | solution.py:115
  19.1 1.7 %collective-permute-done.5.got_ref = f32[128,128]{1,0:T(8,128)S(1)} collective-permute-done((f32[128,128]{1,0:T(8,128)S(1)}, f32[128,128]{1,0:T(8,128)S(1)}, u32[]{:S(2)}, u32[]{:S(2)}) %collective-permute-start.5) | collective-permute-done | bytes 65568 | tf_op jit(solution)/shard_map/ppermute | solution.py:18
  20.7 0.3 %last.1 = (f32[2,16,256]{2,1,0:T(8,128)S(1)}, f32[2,16,256]{2,1,0:T(8,128)S(1)}, f32[2,16,256]{2,1,0:T(8,128)S(1)}, f32[2,16,256]{2,1,0:T(8,128)S(1)}) custom-call(s32[1]{0:T(128)} %bitcast.me_ref, f32[128,128]{1,0:T(8,128)S(1)} %level2_1.1.done_ref, f32[128,128]{1,0:T(8,128)S(1)} %own2_0.1.base_ref, f32[128,128]{1,0:T(8,128)S(1)} %collective-permute-done.5.got_ref, ...), custom_call_target="tpu_custom_call" | custom-call | tf_op jit(solution)/shard_map/last/pallas_call | solution.py:115
  21.0 0.1 collective-permute-start.6
  21.1 1.8 %collective-permute-start.7 = (f32[2,16,256]{2,1,0:T(8,128)S(1)}, f32[2,16,256]{2,1,0:T(8,128)S(1)}, u32[]{:S(2)}, u32[]{:S(2)}) collective-permute-start(f32[2,16,256]{2,1,0:T(8,128)S(1)} %get-tuple-element.31), channel_id=1, source_target_pairs={{0,2},{1,3},{2,0},{3,1},{4,6},{5,7},{6,4},{7,5},{8,10},{9,11},{10,... | collective-permute-start | bytes 98312 | tf_op jit(solution)/shard_map/ppermute | solution.py:18
  22.9 0.1 collective-permute-start.8
  23.0 1.6 %collective-permute-done.6.refs_1_ = f32[2,16,256]{2,1,0:T(8,128)S(1)} collective-permute-done((f32[2,16,256]{2,1,0:T(8,128)S(1)}, f32[2,16,256]{2,1,0:T(8,128)S(1)}, u32[]{:S(2)}, u32[]{:S(2)}) %collective-permute-start.6) | collective-permute-done | bytes 32800 | tf_op jit(solution)/shard_map/ppermute | solution.py:18
  24.5 0.6 %collective-permute-done.7.refs_2_ = f32[2,16,256]{2,1,0:T(8,128)S(1)} collective-permute-done((f32[2,16,256]{2,1,0:T(8,128)S(1)}, f32[2,16,256]{2,1,0:T(8,128)S(1)}, u32[]{:S(2)}, u32[]{:S(2)}) %collective-permute-start.7) | collective-permute-done | bytes 32800 | tf_op jit(solution)/shard_map/ppermute | solution.py:18
  25.1 0.0 collective-permute-done.8.refs_3_
  25.1 0.6 %total.1 = f32[2,16,256]{2,1,0:T(8,128)} custom-call(f32[2,16,256]{2,1,0:T(8,128)S(1)} %get-tuple-element.29.refs_0_, f32[2,16,256]{2,1,0:T(8,128)S(1)} %collective-permute-done.6.refs_1_, f32[2,16,256]{2,1,0:T(8,128)S(1)} %collective-permute-done.7.refs_2_, f32[2,16,256]{2,1,0:T(8,128)S(1)} %collective-permute-done.8.refs_3_), custom_call_target="tpu_custom_call" | custom-call | tf_op jit(solution)/shard_map/total/pallas_call | solution.py:115
  (3 shorter events, 0.0 us)
Async XLA Ops:
  0.0 0.9 %copy-start = (f32[1,2,64,256]{3,2,1,0:T(8,128)S(1)}, f32[1,2,64,256]{3,2,1,0:T(8,128)}, u32[]{:S(2)}) copy-start(f32[1,2,64,256]{3,2,1,0:T(8,128)} %param.2) | copy-start | bytes 393220
  0.9 7.8 %collective-permute-start = (f32[128,128]{1,0:T(8,128)S(1)}, f32[128,128]{1,0:T(8,128)S(1)}, u32[]{:S(2)}, u32[]{:S(2)}) collective-permute-start(f32[128,128]{1,0:T(8,128)S(1)} %get-tuple-element.21.own_ref), channel_id=1, source_target_pairs={{0,16},{4,20},{8,24},{12,28},{16,0},{20,4},{24,8},{28,12},{1,17},{... | collective-permute-start | bytes 196616 | tf_op jit(solution)/shard_map/ppermute | solution.py:18
  5.1 6.5 %collective-permute-start.3 = (f32[128,128]{1,0:T(8,128)S(1)}, f32[128,128]{1,0:T(8,128)S(1)}, u32[]{:S(2)}, u32[]{:S(2)}) collective-permute-start(f32[128,128]{1,0:T(8,128)S(1)} %get-tuple-element.28.own_ref), channel_id=1, source_target_pairs={{0,16},{4,20},{8,24},{12,28},{16,0},{20,4},{24,8},{28,12},{1,17},{... | collective-permute-start | bytes 196616 | tf_op jit(solution)/shard_map/ppermute | solution.py:18
  5.1 1.9 %copy-start.1 = (f32[1,3,16,64,256]{4,3,2,1,0:T(8,128)S(1)}, f32[1,3,16,64,256]{4,3,2,1,0:T(8,128)}, u32[]{:S(2)}) copy-start(f32[1,3,16,64,256]{4,3,2,1,0:T(8,128)} %f_hbm.1) | copy-start | bytes 9437188
  9.0 4.4 %collective-permute-start.1 = (f32[128,128]{1,0:T(8,128)S(1)}, f32[128,128]{1,0:T(8,128)S(1)}, u32[]{:S(2)}, u32[]{:S(2)}) collective-permute-start(f32[128,128]{1,0:T(8,128)S(1)} %level0_1.1.own_ref), channel_id=1, source_target_pairs={{0,8},{4,12},{8,0},{12,4},{16,24},{20,28},{24,16},{28,20},{1,9},{5... | collective-permute-start | bytes 196616 | tf_op jit(solution)/shard_map/ppermute | solution.py:18
  11.8 4.3 %collective-permute-start.4 = (f32[128,128]{1,0:T(8,128)S(1)}, f32[128,128]{1,0:T(8,128)S(1)}, u32[]{:S(2)}, u32[]{:S(2)}) collective-permute-start(f32[128,128]{1,0:T(8,128)S(1)} %level0_0.1.own_ref), channel_id=1, source_target_pairs={{0,8},{4,12},{8,0},{12,4},{16,24},{20,28},{24,16},{28,20},{1,9},{5... | collective-permute-start | bytes 196616 | tf_op jit(solution)/shard_map/ppermute | solution.py:18
  13.6 5.1 %collective-permute-start.2 = (f32[128,128]{1,0:T(8,128)S(1)}, f32[128,128]{1,0:T(8,128)S(1)}, u32[]{:S(2)}, u32[]{:S(2)}) collective-permute-start(f32[128,128]{1,0:T(8,128)S(1)} %level1_1.1.own_ref), channel_id=1, source_target_pairs={{0,4},{4,0},{8,12},{12,8},{16,20},{20,16},{24,28},{28,24},{1,5},{5... | collective-permute-start | bytes 196616 | tf_op jit(solution)/shard_map/ppermute | solution.py:18
  16.4 4.3 %collective-permute-start.5 = (f32[128,128]{1,0:T(8,128)S(1)}, f32[128,128]{1,0:T(8,128)S(1)}, u32[]{:S(2)}, u32[]{:S(2)}) collective-permute-start(f32[128,128]{1,0:T(8,128)S(1)} %level1_0.1.own_ref), channel_id=1, source_target_pairs={{0,4},{4,0},{8,12},{12,8},{16,20},{20,16},{24,28},{28,24},{1,5},{5... | collective-permute-start | bytes 196616 | tf_op jit(solution)/shard_map/ppermute | solution.py:18
  21.0 3.5 %collective-permute-start.6 = (f32[2,16,256]{2,1,0:T(8,128)S(1)}, f32[2,16,256]{2,1,0:T(8,128)S(1)}, u32[]{:S(2)}, u32[]{:S(2)}) collective-permute-start(f32[2,16,256]{2,1,0:T(8,128)S(1)} %get-tuple-element.30), channel_id=1, source_target_pairs={{0,3},{1,2},{2,1},{3,0},{4,7},{5,6},{6,5},{7,4},{8,11},{9,10},{10,... | collective-permute-start | bytes 98312 | tf_op jit(solution)/shard_map/ppermute | solution.py:18
  21.1 4.0 %collective-permute-start.7 = (f32[2,16,256]{2,1,0:T(8,128)S(1)}, f32[2,16,256]{2,1,0:T(8,128)S(1)}, u32[]{:S(2)}, u32[]{:S(2)}) collective-permute-start(f32[2,16,256]{2,1,0:T(8,128)S(1)} %get-tuple-element.31), channel_id=1, source_target_pairs={{0,2},{1,3},{2,0},{3,1},{4,6},{5,7},{6,4},{7,5},{8,10},{9,11},{10,... | collective-permute-start | bytes 98312 | tf_op jit(solution)/shard_map/ppermute | solution.py:18
  22.9 2.3 %collective-permute-start.8 = (f32[2,16,256]{2,1,0:T(8,128)S(1)}, f32[2,16,256]{2,1,0:T(8,128)S(1)}, u32[]{:S(2)}, u32[]{:S(2)}) collective-permute-start(f32[2,16,256]{2,1,0:T(8,128)S(1)} %get-tuple-element.32), channel_id=1, source_target_pairs={{0,1},{1,0},{2,3},{3,2},{4,5},{5,4},{6,7},{7,6},{8,9},{9,8},{10,11... | collective-permute-start | bytes 98312 | tf_op jit(solution)/shard_map/ppermute | solution.py:18

commit v5 on v3

--- a/solution.py
+++ b/solution.py
@@ -47,16 +47,10 @@
 
 
 def prepare_kernel(f_hbm, *refs):
-    *outs, f_ref, sems = refs
-    copies = [
-        pltpu.make_async_copy(f_hbm.at[0, i], f_ref.at[i], sems.at[i]) for i in range(LEVELS)
-    ]
-    for c in copies:
-        c.start()
+    outs, f_ref = refs, f_hbm.at[0]
     rank, depth = f_ref.shape[2:]
     half = depth // 2
     for level in range(LEVELS):
-        copies[level].wait()
         chunks, rows, _ = outs[2 * level].shape
         rows = rows // 2
         per = rows // rank
@@ -73,6 +67,12 @@
 
 def own_kernel(own_ref, f_ref, out_ref, *, i, width):
     out_ref[...] = product(own_ref[...], f_ref[i], width)
+
+
+def owns_kernel(*refs, width):
+    f_ref = refs[CHUNKS]
+    for i, out in enumerate(refs[CHUNKS + 1 :]):
+        out[...] = product(refs[i][...], f_ref[i], width)
 
 
 def level_kernel(base_ref, got_ref, f_ref, out_ref, *, i, width):
@@ -121,13 +121,13 @@
     groups = lax.axis_size("src")
     f32 = jnp.float32
     raw = coefficients.reshape(2 * rank, columns)
-    states = [raw[:, i * step : (i + 1) * step] for i in range(CHUNKS)]
+    one = raw[:, step:]
+    one, rest = lax.optimization_barrier((one, raw))
+    states = [rest[:, :step], one]
     gots = [swapped(s, "bis", 2 ** (middle + 1)) for s in states]
     stacked = jax.ShapeDtypeStruct((CHUNKS, blocks // CHUNKS * rank, 4 * rank), jnp.bfloat16)
     halves = call(
-        prepare_kernel, [stacked] * (2 * LEVELS), factors, specs=[ANY],
-        scratch=[pltpu.VMEM(factors.shape[1:], f32), pltpu.SemaphoreType.DMA((LEVELS,))],
-        name="prepare",
+        prepare_kernel, [stacked] * (2 * LEVELS), factors, name="prepare",
     )
     me = jnp.reshape(lax.axis_index("src"), (1,)).astype(jnp.int32)
     shape = jax.ShapeDtypeStruct((2 * rank, step), f32)
@@ -137,9 +137,17 @@
         own, other = halves[2 * level : 2 * level + 2]
         for i in order:
             kw = dict(i=i, width=width)
-            base = call(
-                functools.partial(own_kernel, **kw), shape, states[i], own, name=f"own{level}_{i}"
-            )
+            if level:
+                base = call(
+                    functools.partial(own_kernel, **kw), shape, states[i], own, name=f"own{level}_{i}"
+                )
+            else:
+                if i == order[0]:
+                    bases = call(
+                        functools.partial(owns_kernel, width=width), [shape] * CHUNKS, *states, own,
+                        name="own0",
+                    )
+                base = bases[i]
             if (level, i) == (LEVELS - 1, order[-1]):
                 pieces = call(
                     functools.partial(last_kernel, **kw), [piece] * groups,

time: 26 us -> 25.9 us (level)
  waiting for transfers between devices: 5.45 us -> 4.54 us
  local copies, waits for them, and re-layouts: 2.77 us -> 3.57 us
  Pallas kernels: 4.69 us -> 4.31 us
    ppermute x9, waiting for transfers between devices: 5.45 us -> 4.54 us  [swapped(): return lax.ppermute(value, axis, pairs)]
    slice x1 -> x2, local copies, waits for them, and re-layouts: 0.88 us -> 1.69 us  [the longest x1 0.84 us: per_device(): states = [rest[:, :step], one]]
    pallas_call x14 -> x13, Pallas kernels: 4.69 us -> 4.31 us  [call(): pl.pallas_call(kernel, out_shape=outs, in_specs=specs or [VMEM] * len(arg...]
  transfers between devices with their start and end apart: 9 -> 9, of which waited for: 7 -> 6; matrix products, arithmetic and copies ran while one was open for 0% -> 3% of each run, Pallas kernels for 15% -> 13%
where the time goes in v5:
time: 25.9 us; the launch traced here: 25.5 us
  starting transfers between devices  12.9 us (50%)
  waiting for transfers between devices  4.54 us (18%)
  Pallas kernels  4.31 us (17%)
  local copies, waits for them, and re-layouts  3.57 us (14%)
    ppermute x9, starting transfers between devices, swapped(): return lax.ppermute(value, axis, pairs)  12.9 us
    ppermute x9, waiting for transfers between devices, swapped(): return lax.ppermute(value, axis, pairs)  4.54 us
    pallas_call x13, Pallas kernels, call(): pl.pallas_call(kernel, out_shape=outs, in_specs=specs or [VMEM] * len(arg...  4.31 us
    unnamed x2, local copies, waits for them, and re-layouts  1.88 us
    slice x1, local copies, waits for them, and re-layouts, per_device(): states = [rest[:, :step], one]  0.84 us
    slice x1, local copies, waits for them, and re-layouts, per_device(): one = raw[:, step:]  0.84 us
  transfers between devices with their start and end apart: 9, of which 6 were waited for; matrix products, arithmetic and copies ran while one was open for 3% of the time, Pallas kernels for 13%

profile of v5, /device:TPU:0, one launch (start us, length us, event | category | flops | bytes accessed | tf_op | source)
XLA Modules:
  0.0 25.5 jit_solution(4501603421469491576)
XLA Ops:
  0.0 0.8 %slice.8.refs_1_ = f32[128,128]{1,0:T(8,128)S(1)} slice(f32[128,256]{1,0:T(8,128)} %bitcast.2), slice={[0:128], [128:256]} | slice | bytes 131072 | tf_op jit(solution)/shard_map/slice | solution.py:124
  0.8 4.0 %collective-permute-start = (f32[128,128]{1,0:T(8,128)S(1)}, f32[128,128]{1,0:T(8,128)S(1)}, u32[]{:S(2)}, u32[]{:S(2)}) collective-permute-start(f32[128,128]{1,0:T(8,128)S(1)} %slice.8.refs_1_), channel_id=1, source_target_pairs={{0,16},{4,20},{8,24},{12,28},{16,0},{20,4},{24,8},{28,12},{1,17},{... | collective-permute-start | bytes 196616 | tf_op jit(solution)/shard_map/ppermute | solution.py:18
  4.9 0.8 %slice.7.refs_0_ = f32[128,128]{1,0:T(8,128)S(1)} slice(f32[128,256]{1,0:T(8,128)} %bitcast.3), slice={[0:128], [0:128]} | slice | bytes 131072 | tf_op jit(solution)/shard_map/slice | solution.py:126
  5.7 0.0 collective-permute-start.3
  5.7 0.0 copy-start
  5.7 1.9 %copy-done = f32[1,3,16,64,256]{4,3,2,1,0:T(8,128)S(1)} copy-done((f32[1,3,16,64,256]{4,3,2,1,0:T(8,128)S(1)}, f32[1,3,16,64,256]{4,3,2,1,0:T(8,128)}, u32[]{:S(2)}) %copy-start) | copy-done | bytes 3145752
  7.6 0.5 %prepare.1 = (bf16[2,512,256]{2,1,0:T(8,128)(2,1)S(1)}, bf16[2,512,256]{2,1,0:T(8,128)(2,1)S(1)}, bf16[2,512,256]{2,1,0:T(8,128)(2,1)S(1)}, bf16[2,512,256]{2,1,...) custom-call(f32[1,3,16,64,256]{4,3,2,1,0:T(8,128)S(1)} %copy-done), custom_call_target="tpu_custom_call" | custom-call | tf_op jit(solution)/shard_map/prepare/pallas_call | solution.py:105
  8.1 0.4 %own0.1 = (f32[128,128]{1,0:T(8,128)S(1)}, f32[128,128]{1,0:T(8,128)S(1)}) custom-call(f32[128,128]{1,0:T(8,128)S(1)} %slice.7.refs_0_, f32[128,128]{1,0:T(8,128)S(1)} %slice.8.refs_1_, bf16[2,512,256]{2,1,0:T(8,128)(2,1)S(1)} %get-tuple-element.21.refs_2_), custom_call_target="tpu_custom_call" | custom-call | tf_op jit(solution)/shard_map/own0/pallas_call | solution.py:105
  8.6 0.0 collective-permute-done.got_ref
  8.6 0.3 %level0_1.1.own_ref = f32[128,128]{1,0:T(8,128)S(1)} custom-call(f32[128,128]{1,0:T(8,128)S(1)} %get-tuple-element.22.base_ref, f32[128,128]{1,0:T(8,128)S(1)} %collective-permute-done.got_ref, bf16[2,512,256]{2,1,0:T(8,128)(2,1)S(1)} %get-tuple-element.23.f_ref), custom_call_target="tpu_custom_call" | custom-call | tf_op jit(solution)/shard_map/level0_1/pallas_call | solution.py:105
  8.8 2.1 %collective-permute-start.1 = (f32[128,128]{1,0:T(8,128)S(1)}, f32[128,128]{1,0:T(8,128)S(1)}, u32[]{:S(2)}, u32[]{:S(2)}) collective-permute-start(f32[128,128]{1,0:T(8,128)S(1)} %level0_1.1.own_ref), channel_id=1, source_target_pairs={{0,8},{4,12},{8,0},{12,4},{16,24},{20,28},{24,16},{28,20},{1,9},{5... | collective-permute-start | bytes 196616 | tf_op jit(solution)/shard_map/ppermute | solution.py:18
  11.0 0.2 collective-permute-done.3.got_ref
  11.2 0.3 %level0_0.1.own_ref = f32[128,128]{1,0:T(8,128)S(1)} custom-call(f32[128,128]{1,0:T(8,128)S(1)} %get-tuple-element.28.base_ref, f32[128,128]{1,0:T(8,128)S(1)} %collective-permute-done.3.got_ref, bf16[2,512,256]{2,1,0:T(8,128)(2,1)S(1)} %get-tuple-element.23.f_ref), custom_call_target="tpu_custom_call" | custom-call | tf_op jit(solution)/shard_map/level0_0/pallas_call | solution.py:105
  11.5 1.3 %collective-permute-start.4 = (f32[128,128]{1,0:T(8,128)S(1)}, f32[128,128]{1,0:T(8,128)S(1)}, u32[]{:S(2)}, u32[]{:S(2)}) collective-permute-start(f32[128,128]{1,0:T(8,128)S(1)} %level0_0.1.own_ref), channel_id=1, source_target_pairs={{0,8},{4,12},{8,0},{12,4},{16,24},{20,28},{24,16},{28,20},{1,9},{5... | collective-permute-start | bytes 196616 | tf_op jit(solution)/shard_map/ppermute | solution.py:18
  12.8 0.3 %own1_0.1.base_ref = f32[128,128]{1,0:T(8,128)S(1)} custom-call(f32[128,128]{1,0:T(8,128)S(1)} %level0_0.1.own_ref, bf16[2,512,256]{2,1,0:T(8,128)(2,1)S(1)} %get-tuple-element.24.f_ref), custom_call_target="tpu_custom_call" | custom-call | tf_op jit(solution)/shard_map/own1_0/pallas_call | solution.py:105
  13.1 0.3 %own1_1.1.base_ref = f32[128,128]{1,0:T(8,128)S(1)} custom-call(f32[128,128]{1,0:T(8,128)S(1)} %level0_1.1.own_ref, bf16[2,512,256]{2,1,0:T(8,128)(2,1)S(1)} %get-tuple-element.24.f_ref), custom_call_target="tpu_custom_call" | custom-call | tf_op jit(solution)/shard_map/own1_1/pallas_call | solution.py:105
  13.4 0.0 collective-permute-done.1.got_ref
  13.4 0.3 %level1_1.1.own_ref = f32[128,128]{1,0:T(8,128)S(1)} custom-call(f32[128,128]{1,0:T(8,128)S(1)} %own1_1.1.base_ref, f32[128,128]{1,0:T(8,128)S(1)} %collective-permute-done.1.got_ref, bf16[2,512,256]{2,1,0:T(8,128)(2,1)S(1)} %get-tuple-element.25.f_ref), custom_call_target="tpu_custom_call" | custom-call | tf_op jit(solution)/shard_map/level1_1/pallas_call | solution.py:105
  13.7 1.9 %collective-permute-start.2 = (f32[128,128]{1,0:T(8,128)S(1)}, f32[128,128]{1,0:T(8,128)S(1)}, u32[]{:S(2)}, u32[]{:S(2)}) collective-permute-start(f32[128,128]{1,0:T(8,128)S(1)} %level1_1.1.own_ref), channel_id=1, source_target_pairs={{0,4},{4,0},{8,12},{12,8},{16,20},{20,16},{24,28},{28,24},{1,5},{5... | collective-permute-start | bytes 196616 | tf_op jit(solution)/shard_map/ppermute | solution.py:18
  15.5 0.3 %collective-permute-done.4.got_ref = f32[128,128]{1,0:T(8,128)S(1)} collective-permute-done((f32[128,128]{1,0:T(8,128)S(1)}, f32[128,128]{1,0:T(8,128)S(1)}, u32[]{:S(2)}, u32[]{:S(2)}) %collective-permute-start.4) | collective-permute-done | bytes 65568 | tf_op jit(solution)/shard_map/ppermute | solution.py:18
  15.8 0.3 %level1_0.1.own_ref = f32[128,128]{1,0:T(8,128)S(1)} custom-call(f32[128,128]{1,0:T(8,128)S(1)} %own1_0.1.base_ref, f32[128,128]{1,0:T(8,128)S(1)} %collective-permute-done.4.got_ref, bf16[2,512,256]{2,1,0:T(8,128)(2,1)S(1)} %get-tuple-element.25.f_ref), custom_call_target="tpu_custom_call" | custom-call | tf_op jit(solution)/shard_map/level1_0/pallas_call | solution.py:105
  16.1 1.6 %collective-permute-start.5 = (f32[128,128]{1,0:T(8,128)S(1)}, f32[128,128]{1,0:T(8,128)S(1)}, u32[]{:S(2)}, u32[]{:S(2)}) collective-permute-start(f32[128,128]{1,0:T(8,128)S(1)} %level1_0.1.own_ref), channel_id=1, source_target_pairs={{0,4},{4,0},{8,12},{12,8},{16,20},{20,16},{24,28},{28,24},{1,5},{5... | collective-permute-start | bytes 196616 | tf_op jit(solution)/shard_map/ppermute | solution.py:18
  17.7 0.3 %own2_0.1.base_ref = f32[128,128]{1,0:T(8,128)S(1)} custom-call(f32[128,128]{1,0:T(8,128)S(1)} %level1_0.1.own_ref, bf16[2,512,256]{2,1,0:T(8,128)(2,1)S(1)} %get-tuple-element.26.f_ref), custom_call_target="tpu_custom_call" | custom-call | tf_op jit(solution)/shard_map/own2_0/pallas_call | solution.py:105
  18.0 0.3 %own2_1.1.base_ref = f32[128,128]{1,0:T(8,128)S(1)} custom-call(f32[128,128]{1,0:T(8,128)S(1)} %level1_1.1.own_ref, bf16[2,512,256]{2,1,0:T(8,128)(2,1)S(1)} %get-tuple-element.26.f_ref), custom_call_target="tpu_custom_call" | custom-call | tf_op jit(solution)/shard_map/own2_1/pallas_call | solution.py:105
  18.2 0.2 collective-permute-done.2.got_ref
  18.4 0.3 %level2_1.1.done_ref = f32[128,128]{1,0:T(8,128)S(1)} custom-call(f32[128,128]{1,0:T(8,128)S(1)} %own2_1.1.base_ref, f32[128,128]{1,0:T(8,128)S(1)} %collective-permute-done.2.got_ref, bf16[2,512,256]{2,1,0:T(8,128)(2,1)S(1)} %get-tuple-element.27.f_ref), custom_call_target="tpu_custom_call" | custom-call | tf_op jit(solution)/shard_map/level2_1/pallas_call | solution.py:105
  18.7 1.7 %collective-permute-done.5.got_ref = f32[128,128]{1,0:T(8,128)S(1)} collective-permute-done((f32[128,128]{1,0:T(8,128)S(1)}, f32[128,128]{1,0:T(8,128)S(1)}, u32[]{:S(2)}, u32[]{:S(2)}) %collective-permute-start.5) | collective-permute-done | bytes 65568 | tf_op jit(solution)/shard_map/ppermute | solution.py:18
  20.4 0.3 %last.1 = (f32[2,16,256]{2,1,0:T(8,128)S(1)}, f32[2,16,256]{2,1,0:T(8,128)S(1)}, f32[2,16,256]{2,1,0:T(8,128)S(1)}, f32[2,16,256]{2,1,0:T(8,128)S(1)}) custom-call(s32[1]{0:T(128)} %bitcast.me_ref, f32[128,128]{1,0:T(8,128)S(1)} %level2_1.1.done_ref, f32[128,128]{1,0:T(8,128)S(1)} %own2_0.1.base_ref, f32[128,128]{1,0:T(8,128)S(1)} %collective-permute-done.5.got_ref, ...), custom_call_target="tpu_custom_call" | custom-call | tf_op jit(solution)/shard_map/last/pallas_call | solution.py:105
  20.7 0.1 collective-permute-start.6
  20.8 1.6 %collective-permute-start.7 = (f32[2,16,256]{2,1,0:T(8,128)S(1)}, f32[2,16,256]{2,1,0:T(8,128)S(1)}, u32[]{:S(2)}, u32[]{:S(2)}) collective-permute-start(f32[2,16,256]{2,1,0:T(8,128)S(1)} %get-tuple-element.31), channel_id=1, source_target_pairs={{0,2},{1,3},{2,0},{3,1},{4,6},{5,7},{6,4},{7,5},{8,10},{9,11},{10,... | collective-permute-start | bytes 98312 | tf_op jit(solution)/shard_map/ppermute | solution.py:18
  22.3 0.3 %collective-permute-start.8 = (f32[2,16,256]{2,1,0:T(8,128)S(1)}, f32[2,16,256]{2,1,0:T(8,128)S(1)}, u32[]{:S(2)}, u32[]{:S(2)}) collective-permute-start(f32[2,16,256]{2,1,0:T(8,128)S(1)} %get-tuple-element.32), channel_id=1, source_target_pairs={{0,1},{1,0},{2,3},{3,2},{4,5},{5,4},{6,7},{7,6},{8,9},{9,8},{10,11... | collective-permute-start | bytes 98312 | tf_op jit(solution)/shard_map/ppermute | solution.py:18
  22.6 1.8 %collective-permute-done.6.refs_1_ = f32[2,16,256]{2,1,0:T(8,128)S(1)} collective-permute-done((f32[2,16,256]{2,1,0:T(8,128)S(1)}, f32[2,16,256]{2,1,0:T(8,128)S(1)}, u32[]{:S(2)}, u32[]{:S(2)}) %collective-permute-start.6) | collective-permute-done | bytes 32800 | tf_op jit(solution)/shard_map/ppermute | solution.py:18
  24.4 0.4 %collective-permute-done.7.refs_2_ = f32[2,16,256]{2,1,0:T(8,128)S(1)} collective-permute-done((f32[2,16,256]{2,1,0:T(8,128)S(1)}, f32[2,16,256]{2,1,0:T(8,128)S(1)}, u32[]{:S(2)}, u32[]{:S(2)}) %collective-permute-start.7) | collective-permute-done | bytes 32800 | tf_op jit(solution)/shard_map/ppermute | solution.py:18
  24.8 0.0 collective-permute-done.8.refs_3_
  24.8 0.6 %total.1 = f32[2,16,256]{2,1,0:T(8,128)} custom-call(f32[2,16,256]{2,1,0:T(8,128)S(1)} %get-tuple-element.29.refs_0_, f32[2,16,256]{2,1,0:T(8,128)S(1)} %collective-permute-done.6.refs_1_, f32[2,16,256]{2,1,0:T(8,128)S(1)} %collective-permute-done.7.refs_2_, f32[2,16,256]{2,1,0:T(8,128)S(1)} %collective-permute-done.8.refs_3_), custom_call_target="tpu_custom_call" | custom-call | tf_op jit(solution)/shard_map/total/pallas_call | solution.py:105
Async XLA Ops:
  0.8 7.7 %collective-permute-start = (f32[128,128]{1,0:T(8,128)S(1)}, f32[128,128]{1,0:T(8,128)S(1)}, u32[]{:S(2)}, u32[]{:S(2)}) collective-permute-start(f32[128,128]{1,0:T(8,128)S(1)} %slice.8.refs_1_), channel_id=1, source_target_pairs={{0,16},{4,20},{8,24},{12,28},{16,0},{20,4},{24,8},{28,12},{1,17},{... | collective-permute-start | bytes 196616 | tf_op jit(solution)/shard_map/ppermute | solution.py:18
  5.7 5.5 %collective-permute-start.3 = (f32[128,128]{1,0:T(8,128)S(1)}, f32[128,128]{1,0:T(8,128)S(1)}, u32[]{:S(2)}, u32[]{:S(2)}) collective-permute-start(f32[128,128]{1,0:T(8,128)S(1)} %slice.7.refs_0_), channel_id=1, source_target_pairs={{0,16},{4,20},{8,24},{12,28},{16,0},{20,4},{24,8},{28,12},{1,17},{... | collective-permute-start | bytes 196616 | tf_op jit(solution)/shard_map/ppermute | solution.py:18
  5.7 1.9 %copy-start = (f32[1,3,16,64,256]{4,3,2,1,0:T(8,128)S(1)}, f32[1,3,16,64,256]{4,3,2,1,0:T(8,128)}, u32[]{:S(2)}) copy-start(f32[1,3,16,64,256]{4,3,2,1,0:T(8,128)} %f_hbm.1) | copy-start | bytes 9437188
  8.8 4.5 %collective-permute-start.1 = (f32[128,128]{1,0:T(8,128)S(1)}, f32[128,128]{1,0:T(8,128)S(1)}, u32[]{:S(2)}, u32[]{:S(2)}) collective-permute-start(f32[128,128]{1,0:T(8,128)S(1)} %level0_1.1.own_ref), channel_id=1, source_target_pairs={{0,8},{4,12},{8,0},{12,4},{16,24},{20,28},{24,16},{28,20},{1,9},{5... | collective-permute-start | bytes 196616 | tf_op jit(solution)/shard_map/ppermute | solution.py:18
  11.5 4.3 %collective-permute-start.4 = (f32[128,128]{1,0:T(8,128)S(1)}, f32[128,128]{1,0:T(8,128)S(1)}, u32[]{:S(2)}, u32[]{:S(2)}) collective-permute-start(f32[128,128]{1,0:T(8,128)S(1)} %level0_0.1.own_ref), channel_id=1, source_target_pairs={{0,8},{4,12},{8,0},{12,4},{16,24},{20,28},{24,16},{28,20},{1,9},{5... | collective-permute-start | bytes 196616 | tf_op jit(solution)/shard_map/ppermute | solution.py:18
  13.7 4.7 %collective-permute-start.2 = (f32[128,128]{1,0:T(8,128)S(1)}, f32[128,128]{1,0:T(8,128)S(1)}, u32[]{:S(2)}, u32[]{:S(2)}) collective-permute-start(f32[128,128]{1,0:T(8,128)S(1)} %level1_1.1.own_ref), channel_id=1, source_target_pairs={{0,4},{4,0},{8,12},{12,8},{16,20},{20,16},{24,28},{28,24},{1,5},{5... | collective-permute-start | bytes 196616 | tf_op jit(solution)/shard_map/ppermute | solution.py:18
  16.1 4.3 %collective-permute-start.5 = (f32[128,128]{1,0:T(8,128)S(1)}, f32[128,128]{1,0:T(8,128)S(1)}, u32[]{:S(2)}, u32[]{:S(2)}) collective-permute-start(f32[128,128]{1,0:T(8,128)S(1)} %level1_0.1.own_ref), channel_id=1, source_target_pairs={{0,4},{4,0},{8,12},{12,8},{16,20},{20,16},{24,28},{28,24},{1,5},{5... | collective-permute-start | bytes 196616 | tf_op jit(solution)/shard_map/ppermute | solution.py:18
  20.7 3.7 %collective-permute-start.6 = (f32[2,16,256]{2,1,0:T(8,128)S(1)}, f32[2,16,256]{2,1,0:T(8,128)S(1)}, u32[]{:S(2)}, u32[]{:S(2)}) collective-permute-start(f32[2,16,256]{2,1,0:T(8,128)S(1)} %get-tuple-element.30), channel_id=1, source_target_pairs={{0,3},{1,2},{2,1},{3,0},{4,7},{5,6},{6,5},{7,4},{8,11},{9,10},{10,... | collective-permute-start | bytes 98312 | tf_op jit(solution)/shard_map/ppermute | solution.py:18
  20.8 4.0 %collective-permute-start.7 = (f32[2,16,256]{2,1,0:T(8,128)S(1)}, f32[2,16,256]{2,1,0:T(8,128)S(1)}, u32[]{:S(2)}, u32[]{:S(2)}) collective-permute-start(f32[2,16,256]{2,1,0:T(8,128)S(1)} %get-tuple-element.31), channel_id=1, source_target_pairs={{0,2},{1,3},{2,0},{3,1},{4,6},{5,7},{6,4},{7,5},{8,10},{9,11},{10,... | collective-permute-start | bytes 98312 | tf_op jit(solution)/shard_map/ppermute | solution.py:18
  22.3 2.5 %collective-permute-start.8 = (f32[2,16,256]{2,1,0:T(8,128)S(1)}, f32[2,16,256]{2,1,0:T(8,128)S(1)}, u32[]{:S(2)}, u32[]{:S(2)}) collective-permute-start(f32[2,16,256]{2,1,0:T(8,128)S(1)} %get-tuple-element.32), channel_id=1, source_target_pairs={{0,1},{1,0},{2,3},{3,2},{4,5},{5,4},{6,7},{7,6},{8,9},{9,8},{10,11... | collective-permute-start | bytes 98312 | tf_op jit(solution)/shard_map/ppermute | solution.py:18

commit v6 on v5

--- a/solution.py
+++ b/solution.py
@@ -79,6 +79,10 @@
     out_ref[...] = base_ref[...] + product(got_ref[...], f_ref[i], width)
 
 
+def both_kernel(own_ref, got_ref, f_ref, g_ref, out_ref, *, i, width):
+    out_ref[...] = product(own_ref[...], f_ref[i], width) + product(got_ref[...], g_ref[i], width)
+
+
 def last_kernel(me_ref, done_ref, base_ref, got_ref, f_ref, *refs, i, width):
     *outs, total_ref = refs
     n = got_ref.shape[1]
@@ -137,6 +141,14 @@
         own, other = halves[2 * level : 2 * level + 2]
         for i in order:
             kw = dict(i=i, width=width)
+            if level == LEVELS - 1 and i == order[0]:
+                states[i] = call(
+                    functools.partial(both_kernel, **kw), shape, states[i], gots[i], own, other,
+                    name=f"level{level}_{i}",
+                )
+                if level < LEVELS - 1:
+                    gots[i] = swapped(states[i], "bis", 2 ** (middle - level))
+                continue
             if level:
                 base = call(
                     functools.partial(own_kernel, **kw), shape, states[i], own, name=f"own{level}_{i}"

time: 25.9 us -> 25.9 us (level)
    pallas_call x13 -> x12, Pallas kernels: 4.31 us -> 4.17 us  [call(): pl.pallas_call(kernel, out_shape=outs, in_specs=specs or [VMEM] * len(arg...]
where the time goes in v6:
time: 25.9 us; the launch traced here: 25.5 us
  starting transfers between devices  12.9 us (50%)
  waiting for transfers between devices  4.69 us (18%)
  Pallas kernels  4.17 us (16%)
  local copies, waits for them, and re-layouts  3.57 us (14%)
    ppermute x9, starting transfers between devices, swapped(): return lax.ppermute(value, axis, pairs)  12.9 us
    ppermute x9, waiting for transfers between devices, swapped(): return lax.ppermute(value, axis, pairs)  4.69 us
    pallas_call x12, Pallas kernels, call(): pl.pallas_call(kernel, out_shape=outs, in_specs=specs or [VMEM] * len(arg...  4.17 us
    unnamed x2, local copies, waits for them, and re-layouts  1.88 us
    slice x1, local copies, waits for them, and re-layouts, per_device(): states = [rest[:, :step], one]  0.84 us
    slice x1, local copies, waits for them, and re-layouts, per_device(): one = raw[:, step:]  0.84 us
  transfers between devices with their start and end apart: 9, of which 6 were waited for; matrix products, arithmetic and copies ran while one was open for 3% of the time, Pallas kernels for 13%

profile of v6, /device:TPU:0, one launch (start us, length us, event | category | flops | bytes accessed | tf_op | source)
XLA Modules:
  0.0 25.5 jit_solution(3058456910672562117)
XLA Ops:
  0.0 0.8 %slice.8.refs_1_ = f32[128,128]{1,0:T(8,128)S(1)} slice(f32[128,256]{1,0:T(8,128)} %bitcast.2), slice={[0:128], [128:256]} | slice | bytes 131072 | tf_op jit(solution)/shard_map/slice | solution.py:128
  0.8 4.0 %collective-permute-start = (f32[128,128]{1,0:T(8,128)S(1)}, f32[128,128]{1,0:T(8,128)S(1)}, u32[]{:S(2)}, u32[]{:S(2)}) collective-permute-start(f32[128,128]{1,0:T(8,128)S(1)} %slice.8.refs_1_), channel_id=1, source_target_pairs={{0,16},{4,20},{8,24},{12,28},{16,0},{20,4},{24,8},{28,12},{1,17},{... | collective-permute-start | bytes 196616 | tf_op jit(solution)/shard_map/ppermute | solution.py:18
  4.9 0.8 %slice.7.refs_0_ = f32[128,128]{1,0:T(8,128)S(1)} slice(f32[128,256]{1,0:T(8,128)} %bitcast.3), slice={[0:128], [0:128]} | slice | bytes 131072 | tf_op jit(solution)/shard_map/slice | solution.py:130
  5.7 0.0 collective-permute-start.3
  5.7 0.0 copy-start
  5.7 1.9 %copy-done = f32[1,3,16,64,256]{4,3,2,1,0:T(8,128)S(1)} copy-done((f32[1,3,16,64,256]{4,3,2,1,0:T(8,128)S(1)}, f32[1,3,16,64,256]{4,3,2,1,0:T(8,128)}, u32[]{:S(2)}) %copy-start) | copy-done | bytes 3145752
  7.6 0.5 %prepare.1 = (bf16[2,512,256]{2,1,0:T(8,128)(2,1)S(1)}, bf16[2,512,256]{2,1,0:T(8,128)(2,1)S(1)}, bf16[2,512,256]{2,1,0:T(8,128)(2,1)S(1)}, bf16[2,512,256]{2,1,...) custom-call(f32[1,3,16,64,256]{4,3,2,1,0:T(8,128)S(1)} %copy-done), custom_call_target="tpu_custom_call" | custom-call | tf_op jit(solution)/shard_map/prepare/pallas_call | solution.py:109
  8.1 0.4 %own0.1 = (f32[128,128]{1,0:T(8,128)S(1)}, f32[128,128]{1,0:T(8,128)S(1)}) custom-call(f32[128,128]{1,0:T(8,128)S(1)} %slice.7.refs_0_, f32[128,128]{1,0:T(8,128)S(1)} %slice.8.refs_1_, bf16[2,512,256]{2,1,0:T(8,128)(2,1)S(1)} %get-tuple-element.21.refs_2_), custom_call_target="tpu_custom_call" | custom-call | tf_op jit(solution)/shard_map/own0/pallas_call | solution.py:109
  8.6 0.0 collective-permute-done.got_ref
  8.6 0.3 %level0_1.1.own_ref = f32[128,128]{1,0:T(8,128)S(1)} custom-call(f32[128,128]{1,0:T(8,128)S(1)} %get-tuple-element.22.base_ref, f32[128,128]{1,0:T(8,128)S(1)} %collective-permute-done.got_ref, bf16[2,512,256]{2,1,0:T(8,128)(2,1)S(1)} %get-tuple-element.23.f_ref), custom_call_target="tpu_custom_call" | custom-call | tf_op jit(solution)/shard_map/level0_1/pallas_call | solution.py:109
  8.8 2.1 %collective-permute-start.1 = (f32[128,128]{1,0:T(8,128)S(1)}, f32[128,128]{1,0:T(8,128)S(1)}, u32[]{:S(2)}, u32[]{:S(2)}) collective-permute-start(f32[128,128]{1,0:T(8,128)S(1)} %level0_1.1.own_ref), channel_id=1, source_target_pairs={{0,8},{4,12},{8,0},{12,4},{16,24},{20,28},{24,16},{28,20},{1,9},{5... | collective-permute-start | bytes 196616 | tf_op jit(solution)/shard_map/ppermute | solution.py:18
  11.0 0.2 collective-permute-done.3.got_ref
  11.2 0.3 %level0_0.1.own_ref = f32[128,128]{1,0:T(8,128)S(1)} custom-call(f32[128,128]{1,0:T(8,128)S(1)} %get-tuple-element.28.base_ref, f32[128,128]{1,0:T(8,128)S(1)} %collective-permute-done.3.got_ref, bf16[2,512,256]{2,1,0:T(8,128)(2,1)S(1)} %get-tuple-element.23.f_ref), custom_call_target="tpu_custom_call" | custom-call | tf_op jit(solution)/shard_map/level0_0/pallas_call | solution.py:109
  11.5 1.3 %collective-permute-start.4 = (f32[128,128]{1,0:T(8,128)S(1)}, f32[128,128]{1,0:T(8,128)S(1)}, u32[]{:S(2)}, u32[]{:S(2)}) collective-permute-start(f32[128,128]{1,0:T(8,128)S(1)} %level0_0.1.own_ref), channel_id=1, source_target_pairs={{0,8},{4,12},{8,0},{12,4},{16,24},{20,28},{24,16},{28,20},{1,9},{5... | collective-permute-start | bytes 196616 | tf_op jit(solution)/shard_map/ppermute | solution.py:18
  12.8 0.3 %own1_0.1.base_ref = f32[128,128]{1,0:T(8,128)S(1)} custom-call(f32[128,128]{1,0:T(8,128)S(1)} %level0_0.1.own_ref, bf16[2,512,256]{2,1,0:T(8,128)(2,1)S(1)} %get-tuple-element.24.f_ref), custom_call_target="tpu_custom_call" | custom-call | tf_op jit(solution)/shard_map/own1_0/pallas_call | solution.py:109
  13.1 0.3 %own1_1.1.base_ref = f32[128,128]{1,0:T(8,128)S(1)} custom-call(f32[128,128]{1,0:T(8,128)S(1)} %level0_1.1.own_ref, bf16[2,512,256]{2,1,0:T(8,128)(2,1)S(1)} %get-tuple-element.24.f_ref), custom_call_target="tpu_custom_call" | custom-call | tf_op jit(solution)/shard_map/own1_1/pallas_call | solution.py:109
  13.4 0.0 collective-permute-done.1.got_ref
  13.4 0.3 %level1_1.1.own_ref = f32[128,128]{1,0:T(8,128)S(1)} custom-call(f32[128,128]{1,0:T(8,128)S(1)} %own1_1.1.base_ref, f32[128,128]{1,0:T(8,128)S(1)} %collective-permute-done.1.got_ref, bf16[2,512,256]{2,1,0:T(8,128)(2,1)S(1)} %get-tuple-element.25.f_ref), custom_call_target="tpu_custom_call" | custom-call | tf_op jit(solution)/shard_map/level1_1/pallas_call | solution.py:109
  13.7 1.9 %collective-permute-start.2 = (f32[128,128]{1,0:T(8,128)S(1)}, f32[128,128]{1,0:T(8,128)S(1)}, u32[]{:S(2)}, u32[]{:S(2)}) collective-permute-start(f32[128,128]{1,0:T(8,128)S(1)} %level1_1.1.own_ref), channel_id=1, source_target_pairs={{0,4},{4,0},{8,12},{12,8},{16,20},{20,16},{24,28},{28,24},{1,5},{5... | collective-permute-start | bytes 196616 | tf_op jit(solution)/shard_map/ppermute | solution.py:18
  15.5 0.3 %collective-permute-done.4.got_ref = f32[128,128]{1,0:T(8,128)S(1)} collective-permute-done((f32[128,128]{1,0:T(8,128)S(1)}, f32[128,128]{1,0:T(8,128)S(1)}, u32[]{:S(2)}, u32[]{:S(2)}) %collective-permute-start.4) | collective-permute-done | bytes 65568 | tf_op jit(solution)/shard_map/ppermute | solution.py:18
  15.8 0.3 %level1_0.1.own_ref = f32[128,128]{1,0:T(8,128)S(1)} custom-call(f32[128,128]{1,0:T(8,128)S(1)} %own1_0.1.base_ref, f32[128,128]{1,0:T(8,128)S(1)} %collective-permute-done.4.got_ref, bf16[2,512,256]{2,1,0:T(8,128)(2,1)S(1)} %get-tuple-element.25.f_ref), custom_call_target="tpu_custom_call" | custom-call | tf_op jit(solution)/shard_map/level1_0/pallas_call | solution.py:109
  16.1 1.6 %collective-permute-start.5 = (f32[128,128]{1,0:T(8,128)S(1)}, f32[128,128]{1,0:T(8,128)S(1)}, u32[]{:S(2)}, u32[]{:S(2)}) collective-permute-start(f32[128,128]{1,0:T(8,128)S(1)} %level1_0.1.own_ref), channel_id=1, source_target_pairs={{0,4},{4,0},{8,12},{12,8},{16,20},{20,16},{24,28},{28,24},{1,5},{5... | collective-permute-start | bytes 196616 | tf_op jit(solution)/shard_map/ppermute | solution.py:18
  17.7 0.3 %own2_0.1.base_ref = f32[128,128]{1,0:T(8,128)S(1)} custom-call(f32[128,128]{1,0:T(8,128)S(1)} %level1_0.1.own_ref, bf16[2,512,256]{2,1,0:T(8,128)(2,1)S(1)} %get-tuple-element.26.f_ref), custom_call_target="tpu_custom_call" | custom-call | tf_op jit(solution)/shard_map/own2_0/pallas_call | solution.py:109
  18.0 0.5 %collective-permute-done.2.got_ref = f32[128,128]{1,0:T(8,128)S(1)} collective-permute-done((f32[128,128]{1,0:T(8,128)S(1)}, f32[128,128]{1,0:T(8,128)S(1)}, u32[]{:S(2)}, u32[]{:S(2)}) %collective-permute-start.2) | collective-permute-done | bytes 65568 | tf_op jit(solution)/shard_map/ppermute | solution.py:18
  18.4 0.4 %level2_1.1.done_ref = f32[128,128]{1,0:T(8,128)S(1)} custom-call(f32[128,128]{1,0:T(8,128)S(1)} %level1_1.1.own_ref, f32[128,128]{1,0:T(8,128)S(1)} %collective-permute-done.2.got_ref, bf16[2,512,256]{2,1,0:T(8,128)(2,1)S(1)} %get-tuple-element.26.f_ref, bf16[2,512,256]{2,1,0:T(8,128)(2,1)S(1)} %get-tuple-element.27.g_ref.f_ref), custom_call_target="tpu_custom_call" | custom-call | tf_op jit(solution)/shard_map/level2_1/pallas_call | solution.py:109
  18.8 1.6 %collective-permute-done.5.got_ref = f32[128,128]{1,0:T(8,128)S(1)} collective-permute-done((f32[128,128]{1,0:T(8,128)S(1)}, f32[128,128]{1,0:T(8,128)S(1)}, u32[]{:S(2)}, u32[]{:S(2)}) %collective-permute-start.5) | collective-permute-done | bytes 65568 | tf_op jit(solution)/shard_map/ppermute | solution.py:18
  20.4 0.3 %last.1 = (f32[2,16,256]{2,1,0:T(8,128)S(1)}, f32[2,16,256]{2,1,0:T(8,128)S(1)}, f32[2,16,256]{2,1,0:T(8,128)S(1)}, f32[2,16,256]{2,1,0:T(8,128)S(1)}) custom-call(s32[1]{0:T(128)} %bitcast.me_ref, f32[128,128]{1,0:T(8,128)S(1)} %level2_1.1.done_ref, f32[128,128]{1,0:T(8,128)S(1)} %own2_0.1.base_ref, f32[128,128]{1,0:T(8,128)S(1)} %collective-permute-done.5.got_ref, ...), custom_call_target="tpu_custom_call" | custom-call | tf_op jit(solution)/shard_map/last/pallas_call | solution.py:109
  20.7 0.1 collective-permute-start.6
  20.8 1.6 %collective-permute-start.7 = (f32[2,16,256]{2,1,0:T(8,128)S(1)}, f32[2,16,256]{2,1,0:T(8,128)S(1)}, u32[]{:S(2)}, u32[]{:S(2)}) collective-permute-start(f32[2,16,256]{2,1,0:T(8,128)S(1)} %get-tuple-element.31), channel_id=1, source_target_pairs={{0,2},{1,3},{2,0},{3,1},{4,6},{5,7},{6,4},{7,5},{8,10},{9,11},{10,... | collective-permute-start | bytes 98312 | tf_op jit(solution)/shard_map/ppermute | solution.py:18
  22.3 0.3 %collective-permute-start.8 = (f32[2,16,256]{2,1,0:T(8,128)S(1)}, f32[2,16,256]{2,1,0:T(8,128)S(1)}, u32[]{:S(2)}, u32[]{:S(2)}) collective-permute-start(f32[2,16,256]{2,1,0:T(8,128)S(1)} %get-tuple-element.32), channel_id=1, source_target_pairs={{0,1},{1,0},{2,3},{3,2},{4,5},{5,4},{6,7},{7,6},{8,9},{9,8},{10,11... | collective-permute-start | bytes 98312 | tf_op jit(solution)/shard_map/ppermute | solution.py:18
  22.6 1.8 %collective-permute-done.6.refs_1_ = f32[2,16,256]{2,1,0:T(8,128)S(1)} collective-permute-done((f32[2,16,256]{2,1,0:T(8,128)S(1)}, f32[2,16,256]{2,1,0:T(8,128)S(1)}, u32[]{:S(2)}, u32[]{:S(2)}) %collective-permute-start.6) | collective-permute-done | bytes 32800 | tf_op jit(solution)/shard_map/ppermute | solution.py:18
  24.4 0.4 %collective-permute-done.7.refs_2_ = f32[2,16,256]{2,1,0:T(8,128)S(1)} collective-permute-done((f32[2,16,256]{2,1,0:T(8,128)S(1)}, f32[2,16,256]{2,1,0:T(8,128)S(1)}, u32[]{:S(2)}, u32[]{:S(2)}) %collective-permute-start.7) | collective-permute-done | bytes 32800 | tf_op jit(solution)/shard_map/ppermute | solution.py:18
  24.8 0.0 collective-permute-done.8.refs_3_
  24.8 0.6 %total.1 = f32[2,16,256]{2,1,0:T(8,128)} custom-call(f32[2,16,256]{2,1,0:T(8,128)S(1)} %get-tuple-element.29.refs_0_, f32[2,16,256]{2,1,0:T(8,128)S(1)} %collective-permute-done.6.refs_1_, f32[2,16,256]{2,1,0:T(8,128)S(1)} %collective-permute-done.7.refs_2_, f32[2,16,256]{2,1,0:T(8,128)S(1)} %collective-permute-done.8.refs_3_), custom_call_target="tpu_custom_call" | custom-call | tf_op jit(solution)/shard_map/total/pallas_call | solution.py:109
Async XLA Ops:
  0.8 7.7 %collective-permute-start = (f32[128,128]{1,0:T(8,128)S(1)}, f32[128,128]{1,0:T(8,128)S(1)}, u32[]{:S(2)}, u32[]{:S(2)}) collective-permute-start(f32[128,128]{1,0:T(8,128)S(1)} %slice.8.refs_1_), channel_id=1, source_target_pairs={{0,16},{4,20},{8,24},{12,28},{16,0},{20,4},{24,8},{28,12},{1,17},{... | collective-permute-start | bytes 196616 | tf_op jit(solution)/shard_map/ppermute | solution.py:18
  5.7 5.5 %collective-permute-start.3 = (f32[128,128]{1,0:T(8,128)S(1)}, f32[128,128]{1,0:T(8,128)S(1)}, u32[]{:S(2)}, u32[]{:S(2)}) collective-permute-start(f32[128,128]{1,0:T(8,128)S(1)} %slice.7.refs_0_), channel_id=1, source_target_pairs={{0,16},{4,20},{8,24},{12,28},{16,0},{20,4},{24,8},{28,12},{1,17},{... | collective-permute-start | bytes 196616 | tf_op jit(solution)/shard_map/ppermute | solution.py:18
  5.7 1.9 %copy-start = (f32[1,3,16,64,256]{4,3,2,1,0:T(8,128)S(1)}, f32[1,3,16,64,256]{4,3,2,1,0:T(8,128)}, u32[]{:S(2)}) copy-start(f32[1,3,16,64,256]{4,3,2,1,0:T(8,128)} %f_hbm.1) | copy-start | bytes 9437188
  8.8 4.5 %collective-permute-start.1 = (f32[128,128]{1,0:T(8,128)S(1)}, f32[128,128]{1,0:T(8,128)S(1)}, u32[]{:S(2)}, u32[]{:S(2)}) collective-permute-start(f32[128,128]{1,0:T(8,128)S(1)} %level0_1.1.own_ref), channel_id=1, source_target_pairs={{0,8},{4,12},{8,0},{12,4},{16,24},{20,28},{24,16},{28,20},{1,9},{5... | collective-permute-start | bytes 196616 | tf_op jit(solution)/shard_map/ppermute | solution.py:18
  11.5 4.3 %collective-permute-start.4 = (f32[128,128]{1,0:T(8,128)S(1)}, f32[128,128]{1,0:T(8,128)S(1)}, u32[]{:S(2)}, u32[]{:S(2)}) collective-permute-start(f32[128,128]{1,0:T(8,128)S(1)} %level0_0.1.own_ref), channel_id=1, source_target_pairs={{0,8},{4,12},{8,0},{12,4},{16,24},{20,28},{24,16},{28,20},{1,9},{5... | collective-permute-start | bytes 196616 | tf_op jit(solution)/shard_map/ppermute | solution.py:18
  13.7 4.7 %collective-permute-start.2 = (f32[128,128]{1,0:T(8,128)S(1)}, f32[128,128]{1,0:T(8,128)S(1)}, u32[]{:S(2)}, u32[]{:S(2)}) collective-permute-start(f32[128,128]{1,0:T(8,128)S(1)} %level1_1.1.own_ref), channel_id=1, source_target_pairs={{0,4},{4,0},{8,12},{12,8},{16,20},{20,16},{24,28},{28,24},{1,5},{5... | collective-permute-start | bytes 196616 | tf_op jit(solution)/shard_map/ppermute | solution.py:18
  16.1 4.3 %collective-permute-start.5 = (f32[128,128]{1,0:T(8,128)S(1)}, f32[128,128]{1,0:T(8,128)S(1)}, u32[]{:S(2)}, u32[]{:S(2)}) collective-permute-start(f32[128,128]{1,0:T(8,128)S(1)} %level1_0.1.own_ref), channel_id=1, source_target_pairs={{0,4},{4,0},{8,12},{12,8},{16,20},{20,16},{24,28},{28,24},{1,5},{5... | collective-permute-start | bytes 196616 | tf_op jit(solution)/shard_map/ppermute | solution.py:18
  20.7 3.7 %collective-permute-start.6 = (f32[2,16,256]{2,1,0:T(8,128)S(1)}, f32[2,16,256]{2,1,0:T(8,128)S(1)}, u32[]{:S(2)}, u32[]{:S(2)}) collective-permute-start(f32[2,16,256]{2,1,0:T(8,128)S(1)} %get-tuple-element.30), channel_id=1, source_target_pairs={{0,3},{1,2},{2,1},{3,0},{4,7},{5,6},{6,5},{7,4},{8,11},{9,10},{10,... | collective-permute-start | bytes 98312 | tf_op jit(solution)/shard_map/ppermute | solution.py:18
  20.8 4.0 %collective-permute-start.7 = (f32[2,16,256]{2,1,0:T(8,128)S(1)}, f32[2,16,256]{2,1,0:T(8,128)S(1)}, u32[]{:S(2)}, u32[]{:S(2)}) collective-permute-start(f32[2,16,256]{2,1,0:T(8,128)S(1)} %get-tuple-element.31), channel_id=1, source_target_pairs={{0,2},{1,3},{2,0},{3,1},{4,6},{5,7},{6,4},{7,5},{8,10},{9,11},{10,... | collective-permute-start | bytes 98312 | tf_op jit(solution)/shard_map/ppermute | solution.py:18
  22.3 2.5 %collective-permute-start.8 = (f32[2,16,256]{2,1,0:T(8,128)S(1)}, f32[2,16,256]{2,1,0:T(8,128)S(1)}, u32[]{:S(2)}, u32[]{:S(2)}) collective-permute-start(f32[2,16,256]{2,1,0:T(8,128)S(1)} %get-tuple-element.32), channel_id=1, source_target_pairs={{0,1},{1,0},{2,3},{3,2},{4,5},{5,4},{6,7},{7,6},{8,9},{9,8},{10,11... | collective-permute-start | bytes 98312 | tf_op jit(solution)/shard_map/ppermute | solution.py:18

commit v7 on v5

--- a/solution.py
+++ b/solution.py
@@ -93,14 +93,6 @@
             out[q] = total_ref[pl.ds(q * rank + start, share), :]
 
 
-def sum_kernel(*refs):
-    *parts, out_ref = refs
-    total = parts[0][...]
-    for r in parts[1:]:
-        total = total + r[...]
-    out_ref[...] = total
-
-
 def call(kernel, outs, *args, specs=None, scratch=(), name=None):
     return pl.pallas_call(
         kernel,
@@ -162,7 +154,10 @@
             if level < LEVELS - 1:
                 gots[i] = swapped(states[i], "bis", 2 ** (middle - level))
     parts = [pieces[0]] + [swapped(pieces[m], "src", m) for m in reversed(range(1, groups))]
-    return call(sum_kernel, piece, *parts, name="total")
+    total = parts[0]
+    for p in parts[1:]:
+        total = total + p
+    return total
 
 
 def solution(mesh):

time: 25.9 us -> 25.9 us (level)
  other arithmetic: 0 us -> 0.63 us
  Pallas kernels: 4.31 us -> 3.69 us
    add x0 -> x1, other arithmetic: none -> 0.63 us  [per_device(): total = total + p]
    pallas_call x13 -> x12, Pallas kernels: 4.31 us -> 3.69 us  [call(): pl.pallas_call(kernel, out_shape=outs, in_specs=specs or [VMEM] * len(arg...]
where the time goes in v7:
time: 25.9 us; the launch traced here: 25.5 us
  starting transfers between devices  12.9 us (50%)
  waiting for transfers between devices  4.54 us (18%)
  Pallas kernels  3.69 us (14%)
  local copies, waits for them, and re-layouts  3.57 us (14%)
  other arithmetic  0.63 us (2%)
    ppermute x9, starting transfers between devices, swapped(): return lax.ppermute(value, axis, pairs)  12.9 us
    ppermute x9, waiting for transfers between devices, swapped(): return lax.ppermute(value, axis, pairs)  4.54 us
    pallas_call x12, Pallas kernels, call(): pl.pallas_call(kernel, out_shape=outs, in_specs=specs or [VMEM] * len(arg...  3.69 us
    unnamed x2, local copies, waits for them, and re-layouts  1.88 us
    slice x1, local copies, waits for them, and re-layouts, per_device(): states = [rest[:, :step], one]  0.84 us
    slice x1, local copies, waits for them, and re-layouts, per_device(): one = raw[:, step:]  0.84 us
    add x1, other arithmetic, per_device(): total = total + p  0.63 us
  transfers between devices with their start and end apart: 9, of which 6 were waited for; matrix products, arithmetic and copies ran while one was open for 3% of the time, Pallas kernels for 13%

profile of v7, /device:TPU:0, one launch (start us, length us, event | category | flops | bytes accessed | tf_op | source)
XLA Modules:
  0.0 25.5 jit_solution(17453269985270514162)
XLA Ops:
  0.0 0.8 %slice.8.refs_1_ = f32[128,128]{1,0:T(8,128)S(1)} slice(f32[128,256]{1,0:T(8,128)} %bitcast.2), slice={[0:128], [128:256]} | slice | bytes 131072 | tf_op jit(solution)/shard_map/slice | solution.py:116
  0.8 4.0 %collective-permute-start = (f32[128,128]{1,0:T(8,128)S(1)}, f32[128,128]{1,0:T(8,128)S(1)}, u32[]{:S(2)}, u32[]{:S(2)}) collective-permute-start(f32[128,128]{1,0:T(8,128)S(1)} %slice.8.refs_1_), channel_id=1, source_target_pairs={{0,16},{4,20},{8,24},{12,28},{16,0},{20,4},{24,8},{28,12},{1,17},{... | collective-permute-start | bytes 196616 | tf_op jit(solution)/shard_map/ppermute | solution.py:18
  4.9 0.8 %slice.7.refs_0_ = f32[128,128]{1,0:T(8,128)S(1)} slice(f32[128,256]{1,0:T(8,128)} %bitcast.3), slice={[0:128], [0:128]} | slice | bytes 131072 | tf_op jit(solution)/shard_map/slice | solution.py:118
  5.7 0.0 collective-permute-start.3
  5.7 0.0 copy-start
  5.7 1.9 %copy-done = f32[1,3,16,64,256]{4,3,2,1,0:T(8,128)S(1)} copy-done((f32[1,3,16,64,256]{4,3,2,1,0:T(8,128)S(1)}, f32[1,3,16,64,256]{4,3,2,1,0:T(8,128)}, u32[]{:S(2)}) %copy-start) | copy-done | bytes 3145752
  7.6 0.5 %prepare.1 = (bf16[2,512,256]{2,1,0:T(8,128)(2,1)S(1)}, bf16[2,512,256]{2,1,0:T(8,128)(2,1)S(1)}, bf16[2,512,256]{2,1,0:T(8,128)(2,1)S(1)}, bf16[2,512,256]{2,1,...) custom-call(f32[1,3,16,64,256]{4,3,2,1,0:T(8,128)S(1)} %copy-done), custom_call_target="tpu_custom_call" | custom-call | tf_op jit(solution)/shard_map/prepare/pallas_call | solution.py:97
  8.1 0.4 %own0.1 = (f32[128,128]{1,0:T(8,128)S(1)}, f32[128,128]{1,0:T(8,128)S(1)}) custom-call(f32[128,128]{1,0:T(8,128)S(1)} %slice.7.refs_0_, f32[128,128]{1,0:T(8,128)S(1)} %slice.8.refs_1_, bf16[2,512,256]{2,1,0:T(8,128)(2,1)S(1)} %get-tuple-element.21.refs_2_), custom_call_target="tpu_custom_call" | custom-call | tf_op jit(solution)/shard_map/own0/pallas_call | solution.py:97
  8.6 0.0 collective-permute-done.got_ref
  8.6 0.3 %level0_1.1.own_ref = f32[128,128]{1,0:T(8,128)S(1)} custom-call(f32[128,128]{1,0:T(8,128)S(1)} %get-tuple-element.22.base_ref, f32[128,128]{1,0:T(8,128)S(1)} %collective-permute-done.got_ref, bf16[2,512,256]{2,1,0:T(8,128)(2,1)S(1)} %get-tuple-element.23.f_ref), custom_call_target="tpu_custom_call" | custom-call | tf_op jit(solution)/shard_map/level0_1/pallas_call | solution.py:97
  8.8 2.1 %collective-permute-start.1 = (f32[128,128]{1,0:T(8,128)S(1)}, f32[128,128]{1,0:T(8,128)S(1)}, u32[]{:S(2)}, u32[]{:S(2)}) collective-permute-start(f32[128,128]{1,0:T(8,128)S(1)} %level0_1.1.own_ref), channel_id=1, source_target_pairs={{0,8},{4,12},{8,0},{12,4},{16,24},{20,28},{24,16},{28,20},{1,9},{5... | collective-permute-start | bytes 196616 | tf_op jit(solution)/shard_map/ppermute | solution.py:18
  11.0 0.2 collective-permute-done.3.got_ref
  11.2 0.3 %level0_0.1.own_ref = f32[128,128]{1,0:T(8,128)S(1)} custom-call(f32[128,128]{1,0:T(8,128)S(1)} %get-tuple-element.28.base_ref, f32[128,128]{1,0:T(8,128)S(1)} %collective-permute-done.3.got_ref, bf16[2,512,256]{2,1,0:T(8,128)(2,1)S(1)} %get-tuple-element.23.f_ref), custom_call_target="tpu_custom_call" | custom-call | tf_op jit(solution)/shard_map/level0_0/pallas_call | solution.py:97
  11.5 1.3 %collective-permute-start.4 = (f32[128,128]{1,0:T(8,128)S(1)}, f32[128,128]{1,0:T(8,128)S(1)}, u32[]{:S(2)}, u32[]{:S(2)}) collective-permute-start(f32[128,128]{1,0:T(8,128)S(1)} %level0_0.1.own_ref), channel_id=1, source_target_pairs={{0,8},{4,12},{8,0},{12,4},{16,24},{20,28},{24,16},{28,20},{1,9},{5... | collective-permute-start | bytes 196616 | tf_op jit(solution)/shard_map/ppermute | solution.py:18
  12.8 0.3 %own1_0.1.base_ref = f32[128,128]{1,0:T(8,128)S(1)} custom-call(f32[128,128]{1,0:T(8,128)S(1)} %level0_0.1.own_ref, bf16[2,512,256]{2,1,0:T(8,128)(2,1)S(1)} %get-tuple-element.24.f_ref), custom_call_target="tpu_custom_call" | custom-call | tf_op jit(solution)/shard_map/own1_0/pallas_call | solution.py:97
  13.1 0.3 %own1_1.1.base_ref = f32[128,128]{1,0:T(8,128)S(1)} custom-call(f32[128,128]{1,0:T(8,128)S(1)} %level0_1.1.own_ref, bf16[2,512,256]{2,1,0:T(8,128)(2,1)S(1)} %get-tuple-element.24.f_ref), custom_call_target="tpu_custom_call" | custom-call | tf_op jit(solution)/shard_map/own1_1/pallas_call | solution.py:97
  13.4 0.0 collective-permute-done.1.got_ref
  13.4 0.3 %level1_1.1.own_ref = f32[128,128]{1,0:T(8,128)S(1)} custom-call(f32[128,128]{1,0:T(8,128)S(1)} %own1_1.1.base_ref, f32[128,128]{1,0:T(8,128)S(1)} %collective-permute-done.1.got_ref, bf16[2,512,256]{2,1,0:T(8,128)(2,1)S(1)} %get-tuple-element.25.f_ref), custom_call_target="tpu_custom_call" | custom-call | tf_op jit(solution)/shard_map/level1_1/pallas_call | solution.py:97
  13.7 1.9 %collective-permute-start.2 = (f32[128,128]{1,0:T(8,128)S(1)}, f32[128,128]{1,0:T(8,128)S(1)}, u32[]{:S(2)}, u32[]{:S(2)}) collective-permute-start(f32[128,128]{1,0:T(8,128)S(1)} %level1_1.1.own_ref), channel_id=1, source_target_pairs={{0,4},{4,0},{8,12},{12,8},{16,20},{20,16},{24,28},{28,24},{1,5},{5... | collective-permute-start | bytes 196616 | tf_op jit(solution)/shard_map/ppermute | solution.py:18
  15.5 0.3 %collective-permute-done.4.got_ref = f32[128,128]{1,0:T(8,128)S(1)} collective-permute-done((f32[128,128]{1,0:T(8,128)S(1)}, f32[128,128]{1,0:T(8,128)S(1)}, u32[]{:S(2)}, u32[]{:S(2)}) %collective-permute-start.4) | collective-permute-done | bytes 65568 | tf_op jit(solution)/shard_map/ppermute | solution.py:18
  15.8 0.3 %level1_0.1.own_ref = f32[128,128]{1,0:T(8,128)S(1)} custom-call(f32[128,128]{1,0:T(8,128)S(1)} %own1_0.1.base_ref, f32[128,128]{1,0:T(8,128)S(1)} %collective-permute-done.4.got_ref, bf16[2,512,256]{2,1,0:T(8,128)(2,1)S(1)} %get-tuple-element.25.f_ref), custom_call_target="tpu_custom_call" | custom-call | tf_op jit(solution)/shard_map/level1_0/pallas_call | solution.py:97
  16.1 1.6 %collective-permute-start.5 = (f32[128,128]{1,0:T(8,128)S(1)}, f32[128,128]{1,0:T(8,128)S(1)}, u32[]{:S(2)}, u32[]{:S(2)}) collective-permute-start(f32[128,128]{1,0:T(8,128)S(1)} %level1_0.1.own_ref), channel_id=1, source_target_pairs={{0,4},{4,0},{8,12},{12,8},{16,20},{20,16},{24,28},{28,24},{1,5},{5... | collective-permute-start | bytes 196616 | tf_op jit(solution)/shard_map/ppermute | solution.py:18
  17.7 0.3 %own2_0.1.base_ref = f32[128,128]{1,0:T(8,128)S(1)} custom-call(f32[128,128]{1,0:T(8,128)S(1)} %level1_0.1.own_ref, bf16[2,512,256]{2,1,0:T(8,128)(2,1)S(1)} %get-tuple-element.26.f_ref), custom_call_target="tpu_custom_call" | custom-call | tf_op jit(solution)/shard_map/own2_0/pallas_call | solution.py:97
  18.0 0.3 %own2_1.1.base_ref = f32[128,128]{1,0:T(8,128)S(1)} custom-call(f32[128,128]{1,0:T(8,128)S(1)} %level1_1.1.own_ref, bf16[2,512,256]{2,1,0:T(8,128)(2,1)S(1)} %get-tuple-element.26.f_ref), custom_call_target="tpu_custom_call" | custom-call | tf_op jit(solution)/shard_map/own2_1/pallas_call | solution.py:97
  18.2 0.2 collective-permute-done.2.got_ref
  18.4 0.3 %level2_1.1.done_ref = f32[128,128]{1,0:T(8,128)S(1)} custom-call(f32[128,128]{1,0:T(8,128)S(1)} %own2_1.1.base_ref, f32[128,128]{1,0:T(8,128)S(1)} %collective-permute-done.2.got_ref, bf16[2,512,256]{2,1,0:T(8,128)(2,1)S(1)} %get-tuple-element.27.f_ref), custom_call_target="tpu_custom_call" | custom-call | tf_op jit(solution)/shard_map/level2_1/pallas_call | solution.py:97
  18.7 1.7 %collective-permute-done.5.got_ref = f32[128,128]{1,0:T(8,128)S(1)} collective-permute-done((f32[128,128]{1,0:T(8,128)S(1)}, f32[128,128]{1,0:T(8,128)S(1)}, u32[]{:S(2)}, u32[]{:S(2)}) %collective-permute-start.5) | collective-permute-done | bytes 65568 | tf_op jit(solution)/shard_map/ppermute | solution.py:18
  20.4 0.3 %last.1 = (f32[2,16,256]{2,1,0:T(8,128)S(1)}, f32[2,16,256]{2,1,0:T(8,128)S(1)}, f32[2,16,256]{2,1,0:T(8,128)S(1)}, f32[2,16,256]{2,1,0:T(8,128)S(1)}) custom-call(s32[1]{0:T(128)} %bitcast.me_ref, f32[128,128]{1,0:T(8,128)S(1)} %level2_1.1.done_ref, f32[128,128]{1,0:T(8,128)S(1)} %own2_0.1.base_ref, f32[128,128]{1,0:T(8,128)S(1)} %collective-permute-done.5.got_ref, ...), custom_call_target="tpu_custom_call" | custom-call | tf_op jit(solution)/shard_map/last/pallas_call | solution.py:97
  20.7 0.1 collective-permute-start.6
  20.8 1.6 %collective-permute-start.7 = (f32[2,16,256]{2,1,0:T(8,128)S(1)}, f32[2,16,256]{2,1,0:T(8,128)S(1)}, u32[]{:S(2)}, u32[]{:S(2)}) collective-permute-start(f32[2,16,256]{2,1,0:T(8,128)S(1)} %get-tuple-element.31), channel_id=1, source_target_pairs={{0,2},{1,3},{2,0},{3,1},{4,6},{5,7},{6,4},{7,5},{8,10},{9,11},{10,... | collective-permute-start | bytes 98312 | tf_op jit(solution)/shard_map/ppermute | solution.py:18
  22.3 0.3 %collective-permute-start.8 = (f32[2,16,256]{2,1,0:T(8,128)S(1)}, f32[2,16,256]{2,1,0:T(8,128)S(1)}, u32[]{:S(2)}, u32[]{:S(2)}) collective-permute-start(f32[2,16,256]{2,1,0:T(8,128)S(1)} %get-tuple-element.32), channel_id=1, source_target_pairs={{0,1},{1,0},{2,3},{3,2},{4,5},{5,4},{6,7},{7,6},{8,9},{9,8},{10,11... | collective-permute-start | bytes 98312 | tf_op jit(solution)/shard_map/ppermute | solution.py:18
  22.6 1.8 %collective-permute-done.6 = f32[2,16,256]{2,1,0:T(8,128)S(1)} collective-permute-done((f32[2,16,256]{2,1,0:T(8,128)S(1)}, f32[2,16,256]{2,1,0:T(8,128)S(1)}, u32[]{:S(2)}, u32[]{:S(2)}) %collective-permute-start.6) | collective-permute-done | bytes 32800 | tf_op jit(solution)/shard_map/ppermute | solution.py:18
  24.4 0.4 %collective-permute-done.7 = f32[2,16,256]{2,1,0:T(8,128)S(1)} collective-permute-done((f32[2,16,256]{2,1,0:T(8,128)S(1)}, f32[2,16,256]{2,1,0:T(8,128)S(1)}, u32[]{:S(2)}, u32[]{:S(2)}) %collective-permute-start.7) | collective-permute-done | bytes 32800 | tf_op jit(solution)/shard_map/ppermute | solution.py:18
  24.8 0.0 collective-permute-done.8
  24.8 0.6 %add_add_fusion = f32[2,16,256]{2,1,0:T(8,128)} fusion(f32[2,16,256]{2,1,0:T(8,128)S(1)} %collective-permute-done.8, f32[2,16,256]{2,1,0:T(8,128)S(1)} %collective-permute-done.7, f32[2,16,256]{2,1,0:T(8,128)S(1)} %get-tuple-element.29, f32[2,16,256]{2,1,0:T(8,128)S(1)} %collective-permute-done.6), kind=kLoop, calls=%fused_computation | loop fusion | flops 24576 | bytes 163840 | tf_op jit(solution)/shard_map/add | solution.py:159
Async XLA Ops:
  0.8 7.7 %collective-permute-start = (f32[128,128]{1,0:T(8,128)S(1)}, f32[128,128]{1,0:T(8,128)S(1)}, u32[]{:S(2)}, u32[]{:S(2)}) collective-permute-start(f32[128,128]{1,0:T(8,128)S(1)} %slice.8.refs_1_), channel_id=1, source_target_pairs={{0,16},{4,20},{8,24},{12,28},{16,0},{20,4},{24,8},{28,12},{1,17},{... | collective-permute-start | bytes 196616 | tf_op jit(solution)/shard_map/ppermute | solution.py:18
  5.7 5.5 %collective-permute-start.3 = (f32[128,128]{1,0:T(8,128)S(1)}, f32[128,128]{1,0:T(8,128)S(1)}, u32[]{:S(2)}, u32[]{:S(2)}) collective-permute-start(f32[128,128]{1,0:T(8,128)S(1)} %slice.7.refs_0_), channel_id=1, source_target_pairs={{0,16},{4,20},{8,24},{12,28},{16,0},{20,4},{24,8},{28,12},{1,17},{... | collective-permute-start | bytes 196616 | tf_op jit(solution)/shard_map/ppermute | solution.py:18
  5.7 1.9 %copy-start = (f32[1,3,16,64,256]{4,3,2,1,0:T(8,128)S(1)}, f32[1,3,16,64,256]{4,3,2,1,0:T(8,128)}, u32[]{:S(2)}) copy-start(f32[1,3,16,64,256]{4,3,2,1,0:T(8,128)} %f_hbm.1) | copy-start | bytes 9437188
  8.8 4.5 %collective-permute-start.1 = (f32[128,128]{1,0:T(8,128)S(1)}, f32[128,128]{1,0:T(8,128)S(1)}, u32[]{:S(2)}, u32[]{:S(2)}) collective-permute-start(f32[128,128]{1,0:T(8,128)S(1)} %level0_1.1.own_ref), channel_id=1, source_target_pairs={{0,8},{4,12},{8,0},{12,4},{16,24},{20,28},{24,16},{28,20},{1,9},{5... | collective-permute-start | bytes 196616 | tf_op jit(solution)/shard_map/ppermute | solution.py:18
  11.5 4.3 %collective-permute-start.4 = (f32[128,128]{1,0:T(8,128)S(1)}, f32[128,128]{1,0:T(8,128)S(1)}, u32[]{:S(2)}, u32[]{:S(2)}) collective-permute-start(f32[128,128]{1,0:T(8,128)S(1)} %level0_0.1.own_ref), channel_id=1, source_target_pairs={{0,8},{4,12},{8,0},{12,4},{16,24},{20,28},{24,16},{28,20},{1,9},{5... | collective-permute-start | bytes 196616 | tf_op jit(solution)/shard_map/ppermute | solution.py:18
  13.7 4.7 %collective-permute-start.2 = (f32[128,128]{1,0:T(8,128)S(1)}, f32[128,128]{1,0:T(8,128)S(1)}, u32[]{:S(2)}, u32[]{:S(2)}) collective-permute-start(f32[128,128]{1,0:T(8,128)S(1)} %level1_1.1.own_ref), channel_id=1, source_target_pairs={{0,4},{4,0},{8,12},{12,8},{16,20},{20,16},{24,28},{28,24},{1,5},{5... | collective-permute-start | bytes 196616 | tf_op jit(solution)/shard_map/ppermute | solution.py:18
  16.1 4.3 %collective-permute-start.5 = (f32[128,128]{1,0:T(8,128)S(1)}, f32[128,128]{1,0:T(8,128)S(1)}, u32[]{:S(2)}, u32[]{:S(2)}) collective-permute-start(f32[128,128]{1,0:T(8,128)S(1)} %level1_0.1.own_ref), channel_id=1, source_target_pairs={{0,4},{4,0},{8,12},{12,8},{16,20},{20,16},{24,28},{28,24},{1,5},{5... | collective-permute-start | bytes 196616 | tf_op jit(solution)/shard_map/ppermute | solution.py:18
  20.7 3.7 %collective-permute-start.6 = (f32[2,16,256]{2,1,0:T(8,128)S(1)}, f32[2,16,256]{2,1,0:T(8,128)S(1)}, u32[]{:S(2)}, u32[]{:S(2)}) collective-permute-start(f32[2,16,256]{2,1,0:T(8,128)S(1)} %get-tuple-element.30), channel_id=1, source_target_pairs={{0,3},{1,2},{2,1},{3,0},{4,7},{5,6},{6,5},{7,4},{8,11},{9,10},{10,... | collective-permute-start | bytes 98312 | tf_op jit(solution)/shard_map/ppermute | solution.py:18
  20.8 4.0 %collective-permute-start.7 = (f32[2,16,256]{2,1,0:T(8,128)S(1)}, f32[2,16,256]{2,1,0:T(8,128)S(1)}, u32[]{:S(2)}, u32[]{:S(2)}) collective-permute-start(f32[2,16,256]{2,1,0:T(8,128)S(1)} %get-tuple-element.31), channel_id=1, source_target_pairs={{0,2},{1,3},{2,0},{3,1},{4,6},{5,7},{6,4},{7,5},{8,10},{9,11},{10,... | collective-permute-start | bytes 98312 | tf_op jit(solution)/shard_map/ppermute | solution.py:18
  22.3 2.5 %collective-permute-start.8 = (f32[2,16,256]{2,1,0:T(8,128)S(1)}, f32[2,16,256]{2,1,0:T(8,128)S(1)}, u32[]{:S(2)}, u32[]{:S(2)}) collective-permute-start(f32[2,16,256]{2,1,0:T(8,128)S(1)} %get-tuple-element.32), channel_id=1, source_target_pairs={{0,1},{1,0},{2,3},{3,2},{4,5},{5,4},{6,7},{7,6},{8,9},{9,8},{10,11... | collective-permute-start | bytes 98312 | tf_op jit(solution)/shard_map/ppermute | solution.py:18

commit v8 on v7

--- a/solution.py
+++ b/solution.py
@@ -38,7 +38,7 @@
     high, low = split(stack)
     rows = factor.shape[0] // 2
     dot = functools.partial(jnp.dot, preferred_element_type=jnp.float32)
-    full = dot(factor[:rows], high) + dot(factor[:rows], low) + dot(factor[rows:], high)
+    full = dot(factor[:rows], high) + dot(factor[rows:], high) + dot(factor[:rows], low)
     block = lax.broadcasted_iota(jnp.int32, (rank, 2 * n), 1) % (n // 2) // width
     out = full[:rank]
     for p in range(1, rows // rank):

time: 25.9 us -> 25.9 us (level)
  no operation moved by 1% of the time
where the time goes in v8:
time: 25.9 us; the launch traced here: 25.4 us
  starting transfers between devices  12.9 us (50%)
  waiting for transfers between devices  4.62 us (18%)
  Pallas kernels  3.66 us (14%)
  local copies, waits for them, and re-layouts  3.57 us (14%)
  other arithmetic  0.63 us (2%)
    ppermute x9, starting transfers between devices, swapped(): return lax.ppermute(value, axis, pairs)  12.9 us
    ppermute x9, waiting for transfers between devices, swapped(): return lax.ppermute(value, axis, pairs)  4.62 us
    pallas_call x12, Pallas kernels, call(): pl.pallas_call(kernel, out_shape=outs, in_specs=specs or [VMEM] * len(arg...  3.66 us
    unnamed x2, local copies, waits for them, and re-layouts  1.88 us
    slice x1, local copies, waits for them, and re-layouts, per_device(): one = raw[:, step:]  0.84 us
    slice x1, local copies, waits for them, and re-layouts, per_device(): states = [rest[:, :step], one]  0.84 us
    add x1, other arithmetic, per_device(): total = total + p  0.63 us
  transfers between devices with their start and end apart: 9, of which 6 were waited for; matrix products, arithmetic and copies ran while one was open for 3% of the time, Pallas kernels for 13%

profile of v8, /device:TPU:0, one launch (start us, length us, event | category | flops | bytes accessed | tf_op | source)
XLA Modules:
  0.0 25.4 jit_solution(7191753544748773722)
XLA Ops:
  0.0 0.8 %slice.8.refs_1_ = f32[128,128]{1,0:T(8,128)S(1)} slice(f32[128,256]{1,0:T(8,128)} %bitcast.2), slice={[0:128], [128:256]} | slice | bytes 131072 | tf_op jit(solution)/shard_map/slice | solution.py:116
  0.8 4.0 %collective-permute-start = (f32[128,128]{1,0:T(8,128)S(1)}, f32[128,128]{1,0:T(8,128)S(1)}, u32[]{:S(2)}, u32[]{:S(2)}) collective-permute-start(f32[128,128]{1,0:T(8,128)S(1)} %slice.8.refs_1_), channel_id=1, source_target_pairs={{0,16},{4,20},{8,24},{12,28},{16,0},{20,4},{24,8},{28,12},{1,17},{... | collective-permute-start | bytes 196616 | tf_op jit(solution)/shard_map/ppermute | solution.py:18
  4.9 0.8 %slice.7.refs_0_ = f32[128,128]{1,0:T(8,128)S(1)} slice(f32[128,256]{1,0:T(8,128)} %bitcast.3), slice={[0:128], [0:128]} | slice | bytes 131072 | tf_op jit(solution)/shard_map/slice | solution.py:118
  5.7 0.0 collective-permute-start.3
  5.7 0.0 copy-start
  5.7 1.9 %copy-done = f32[1,3,16,64,256]{4,3,2,1,0:T(8,128)S(1)} copy-done((f32[1,3,16,64,256]{4,3,2,1,0:T(8,128)S(1)}, f32[1,3,16,64,256]{4,3,2,1,0:T(8,128)}, u32[]{:S(2)}) %copy-start) | copy-done | bytes 3145752
  7.6 0.5 %prepare.1 = (bf16[2,512,256]{2,1,0:T(8,128)(2,1)S(1)}, bf16[2,512,256]{2,1,0:T(8,128)(2,1)S(1)}, bf16[2,512,256]{2,1,0:T(8,128)(2,1)S(1)}, bf16[2,512,256]{2,1,...) custom-call(f32[1,3,16,64,256]{4,3,2,1,0:T(8,128)S(1)} %copy-done), custom_call_target="tpu_custom_call" | custom-call | tf_op jit(solution)/shard_map/prepare/pallas_call | solution.py:97
  8.1 0.4 %own0.1 = (f32[128,128]{1,0:T(8,128)S(1)}, f32[128,128]{1,0:T(8,128)S(1)}) custom-call(f32[128,128]{1,0:T(8,128)S(1)} %slice.7.refs_0_, f32[128,128]{1,0:T(8,128)S(1)} %slice.8.refs_1_, bf16[2,512,256]{2,1,0:T(8,128)(2,1)S(1)} %get-tuple-element.21.refs_2_), custom_call_target="tpu_custom_call" | custom-call | tf_op jit(solution)/shard_map/own0/pallas_call | solution.py:97
  8.5 0.0 collective-permute-done.got_ref
  8.5 0.3 %level0_1.1.own_ref = f32[128,128]{1,0:T(8,128)S(1)} custom-call(f32[128,128]{1,0:T(8,128)S(1)} %get-tuple-element.22.base_ref, f32[128,128]{1,0:T(8,128)S(1)} %collective-permute-done.got_ref, bf16[2,512,256]{2,1,0:T(8,128)(2,1)S(1)} %get-tuple-element.23.f_ref), custom_call_target="tpu_custom_call" | custom-call | tf_op jit(solution)/shard_map/level0_1/pallas_call | solution.py:97
  8.8 2.2 %collective-permute-start.1 = (f32[128,128]{1,0:T(8,128)S(1)}, f32[128,128]{1,0:T(8,128)S(1)}, u32[]{:S(2)}, u32[]{:S(2)}) collective-permute-start(f32[128,128]{1,0:T(8,128)S(1)} %level0_1.1.own_ref), channel_id=1, source_target_pairs={{0,8},{4,12},{8,0},{12,4},{16,24},{20,28},{24,16},{28,20},{1,9},{5... | collective-permute-start | bytes 196616 | tf_op jit(solution)/shard_map/ppermute | solution.py:18
  11.0 0.2 collective-permute-done.3.got_ref
  11.2 0.3 %level0_0.1.own_ref = f32[128,128]{1,0:T(8,128)S(1)} custom-call(f32[128,128]{1,0:T(8,128)S(1)} %get-tuple-element.28.base_ref, f32[128,128]{1,0:T(8,128)S(1)} %collective-permute-done.3.got_ref, bf16[2,512,256]{2,1,0:T(8,128)(2,1)S(1)} %get-tuple-element.23.f_ref), custom_call_target="tpu_custom_call" | custom-call | tf_op jit(solution)/shard_map/level0_0/pallas_call | solution.py:97
  11.5 1.3 %collective-permute-start.4 = (f32[128,128]{1,0:T(8,128)S(1)}, f32[128,128]{1,0:T(8,128)S(1)}, u32[]{:S(2)}, u32[]{:S(2)}) collective-permute-start(f32[128,128]{1,0:T(8,128)S(1)} %level0_0.1.own_ref), channel_id=1, source_target_pairs={{0,8},{4,12},{8,0},{12,4},{16,24},{20,28},{24,16},{28,20},{1,9},{5... | collective-permute-start | bytes 196616 | tf_op jit(solution)/shard_map/ppermute | solution.py:18
  12.8 0.3 %own1_0.1.base_ref = f32[128,128]{1,0:T(8,128)S(1)} custom-call(f32[128,128]{1,0:T(8,128)S(1)} %level0_0.1.own_ref, bf16[2,512,256]{2,1,0:T(8,128)(2,1)S(1)} %get-tuple-element.24.f_ref), custom_call_target="tpu_custom_call" | custom-call | tf_op jit(solution)/shard_map/own1_0/pallas_call | solution.py:97
  13.1 0.3 %own1_1.1.base_ref = f32[128,128]{1,0:T(8,128)S(1)} custom-call(f32[128,128]{1,0:T(8,128)S(1)} %level0_1.1.own_ref, bf16[2,512,256]{2,1,0:T(8,128)(2,1)S(1)} %get-tuple-element.24.f_ref), custom_call_target="tpu_custom_call" | custom-call | tf_op jit(solution)/shard_map/own1_1/pallas_call | solution.py:97
  13.4 0.0 collective-permute-done.1.got_ref
  13.4 0.3 %level1_1.1.own_ref = f32[128,128]{1,0:T(8,128)S(1)} custom-call(f32[128,128]{1,0:T(8,128)S(1)} %own1_1.1.base_ref, f32[128,128]{1,0:T(8,128)S(1)} %collective-permute-done.1.got_ref, bf16[2,512,256]{2,1,0:T(8,128)(2,1)S(1)} %get-tuple-element.25.f_ref), custom_call_target="tpu_custom_call" | custom-call | tf_op jit(solution)/shard_map/level1_1/pallas_call | solution.py:97
  13.7 1.8 %collective-permute-start.2 = (f32[128,128]{1,0:T(8,128)S(1)}, f32[128,128]{1,0:T(8,128)S(1)}, u32[]{:S(2)}, u32[]{:S(2)}) collective-permute-start(f32[128,128]{1,0:T(8,128)S(1)} %level1_1.1.own_ref), channel_id=1, source_target_pairs={{0,4},{4,0},{8,12},{12,8},{16,20},{20,16},{24,28},{28,24},{1,5},{5... | collective-permute-start | bytes 196616 | tf_op jit(solution)/shard_map/ppermute | solution.py:18
  15.5 0.3 %collective-permute-done.4.got_ref = f32[128,128]{1,0:T(8,128)S(1)} collective-permute-done((f32[128,128]{1,0:T(8,128)S(1)}, f32[128,128]{1,0:T(8,128)S(1)}, u32[]{:S(2)}, u32[]{:S(2)}) %collective-permute-start.4) | collective-permute-done | bytes 65568 | tf_op jit(solution)/shard_map/ppermute | solution.py:18
  15.8 0.3 %level1_0.1.own_ref = f32[128,128]{1,0:T(8,128)S(1)} custom-call(f32[128,128]{1,0:T(8,128)S(1)} %own1_0.1.base_ref, f32[128,128]{1,0:T(8,128)S(1)} %collective-permute-done.4.got_ref, bf16[2,512,256]{2,1,0:T(8,128)(2,1)S(1)} %get-tuple-element.25.f_ref), custom_call_target="tpu_custom_call" | custom-call | tf_op jit(solution)/shard_map/level1_0/pallas_call | solution.py:97
  16.1 1.6 %collective-permute-start.5 = (f32[128,128]{1,0:T(8,128)S(1)}, f32[128,128]{1,0:T(8,128)S(1)}, u32[]{:S(2)}, u32[]{:S(2)}) collective-permute-start(f32[128,128]{1,0:T(8,128)S(1)} %level1_0.1.own_ref), channel_id=1, source_target_pairs={{0,4},{4,0},{8,12},{12,8},{16,20},{20,16},{24,28},{28,24},{1,5},{5... | collective-permute-start | bytes 196616 | tf_op jit(solution)/shard_map/ppermute | solution.py:18
  17.7 0.3 %own2_0.1.base_ref = f32[128,128]{1,0:T(8,128)S(1)} custom-call(f32[128,128]{1,0:T(8,128)S(1)} %level1_0.1.own_ref, bf16[2,512,256]{2,1,0:T(8,128)(2,1)S(1)} %get-tuple-element.26.f_ref), custom_call_target="tpu_custom_call" | custom-call | tf_op jit(solution)/shard_map/own2_0/pallas_call | solution.py:97
  18.0 0.3 %own2_1.1.base_ref = f32[128,128]{1,0:T(8,128)S(1)} custom-call(f32[128,128]{1,0:T(8,128)S(1)} %level1_1.1.own_ref, bf16[2,512,256]{2,1,0:T(8,128)(2,1)S(1)} %get-tuple-element.26.f_ref), custom_call_target="tpu_custom_call" | custom-call | tf_op jit(solution)/shard_map/own2_1/pallas_call | solution.py:97
  18.2 0.2 collective-permute-done.2.got_ref
  18.4 0.3 %level2_1.1.done_ref = f32[128,128]{1,0:T(8,128)S(1)} custom-call(f32[128,128]{1,0:T(8,128)S(1)} %own2_1.1.base_ref, f32[128,128]{1,0:T(8,128)S(1)} %collective-permute-done.2.got_ref, bf16[2,512,256]{2,1,0:T(8,128)(2,1)S(1)} %get-tuple-element.27.f_ref), custom_call_target="tpu_custom_call" | custom-call | tf_op jit(solution)/shard_map/level2_1/pallas_call | solution.py:97
  18.7 1.7 %collective-permute-done.5.got_ref = f32[128,128]{1,0:T(8,128)S(1)} collective-permute-done((f32[128,128]{1,0:T(8,128)S(1)}, f32[128,128]{1,0:T(8,128)S(1)}, u32[]{:S(2)}, u32[]{:S(2)}) %collective-permute-start.5) | collective-permute-done | bytes 65568 | tf_op jit(solution)/shard_map/ppermute | solution.py:18
  20.4 0.3 %last.1 = (f32[2,16,256]{2,1,0:T(8,128)S(1)}, f32[2,16,256]{2,1,0:T(8,128)S(1)}, f32[2,16,256]{2,1,0:T(8,128)S(1)}, f32[2,16,256]{2,1,0:T(8,128)S(1)}) custom-call(s32[1]{0:T(128)} %bitcast.me_ref, f32[128,128]{1,0:T(8,128)S(1)} %level2_1.1.done_ref, f32[128,128]{1,0:T(8,128)S(1)} %own2_0.1.base_ref, f32[128,128]{1,0:T(8,128)S(1)} %collective-permute-done.5.got_ref, ...), custom_call_target="tpu_custom_call" | custom-call | tf_op jit(solution)/shard_map/last/pallas_call | solution.py:97
  20.7 0.1 collective-permute-start.6
  20.8 1.6 %collective-permute-start.7 = (f32[2,16,256]{2,1,0:T(8,128)S(1)}, f32[2,16,256]{2,1,0:T(8,128)S(1)}, u32[]{:S(2)}, u32[]{:S(2)}) collective-permute-start(f32[2,16,256]{2,1,0:T(8,128)S(1)} %get-tuple-element.31), channel_id=1, source_target_pairs={{0,2},{1,3},{2,0},{3,1},{4,6},{5,7},{6,4},{7,5},{8,10},{9,11},{10,... | collective-permute-start | bytes 98312 | tf_op jit(solution)/shard_map/ppermute | solution.py:18
  22.3 0.3 %collective-permute-start.8 = (f32[2,16,256]{2,1,0:T(8,128)S(1)}, f32[2,16,256]{2,1,0:T(8,128)S(1)}, u32[]{:S(2)}, u32[]{:S(2)}) collective-permute-start(f32[2,16,256]{2,1,0:T(8,128)S(1)} %get-tuple-element.32), channel_id=1, source_target_pairs={{0,1},{1,0},{2,3},{3,2},{4,5},{5,4},{6,7},{7,6},{8,9},{9,8},{10,11... | collective-permute-start | bytes 98312 | tf_op jit(solution)/shard_map/ppermute | solution.py:18
  22.6 1.8 %collective-permute-done.6 = f32[2,16,256]{2,1,0:T(8,128)S(1)} collective-permute-done((f32[2,16,256]{2,1,0:T(8,128)S(1)}, f32[2,16,256]{2,1,0:T(8,128)S(1)}, u32[]{:S(2)}, u32[]{:S(2)}) %collective-permute-start.6) | collective-permute-done | bytes 32800 | tf_op jit(solution)/shard_map/ppermute | solution.py:18
  24.4 0.4 %collective-permute-done.7 = f32[2,16,256]{2,1,0:T(8,128)S(1)} collective-permute-done((f32[2,16,256]{2,1,0:T(8,128)S(1)}, f32[2,16,256]{2,1,0:T(8,128)S(1)}, u32[]{:S(2)}, u32[]{:S(2)}) %collective-permute-start.7) | collective-permute-done | bytes 32800 | tf_op jit(solution)/shard_map/ppermute | solution.py:18
  24.8 0.0 collective-permute-done.8
  24.8 0.6 %add_add_fusion = f32[2,16,256]{2,1,0:T(8,128)} fusion(f32[2,16,256]{2,1,0:T(8,128)S(1)} %collective-permute-done.8, f32[2,16,256]{2,1,0:T(8,128)S(1)} %collective-permute-done.7, f32[2,16,256]{2,1,0:T(8,128)S(1)} %get-tuple-element.29, f32[2,16,256]{2,1,0:T(8,128)S(1)} %collective-permute-done.6), kind=kLoop, calls=%fused_computation | loop fusion | flops 24576 | bytes 163840 | tf_op jit(solution)/shard_map/add | solution.py:159
Async XLA Ops:
  0.8 7.7 %collective-permute-start = (f32[128,128]{1,0:T(8,128)S(1)}, f32[128,128]{1,0:T(8,128)S(1)}, u32[]{:S(2)}, u32[]{:S(2)}) collective-permute-start(f32[128,128]{1,0:T(8,128)S(1)} %slice.8.refs_1_), channel_id=1, source_target_pairs={{0,16},{4,20},{8,24},{12,28},{16,0},{20,4},{24,8},{28,12},{1,17},{... | collective-permute-start | bytes 196616 | tf_op jit(solution)/shard_map/ppermute | solution.py:18
  5.7 5.5 %collective-permute-start.3 = (f32[128,128]{1,0:T(8,128)S(1)}, f32[128,128]{1,0:T(8,128)S(1)}, u32[]{:S(2)}, u32[]{:S(2)}) collective-permute-start(f32[128,128]{1,0:T(8,128)S(1)} %slice.7.refs_0_), channel_id=1, source_target_pairs={{0,16},{4,20},{8,24},{12,28},{16,0},{20,4},{24,8},{28,12},{1,17},{... | collective-permute-start | bytes 196616 | tf_op jit(solution)/shard_map/ppermute | solution.py:18
  5.7 1.9 %copy-start = (f32[1,3,16,64,256]{4,3,2,1,0:T(8,128)S(1)}, f32[1,3,16,64,256]{4,3,2,1,0:T(8,128)}, u32[]{:S(2)}) copy-start(f32[1,3,16,64,256]{4,3,2,1,0:T(8,128)} %f_hbm.1) | copy-start | bytes 9437188
  8.8 4.6 %collective-permute-start.1 = (f32[128,128]{1,0:T(8,128)S(1)}, f32[128,128]{1,0:T(8,128)S(1)}, u32[]{:S(2)}, u32[]{:S(2)}) collective-permute-start(f32[128,128]{1,0:T(8,128)S(1)} %level0_1.1.own_ref), channel_id=1, source_target_pairs={{0,8},{4,12},{8,0},{12,4},{16,24},{20,28},{24,16},{28,20},{1,9},{5... | collective-permute-start | bytes 196616 | tf_op jit(solution)/shard_map/ppermute | solution.py:18
  11.5 4.3 %collective-permute-start.4 = (f32[128,128]{1,0:T(8,128)S(1)}, f32[128,128]{1,0:T(8,128)S(1)}, u32[]{:S(2)}, u32[]{:S(2)}) collective-permute-start(f32[128,128]{1,0:T(8,128)S(1)} %level0_0.1.own_ref), channel_id=1, source_target_pairs={{0,8},{4,12},{8,0},{12,4},{16,24},{20,28},{24,16},{28,20},{1,9},{5... | collective-permute-start | bytes 196616 | tf_op jit(solution)/shard_map/ppermute | solution.py:18
  13.7 4.7 %collective-permute-start.2 = (f32[128,128]{1,0:T(8,128)S(1)}, f32[128,128]{1,0:T(8,128)S(1)}, u32[]{:S(2)}, u32[]{:S(2)}) collective-permute-start(f32[128,128]{1,0:T(8,128)S(1)} %level1_1.1.own_ref), channel_id=1, source_target_pairs={{0,4},{4,0},{8,12},{12,8},{16,20},{20,16},{24,28},{28,24},{1,5},{5... | collective-permute-start | bytes 196616 | tf_op jit(solution)/shard_map/ppermute | solution.py:18
  16.1 4.3 %collective-permute-start.5 = (f32[128,128]{1,0:T(8,128)S(1)}, f32[128,128]{1,0:T(8,128)S(1)}, u32[]{:S(2)}, u32[]{:S(2)}) collective-permute-start(f32[128,128]{1,0:T(8,128)S(1)} %level1_0.1.own_ref), channel_id=1, source_target_pairs={{0,4},{4,0},{8,12},{12,8},{16,20},{20,16},{24,28},{28,24},{1,5},{5... | collective-permute-start | bytes 196616 | tf_op jit(solution)/shard_map/ppermute | solution.py:18
  20.7 3.7 %collective-permute-start.6 = (f32[2,16,256]{2,1,0:T(8,128)S(1)}, f32[2,16,256]{2,1,0:T(8,128)S(1)}, u32[]{:S(2)}, u32[]{:S(2)}) collective-permute-start(f32[2,16,256]{2,1,0:T(8,128)S(1)} %get-tuple-element.30), channel_id=1, source_target_pairs={{0,3},{1,2},{2,1},{3,0},{4,7},{5,6},{6,5},{7,4},{8,11},{9,10},{10,... | collective-permute-start | bytes 98312 | tf_op jit(solution)/shard_map/ppermute | solution.py:18
  20.8 4.0 %collective-permute-start.7 = (f32[2,16,256]{2,1,0:T(8,128)S(1)}, f32[2,16,256]{2,1,0:T(8,128)S(1)}, u32[]{:S(2)}, u32[]{:S(2)}) collective-permute-start(f32[2,16,256]{2,1,0:T(8,128)S(1)} %get-tuple-element.31), channel_id=1, source_target_pairs={{0,2},{1,3},{2,0},{3,1},{4,6},{5,7},{6,4},{7,5},{8,10},{9,11},{10,... | collective-permute-start | bytes 98312 | tf_op jit(solution)/shard_map/ppermute | solution.py:18
  22.3 2.5 %collective-permute-start.8 = (f32[2,16,256]{2,1,0:T(8,128)S(1)}, f32[2,16,256]{2,1,0:T(8,128)S(1)}, u32[]{:S(2)}, u32[]{:S(2)}) collective-permute-start(f32[2,16,256]{2,1,0:T(8,128)S(1)} %get-tuple-element.32), channel_id=1, source_target_pairs={{0,1},{1,0},{2,3},{3,2},{4,5},{5,4},{6,7},{7,6},{8,9},{9,8},{10,11... | collective-permute-start | bytes 98312 | tf_op jit(solution)/shard_map/ppermute | solution.py:18

commit v9 on v8

--- a/solution.py
+++ b/solution.py
@@ -65,10 +65,6 @@
                     out[c, rows:, side] = low[:, part * half : (part + 1) * half]
 
 
-def own_kernel(own_ref, f_ref, out_ref, *, i, width):
-    out_ref[...] = product(own_ref[...], f_ref[i], width)
-
-
 def owns_kernel(*refs, width):
     f_ref = refs[CHUNKS]
     for i, out in enumerate(refs[CHUNKS + 1 :]):
@@ -129,17 +125,12 @@
         own, other = halves[2 * level : 2 * level + 2]
         for i in order:
             kw = dict(i=i, width=width)
-            if level:
-                base = call(
-                    functools.partial(own_kernel, **kw), shape, states[i], own, name=f"own{level}_{i}"
+            if i == order[0]:
+                bases = call(
+                    functools.partial(owns_kernel, width=width), [shape] * CHUNKS, *states, own,
+                    name=f"own{level}",
                 )
-            else:
-                if i == order[0]:
-                    bases = call(
-                        functools.partial(owns_kernel, width=width), [shape] * CHUNKS, *states, own,
-                        name="own0",
-                    )
-                base = bases[i]
+            base = bases[i]
             if (level, i) == (LEVELS - 1, order[-1]):
                 pieces = call(
                     functools.partial(last_kernel, **kw), [piece] * groups,

time: 25.9 us -> 25.9 us (level)
  Pallas kernels: 3.66 us -> 3.33 us
    pallas_call x12 -> x10, Pallas kernels: 3.66 us -> 3.33 us  [call(): pl.pallas_call(kernel, out_shape=outs, in_specs=specs or [VMEM] * len(arg...]
  transfers between devices with their start and end apart: 9 -> 9, of which waited for: 6 -> 6; matrix products, arithmetic and copies ran while one was open for 3% -> 3% of each run, Pallas kernels for 13% -> 12%
where the time goes in v9:
time: 25.9 us; the launch traced here: 25.4 us
  starting transfers between devices  13 us (50%)
  waiting for transfers between devices  4.82 us (19%)
  local copies, waits for them, and re-layouts  3.57 us (14%)
  Pallas kernels  3.33 us (13%)
  other arithmetic  0.63 us (2%)
    ppermute x9, starting transfers between devices, swapped(): return lax.ppermute(value, axis, pairs)  13 us
    ppermute x9, waiting for transfers between devices, swapped(): return lax.ppermute(value, axis, pairs)  4.82 us
    pallas_call x10, Pallas kernels, call(): pl.pallas_call(kernel, out_shape=outs, in_specs=specs or [VMEM] * len(arg...  3.33 us
    unnamed x2, local copies, waits for them, and re-layouts  1.88 us
    slice x1, local copies, waits for them, and re-layouts, per_device(): one = raw[:, step:]  0.84 us
    slice x1, local copies, waits for them, and re-layouts, per_device(): states = [rest[:, :step], one]  0.84 us
    add x1, other arithmetic, per_device(): total = total + p  0.63 us
  transfers between devices with their start and end apart: 9, of which 6 were waited for; matrix products, arithmetic and copies ran while one was open for 3% of the time, Pallas kernels for 12%

profile of v9, /device:TPU:0, one launch (start us, length us, event | category | flops | bytes accessed | tf_op | source)
XLA Modules:
  0.0 25.4 jit_solution(2095516395329296657)
XLA Ops:
  0.0 0.8 %slice.8.refs_1_ = f32[128,128]{1,0:T(8,128)S(1)} slice(f32[128,256]{1,0:T(8,128)} %bitcast.2), slice={[0:128], [128:256]} | slice | bytes 131072 | tf_op jit(solution)/shard_map/slice | solution.py:112
  0.8 4.0 %collective-permute-start.1 = (f32[128,128]{1,0:T(8,128)S(1)}, f32[128,128]{1,0:T(8,128)S(1)}, u32[]{:S(2)}, u32[]{:S(2)}) collective-permute-start(f32[128,128]{1,0:T(8,128)S(1)} %slice.8.refs_1_), channel_id=1, source_target_pairs={{0,16},{4,20},{8,24},{12,28},{16,0},{20,4},{24,8},{28,12},{1,17},{... | collective-permute-start | bytes 196616 | tf_op jit(solution)/shard_map/ppermute | solution.py:18
  4.9 0.8 %slice.7.refs_0_ = f32[128,128]{1,0:T(8,128)S(1)} slice(f32[128,256]{1,0:T(8,128)} %bitcast.3), slice={[0:128], [0:128]} | slice | bytes 131072 | tf_op jit(solution)/shard_map/slice | solution.py:114
  5.7 0.0 collective-permute-start
  5.7 0.0 copy-start
  5.7 1.9 %copy-done = f32[1,3,16,64,256]{4,3,2,1,0:T(8,128)S(1)} copy-done((f32[1,3,16,64,256]{4,3,2,1,0:T(8,128)S(1)}, f32[1,3,16,64,256]{4,3,2,1,0:T(8,128)}, u32[]{:S(2)}) %copy-start) | copy-done | bytes 3145752
  7.6 0.5 %prepare.1 = (bf16[2,512,256]{2,1,0:T(8,128)(2,1)S(1)}, bf16[2,512,256]{2,1,0:T(8,128)(2,1)S(1)}, bf16[2,512,256]{2,1,0:T(8,128)(2,1)S(1)}, bf16[2,512,256]{2,1,...) custom-call(f32[1,3,16,64,256]{4,3,2,1,0:T(8,128)S(1)} %copy-done), custom_call_target="tpu_custom_call" | custom-call | tf_op jit(solution)/shard_map/prepare/pallas_call | solution.py:93
  8.1 0.4 %own0.1 = (f32[128,128]{1,0:T(8,128)S(1)}, f32[128,128]{1,0:T(8,128)S(1)}) custom-call(f32[128,128]{1,0:T(8,128)S(1)} %slice.7.refs_0_, f32[128,128]{1,0:T(8,128)S(1)} %slice.8.refs_1_, bf16[2,512,256]{2,1,0:T(8,128)(2,1)S(1)} %get-tuple-element.25.refs_2_), custom_call_target="tpu_custom_call" | custom-call | tf_op jit(solution)/shard_map/own0/pallas_call | solution.py:93
  8.5 0.0 collective-permute-done.1.got_ref
  8.5 0.3 %level0_1.1.refs_1_ = f32[128,128]{1,0:T(8,128)S(1)} custom-call(f32[128,128]{1,0:T(8,128)S(1)} %get-tuple-element.28.base_ref, f32[128,128]{1,0:T(8,128)S(1)} %collective-permute-done.1.got_ref, bf16[2,512,256]{2,1,0:T(8,128)(2,1)S(1)} %get-tuple-element.27.f_ref), custom_call_target="tpu_custom_call" | custom-call | tf_op jit(solution)/shard_map/level0_1/pallas_call | solution.py:93
  8.8 2.2 %collective-permute-start.3 = (f32[128,128]{1,0:T(8,128)S(1)}, f32[128,128]{1,0:T(8,128)S(1)}, u32[]{:S(2)}, u32[]{:S(2)}) collective-permute-start(f32[128,128]{1,0:T(8,128)S(1)} %level0_1.1.refs_1_), channel_id=1, source_target_pairs={{0,8},{4,12},{8,0},{12,4},{16,24},{20,28},{24,16},{28,20},{1,9},{5... | collective-permute-start | bytes 196616 | tf_op jit(solution)/shard_map/ppermute | solution.py:18
  11.0 0.2 collective-permute-done.got_ref
  11.2 0.3 %level0_0.1.refs_0_ = f32[128,128]{1,0:T(8,128)S(1)} custom-call(f32[128,128]{1,0:T(8,128)S(1)} %get-tuple-element.26.base_ref, f32[128,128]{1,0:T(8,128)S(1)} %collective-permute-done.got_ref, bf16[2,512,256]{2,1,0:T(8,128)(2,1)S(1)} %get-tuple-element.27.f_ref), custom_call_target="tpu_custom_call" | custom-call | tf_op jit(solution)/shard_map/level0_0/pallas_call | solution.py:93
  11.5 1.3 %collective-permute-start.2 = (f32[128,128]{1,0:T(8,128)S(1)}, f32[128,128]{1,0:T(8,128)S(1)}, u32[]{:S(2)}, u32[]{:S(2)}) collective-permute-start(f32[128,128]{1,0:T(8,128)S(1)} %level0_0.1.refs_0_), channel_id=1, source_target_pairs={{0,8},{4,12},{8,0},{12,4},{16,24},{20,28},{24,16},{28,20},{1,9},{5... | collective-permute-start | bytes 196616 | tf_op jit(solution)/shard_map/ppermute | solution.py:18
  12.8 0.4 %own1.1 = (f32[128,128]{1,0:T(8,128)S(1)}, f32[128,128]{1,0:T(8,128)S(1)}) custom-call(f32[128,128]{1,0:T(8,128)S(1)} %level0_0.1.refs_0_, f32[128,128]{1,0:T(8,128)S(1)} %level0_1.1.refs_1_, bf16[2,512,256]{2,1,0:T(8,128)(2,1)S(1)} %get-tuple-element.29.refs_2_), custom_call_target="tpu_custom_call" | custom-call | tf_op jit(solution)/shard_map/own1/pallas_call | solution.py:93
  13.2 0.0 collective-permute-done.3.got_ref
  13.2 0.3 %level1_1.1.refs_1_ = f32[128,128]{1,0:T(8,128)S(1)} custom-call(f32[128,128]{1,0:T(8,128)S(1)} %get-tuple-element.32.base_ref, f32[128,128]{1,0:T(8,128)S(1)} %collective-permute-done.3.got_ref, bf16[2,512,256]{2,1,0:T(8,128)(2,1)S(1)} %get-tuple-element.31.f_ref), custom_call_target="tpu_custom_call" | custom-call | tf_op jit(solution)/shard_map/level1_1/pallas_call | solution.py:93
  13.5 1.9 %collective-permute-start.4 = (f32[128,128]{1,0:T(8,128)S(1)}, f32[128,128]{1,0:T(8,128)S(1)}, u32[]{:S(2)}, u32[]{:S(2)}) collective-permute-start(f32[128,128]{1,0:T(8,128)S(1)} %level1_1.1.refs_1_), channel_id=1, source_target_pairs={{0,4},{4,0},{8,12},{12,8},{16,20},{20,16},{24,28},{28,24},{1,5},{5... | collective-permute-start | bytes 196616 | tf_op jit(solution)/shard_map/ppermute | solution.py:18
  15.5 0.3 %collective-permute-done.2.got_ref = f32[128,128]{1,0:T(8,128)S(1)} collective-permute-done((f32[128,128]{1,0:T(8,128)S(1)}, f32[128,128]{1,0:T(8,128)S(1)}, u32[]{:S(2)}, u32[]{:S(2)}) %collective-permute-start.2) | collective-permute-done | bytes 65568 | tf_op jit(solution)/shard_map/ppermute | solution.py:18
  15.8 0.3 %level1_0.1.refs_0_ = f32[128,128]{1,0:T(8,128)S(1)} custom-call(f32[128,128]{1,0:T(8,128)S(1)} %get-tuple-element.30.base_ref, f32[128,128]{1,0:T(8,128)S(1)} %collective-permute-done.2.got_ref, bf16[2,512,256]{2,1,0:T(8,128)(2,1)S(1)} %get-tuple-element.31.f_ref), custom_call_target="tpu_custom_call" | custom-call | tf_op jit(solution)/shard_map/level1_0/pallas_call | solution.py:93
  16.1 1.6 %collective-permute-start.5 = (f32[128,128]{1,0:T(8,128)S(1)}, f32[128,128]{1,0:T(8,128)S(1)}, u32[]{:S(2)}, u32[]{:S(2)}) collective-permute-start(f32[128,128]{1,0:T(8,128)S(1)} %level1_0.1.refs_0_), channel_id=1, source_target_pairs={{0,4},{4,0},{8,12},{12,8},{16,20},{20,16},{24,28},{28,24},{1,5},{5... | collective-permute-start | bytes 196616 | tf_op jit(solution)/shard_map/ppermute | solution.py:18
  17.7 0.4 %own2.1 = (f32[128,128]{1,0:T(8,128)S(1)}, f32[128,128]{1,0:T(8,128)S(1)}) custom-call(f32[128,128]{1,0:T(8,128)S(1)} %level1_0.1.refs_0_, f32[128,128]{1,0:T(8,128)S(1)} %level1_1.1.refs_1_, bf16[2,512,256]{2,1,0:T(8,128)(2,1)S(1)} %get-tuple-element.33.refs_2_), custom_call_target="tpu_custom_call" | custom-call | tf_op jit(solution)/shard_map/own2/pallas_call | solution.py:93
  18.1 0.3 %collective-permute-done.4.got_ref = f32[128,128]{1,0:T(8,128)S(1)} collective-permute-done((f32[128,128]{1,0:T(8,128)S(1)}, f32[128,128]{1,0:T(8,128)S(1)}, u32[]{:S(2)}, u32[]{:S(2)}) %collective-permute-start.4) | collective-permute-done | bytes 65568 | tf_op jit(solution)/shard_map/ppermute | solution.py:18
  18.4 0.3 %level2_1.1.done_ref = f32[128,128]{1,0:T(8,128)S(1)} custom-call(f32[128,128]{1,0:T(8,128)S(1)} %get-tuple-element.34.base_ref, f32[128,128]{1,0:T(8,128)S(1)} %collective-permute-done.4.got_ref, bf16[2,512,256]{2,1,0:T(8,128)(2,1)S(1)} %get-tuple-element.35.f_ref), custom_call_target="tpu_custom_call" | custom-call | tf_op jit(solution)/shard_map/level2_1/pallas_call | solution.py:93
  18.6 1.8 %collective-permute-done.5.got_ref = f32[128,128]{1,0:T(8,128)S(1)} collective-permute-done((f32[128,128]{1,0:T(8,128)S(1)}, f32[128,128]{1,0:T(8,128)S(1)}, u32[]{:S(2)}, u32[]{:S(2)}) %collective-permute-start.5) | collective-permute-done | bytes 65568 | tf_op jit(solution)/shard_map/ppermute | solution.py:18
  20.4 0.3 %last.1 = (f32[2,16,256]{2,1,0:T(8,128)S(1)}, f32[2,16,256]{2,1,0:T(8,128)S(1)}, f32[2,16,256]{2,1,0:T(8,128)S(1)}, f32[2,16,256]{2,1,0:T(8,128)S(1)}) custom-call(s32[1]{0:T(128)} %bitcast.me_ref, f32[128,128]{1,0:T(8,128)S(1)} %level2_1.1.done_ref, f32[128,128]{1,0:T(8,128)S(1)} %get-tuple-element.36.base_ref, ...), custom_call_target="tpu_custom_call" | custom-call | tf_op jit(solution)/shard_map/last/pallas_call | solution.py:93
  20.7 0.1 collective-permute-start.6
  20.8 1.6 %collective-permute-start.7 = (f32[2,16,256]{2,1,0:T(8,128)S(1)}, f32[2,16,256]{2,1,0:T(8,128)S(1)}, u32[]{:S(2)}, u32[]{:S(2)}) collective-permute-start(f32[2,16,256]{2,1,0:T(8,128)S(1)} %get-tuple-element.39), channel_id=1, source_target_pairs={{0,2},{1,3},{2,0},{3,1},{4,6},{5,7},{6,4},{7,5},{8,10},{9,11},{10,... | collective-permute-start | bytes 98312 | tf_op jit(solution)/shard_map/ppermute | solution.py:18
  22.3 0.3 %collective-permute-start.8 = (f32[2,16,256]{2,1,0:T(8,128)S(1)}, f32[2,16,256]{2,1,0:T(8,128)S(1)}, u32[]{:S(2)}, u32[]{:S(2)}) collective-permute-start(f32[2,16,256]{2,1,0:T(8,128)S(1)} %get-tuple-element.40), channel_id=1, source_target_pairs={{0,1},{1,0},{2,3},{3,2},{4,5},{5,4},{6,7},{7,6},{8,9},{9,8},{10,11... | collective-permute-start | bytes 98312 | tf_op jit(solution)/shard_map/ppermute | solution.py:18
  22.6 1.8 %collective-permute-done.6 = f32[2,16,256]{2,1,0:T(8,128)S(1)} collective-permute-done((f32[2,16,256]{2,1,0:T(8,128)S(1)}, f32[2,16,256]{2,1,0:T(8,128)S(1)}, u32[]{:S(2)}, u32[]{:S(2)}) %collective-permute-start.6) | collective-permute-done | bytes 32800 | tf_op jit(solution)/shard_map/ppermute | solution.py:18
  24.4 0.4 %collective-permute-done.7 = f32[2,16,256]{2,1,0:T(8,128)S(1)} collective-permute-done((f32[2,16,256]{2,1,0:T(8,128)S(1)}, f32[2,16,256]{2,1,0:T(8,128)S(1)}, u32[]{:S(2)}, u32[]{:S(2)}) %collective-permute-start.7) | collective-permute-done | bytes 32800 | tf_op jit(solution)/shard_map/ppermute | solution.py:18
  24.8 0.0 collective-permute-done.8
  24.8 0.6 %add_add_fusion = f32[2,16,256]{2,1,0:T(8,128)} fusion(f32[2,16,256]{2,1,0:T(8,128)S(1)} %collective-permute-done.8, f32[2,16,256]{2,1,0:T(8,128)S(1)} %collective-permute-done.7, f32[2,16,256]{2,1,0:T(8,128)S(1)} %get-tuple-element.37, f32[2,16,256]{2,1,0:T(8,128)S(1)} %collective-permute-done.6), kind=kLoop, calls=%fused_computation | loop fusion | flops 24576 | bytes 163840 | tf_op jit(solution)/shard_map/add | solution.py:150
Async XLA Ops:
  0.8 7.7 %collective-permute-start.1 = (f32[128,128]{1,0:T(8,128)S(1)}, f32[128,128]{1,0:T(8,128)S(1)}, u32[]{:S(2)}, u32[]{:S(2)}) collective-permute-start(f32[128,128]{1,0:T(8,128)S(1)} %slice.8.refs_1_), channel_id=1, source_target_pairs={{0,16},{4,20},{8,24},{12,28},{16,0},{20,4},{24,8},{28,12},{1,17},{... | collective-permute-start | bytes 196616 | tf_op jit(solution)/shard_map/ppermute | solution.py:18
  5.7 5.5 %collective-permute-start = (f32[128,128]{1,0:T(8,128)S(1)}, f32[128,128]{1,0:T(8,128)S(1)}, u32[]{:S(2)}, u32[]{:S(2)}) collective-permute-start(f32[128,128]{1,0:T(8,128)S(1)} %slice.7.refs_0_), channel_id=1, source_target_pairs={{0,16},{4,20},{8,24},{12,28},{16,0},{20,4},{24,8},{28,12},{1,17},{... | collective-permute-start | bytes 196616 | tf_op jit(solution)/shard_map/ppermute | solution.py:18
  5.7 1.9 %copy-start = (f32[1,3,16,64,256]{4,3,2,1,0:T(8,128)S(1)}, f32[1,3,16,64,256]{4,3,2,1,0:T(8,128)}, u32[]{:S(2)}) copy-start(f32[1,3,16,64,256]{4,3,2,1,0:T(8,128)} %f_hbm.1) | copy-start | bytes 9437188
  8.8 4.4 %collective-permute-start.3 = (f32[128,128]{1,0:T(8,128)S(1)}, f32[128,128]{1,0:T(8,128)S(1)}, u32[]{:S(2)}, u32[]{:S(2)}) collective-permute-start(f32[128,128]{1,0:T(8,128)S(1)} %level0_1.1.refs_1_), channel_id=1, source_target_pairs={{0,8},{4,12},{8,0},{12,4},{16,24},{20,28},{24,16},{28,20},{1,9},{5... | collective-permute-start | bytes 196616 | tf_op jit(solution)/shard_map/ppermute | solution.py:18
  11.5 4.3 %collective-permute-start.2 = (f32[128,128]{1,0:T(8,128)S(1)}, f32[128,128]{1,0:T(8,128)S(1)}, u32[]{:S(2)}, u32[]{:S(2)}) collective-permute-start(f32[128,128]{1,0:T(8,128)S(1)} %level0_0.1.refs_0_), channel_id=1, source_target_pairs={{0,8},{4,12},{8,0},{12,4},{16,24},{20,28},{24,16},{28,20},{1,9},{5... | collective-permute-start | bytes 196616 | tf_op jit(solution)/shard_map/ppermute | solution.py:18
  13.5 4.8 %collective-permute-start.4 = (f32[128,128]{1,0:T(8,128)S(1)}, f32[128,128]{1,0:T(8,128)S(1)}, u32[]{:S(2)}, u32[]{:S(2)}) collective-permute-start(f32[128,128]{1,0:T(8,128)S(1)} %level1_1.1.refs_1_), channel_id=1, source_target_pairs={{0,4},{4,0},{8,12},{12,8},{16,20},{20,16},{24,28},{28,24},{1,5},{5... | collective-permute-start | bytes 196616 | tf_op jit(solution)/shard_map/ppermute | solution.py:18
  16.1 4.3 %collective-permute-start.5 = (f32[128,128]{1,0:T(8,128)S(1)}, f32[128,128]{1,0:T(8,128)S(1)}, u32[]{:S(2)}, u32[]{:S(2)}) collective-permute-start(f32[128,128]{1,0:T(8,128)S(1)} %level1_0.1.refs_0_), channel_id=1, source_target_pairs={{0,4},{4,0},{8,12},{12,8},{16,20},{20,16},{24,28},{28,24},{1,5},{5... | collective-permute-start | bytes 196616 | tf_op jit(solution)/shard_map/ppermute | solution.py:18
  20.7 3.7 %collective-permute-start.6 = (f32[2,16,256]{2,1,0:T(8,128)S(1)}, f32[2,16,256]{2,1,0:T(8,128)S(1)}, u32[]{:S(2)}, u32[]{:S(2)}) collective-permute-start(f32[2,16,256]{2,1,0:T(8,128)S(1)} %get-tuple-element.38), channel_id=1, source_target_pairs={{0,3},{1,2},{2,1},{3,0},{4,7},{5,6},{6,5},{7,4},{8,11},{9,10},{10,... | collective-permute-start | bytes 98312 | tf_op jit(solution)/shard_map/ppermute | solution.py:18
  20.8 4.0 %collective-permute-start.7 = (f32[2,16,256]{2,1,0:T(8,128)S(1)}, f32[2,16,256]{2,1,0:T(8,128)S(1)}, u32[]{:S(2)}, u32[]{:S(2)}) collective-permute-start(f32[2,16,256]{2,1,0:T(8,128)S(1)} %get-tuple-element.39), channel_id=1, source_target_pairs={{0,2},{1,3},{2,0},{3,1},{4,6},{5,7},{6,4},{7,5},{8,10},{9,11},{10,... | collective-permute-start | bytes 98312 | tf_op jit(solution)/shard_map/ppermute | solution.py:18
  22.3 2.5 %collective-permute-start.8 = (f32[2,16,256]{2,1,0:T(8,128)S(1)}, f32[2,16,256]{2,1,0:T(8,128)S(1)}, u32[]{:S(2)}, u32[]{:S(2)}) collective-permute-start(f32[2,16,256]{2,1,0:T(8,128)S(1)} %get-tuple-element.40), channel_id=1, source_target_pairs={{0,1},{1,0},{2,3},{3,2},{4,5},{5,4},{6,7},{7,6},{8,9},{9,8},{10,11... | collective-permute-start | bytes 98312 | tf_op jit(solution)/shard_map/ppermute | solution.py:18
